TPU v7x, 32 devices: a whole 2x2x4 slice. The times are simulated.
32 devices in a mesh: exp: 16 (over z, y, core), et: 2 (over x).
Axes of the slice: x: 2, y: 2, z: 4, core: 2. Of those that a mesh axis runs over, the one named last changes fastest.
Arguments:
- tokens: bfloat16 [192, 7168], P(('exp', 'et')), may hold values from -6 to 6
- grad_out: bfloat16 [192, 7168], P(('exp', 'et')), may hold values from -6 to 6
- gates: bfloat16 [192, 8], P(('exp', 'et')), may hold values from 0.049804688 to 1
- expert_ids: int32 [192, 8], P(('exp', 'et')), may hold values from 0 to 15, all different within a row; in each aligned block of 6 rows (0 to 5, 6 to 11, ...) at most 3 rows name the same one
- gate_weight: bfloat16 [16, 7168, 1024], P('exp', None, 'et'), may hold values from -0.0625 to 0.0625
- up_weight: bfloat16 [16, 7168, 1024], P('exp', None, 'et'), may hold values from -0.0625 to 0.0625
- down_weight: bfloat16 [16, 1024, 7168], P('exp', 'et'), may hold values from -0.1875 to 0.1875
Outputs:
- input_grad: bfloat16 [192, 7168], P(('exp', 'et'))
- gate_grad: float32 [192, 8], P(('exp', 'et'))
- gate_weight_grad: bfloat16 [16, 7168, 1024], P('exp', None, 'et')
- up_weight_grad: bfloat16 [16, 7168, 1024], P('exp', None, 'et')
- down_weight_grad: bfloat16 [16, 1024, 7168], P('exp', 'et')
Inputs may be any that keep to these rules, and one draw needn't show every extreme that they name: `expert_ids`: each row names 8 different experts. Among the 6 tokens of one device no expert is named by more than 3 tokens, and in every draw some expert is named by exactly 3 tokens of some device.
All inputs are finite; a program needn't handle non-finite values.
Results may differ from a plain program's by a relative error of at most 0.017.
Values may be sent and summed in bfloat16 or wider, within the bound.
No kernel may reach another device: no remote copies, remote signals or barrier semaphores. Data moves between devices by JAX's collectives and lax.ppermute only.
A program may use at most 128 MiB of HBM per device.

v0:
```python
import jax
import jax.numpy as jnp
from jax import lax
from jax.sharding import PartitionSpec as P

TOP = 8
EXP_DEV = 1


def expert_terms(rows_x, rows_dy, rows_g, w_gate, w_up, w_down):
    gate_pre = jnp.dot(rows_x, w_gate, preferred_element_type=jnp.float32)
    up_pre = jnp.dot(rows_x, w_up, preferred_element_type=jnp.float32)
    sigma = jax.nn.sigmoid(gate_pre)
    silu_val = gate_pre * sigma
    act = silu_val * up_pre
    back = lax.dot_general(
        rows_dy, w_down, (((1,), (1,)), ((), ())), preferred_element_type=jnp.float32
    )
    score = jnp.sum(act * back, axis=1)
    scale = rows_g.astype(jnp.float32)[:, None]
    weighted = (scale * act).astype(jnp.bfloat16)
    dact = scale * back
    grad_gate = (dact * up_pre * sigma * (1.0 + gate_pre * (1.0 - sigma))).astype(jnp.bfloat16)
    grad_up = (dact * silu_val).astype(jnp.bfloat16)
    inward = lax.dot_general(
        grad_gate, w_gate, (((1,), (1,)), ((), ())), preferred_element_type=jnp.float32
    )
    inward = inward + lax.dot_general(
        grad_up, w_up, (((1,), (1,)), ((), ())), preferred_element_type=jnp.float32
    )
    d_gate = lax.dot_general(
        rows_x, grad_gate, (((0,), (0,)), ((), ())), preferred_element_type=jnp.float32
    )
    d_up = lax.dot_general(
        rows_x, grad_up, (((0,), (0,)), ((), ())), preferred_element_type=jnp.float32
    )
    d_down = lax.dot_general(
        weighted, rows_dy, (((0,), (0,)), ((), ())), preferred_element_type=jnp.float32
    )
    return (d_gate, d_up, d_down, inward, score)


def slot_table(routes, experts, width):
    flat = routes.reshape(-1)
    onehot = (flat[:, None] == jnp.arange(experts, dtype=jnp.int32)[None, :]).astype(jnp.int32)
    before = jnp.cumsum(onehot, axis=0) - onehot
    rank = jnp.sum(before * onehot, axis=1)
    return flat * width + rank


def pack_rows(values, slots, total):
    return jnp.zeros((total,) + values.shape[1:], values.dtype).at[slots].set(values)


def build_buffers(owned_x, owned_dy, owned_g, slots, total, n_exp, block):
    depth = owned_x.shape[1]
    buf_x = pack_rows(jnp.repeat(owned_x, TOP, axis=0), slots, total).reshape(n_exp, block, depth)
    buf_dy = pack_rows(jnp.repeat(owned_dy, TOP, axis=0), slots, total).reshape(n_exp, block, depth)
    buf_g = pack_rows(owned_g.reshape(-1), slots, total).reshape(n_exp, block)
    return (buf_x, buf_dy, buf_g)


def on_device(tokens, grad_out, gates, expert_ids, gate_weight, up_weight, down_weight):
    count = tokens.shape[0]
    depth = tokens.shape[1]
    ff_dev = gate_weight.shape[2]
    n_exp = lax.axis_size("exp")
    n_et = lax.axis_size("et")
    experts = n_exp * EXP_DEV
    capacity = max(2, (count * TOP + experts - 1) // experts)
    total = experts * capacity
    slots = slot_table(expert_ids, experts, capacity)
    buf_x, buf_dy, buf_g = build_buffers(
        tokens, grad_out, gates, slots, total, n_exp, EXP_DEV * capacity
    )
    got_x, got_dy, got_g = (
        lax.all_to_all(buf_x, "exp", split_axis=0, concat_axis=0, tiled=True),
        lax.all_to_all(buf_dy, "exp", split_axis=0, concat_axis=0, tiled=True),
        lax.all_to_all(buf_g, "exp", split_axis=0, concat_axis=0, tiled=True),
    )
    got_x = got_x.reshape(n_exp, EXP_DEV, capacity, depth)
    got_dy = got_dy.reshape(n_exp, EXP_DEV, capacity, depth)
    got_g = got_g.reshape(n_exp, EXP_DEV, capacity)
    rows_x = got_x[:, 0].reshape(n_exp * capacity, depth)
    rows_dy = got_dy[:, 0].reshape(n_exp * capacity, depth)
    rows_g = got_g[:, 0].reshape(n_exp * capacity)
    w_gate = gate_weight[0]
    w_up = up_weight[0]
    w_down = down_weight[0]
    height = rows_x.shape[0]

    def accumulate(carry, piece, start, w_gate=w_gate, w_up=w_up, w_down=w_down):
        terms = expert_terms(piece[0], piece[1], piece[2], w_gate, w_up, w_down)
        inward = terms[3]
        score = terms[4]
        return (terms[0], terms[1], terms[2], inward, score)

    init = (
        jnp.zeros((depth, ff_dev), jnp.float32),
        jnp.zeros((depth, ff_dev), jnp.float32),
        jnp.zeros((ff_dev, depth), jnp.float32),
        jnp.zeros((n_et * height, depth), jnp.float32),
        jnp.zeros((n_et * height,), jnp.float32),
    )
    folded = accumulate(
        init,
        (
            lax.all_gather(rows_x, "et", axis=0, tiled=True),
            lax.all_gather(rows_dy, "et", axis=0, tiled=True),
            lax.all_gather(rows_g, "et", axis=0, tiled=True),
        ),
        jnp.int32(0),
    )
    own_part = lax.psum_scatter(
        folded[3].astype(jnp.bfloat16), "et", scatter_dimension=0, tiled=True
    ).astype(jnp.float32)
    own_score = lax.psum_scatter(
        folded[4].astype(jnp.bfloat16), "et", scatter_dimension=0, tiled=True
    ).astype(jnp.float32)
    grads_gate = [folded[0].astype(jnp.bfloat16)]
    grads_up = [folded[1].astype(jnp.bfloat16)]
    grads_down = [folded[2].astype(jnp.bfloat16)]
    parts = [own_part.reshape(n_exp, capacity, depth)]
    scores = [own_score.reshape(n_exp, capacity)]
    part_all = jnp.stack(parts, axis=1).reshape(n_exp, EXP_DEV * capacity, depth)
    score_all = jnp.stack(scores, axis=1).reshape(n_exp, EXP_DEV * capacity)
    back_part, back_score = (
        lax.all_to_all(
            part_all.astype(jnp.bfloat16), "exp", split_axis=0, concat_axis=0, tiled=True
        ).astype(part_all.dtype),
        lax.all_to_all(
            score_all.astype(jnp.bfloat16), "exp", split_axis=0, concat_axis=0, tiled=True
        ).astype(score_all.dtype),
    )
    pair_grad = back_part.reshape(total, depth)[slots].reshape(count, TOP, depth)
    input_grad = jnp.sum(pair_grad, axis=1).astype(jnp.bfloat16)
    gate_grad = back_score.reshape(total)[slots].reshape(count, TOP)
    return (
        input_grad,
        gate_grad,
        jnp.stack(grads_gate, axis=0),
        jnp.stack(grads_up, axis=0),
        jnp.stack(grads_down, axis=0),
    )


def solution(mesh):
    placed = (
        P(("exp", "et"), None),
        P(("exp", "et"), None),
        P(("exp", "et"), None),
        P(("exp", "et"), None),
        P("exp", None, "et"),
        P("exp", None, "et"),
        P("exp", "et", None),
    )
    return jax.shard_map(
        on_device,
        mesh=mesh,
        in_specs=placed,
        out_specs=(
            P(("exp", "et"), None),
            P(("exp", "et"), None),
            P("exp", None, "et"),
            P("exp", None, "et"),
            P("exp", "et", None),
        ),
        check_vma=False,
    )
```

profile of v0, /device:TPU:0, one launch (start us, length us, event | category | flops | bytes accessed | tf_op | source)
XLA Modules:
  0.0 179.7 jit_solution(9083507120403732540)
XLA Ops:
  7.2 0.8 eq.15
  8.0 0.7 broadcast_multiply_fusion
  8.7 0.1 mul.59
  8.8 0.1 fusion.24
  8.8 0.1 reduce_window_sum.11
  8.9 0.2 select_reduce_fusion
  9.1 1.7 scatter_custom_fusion.2
  10.8 0.4 reshape.95
  11.3 29.7 %all_to_all.31 = bf16[16,3,7168]{2,1,0:T(4,128)(2,1)S(1)} all-to-all(bf16[16,3,7168]{2,1,0:T(4,128)(2,1)S(1)} %reshape.95), channel_id=1, replica_groups=mesh['exp'=16,'et'=2] {'exp'}, dimensions={0} | all-to-all | bytes 1376256 | tf_op jit(solution)/shard_map/all_to_all | solution.py:77
  41.0 1.3 reshape_squeeze_reshape.11
  42.4 0.0 all-gather.3.cloned.1.call-start
  42.4 1.7 scatter_custom_fusion.1
  44.2 0.4 reshape.93
  44.6 26.8 %all_to_all.32 = bf16[16,3,7168]{2,1,0:T(4,128)(2,1)S(1)} all-to-all(bf16[16,3,7168]{2,1,0:T(4,128)(2,1)S(1)} %reshape.93), channel_id=1, replica_groups=mesh['exp'=16,'et'=2] {'exp'}, dimensions={0} | all-to-all | bytes 1376256 | tf_op jit(solution)/shard_map/all_to_all | solution.py:78
  71.5 1.3 reshape_squeeze_reshape.10
  72.8 0.1 reshape.123
  72.9 0.9 scatter_custom_fusion
  73.8 0.7 all_to_all.25
  74.5 4.5 %all-to-all-start = ((bf16[16,1,3]{2,1,0:T(2,128)(2,1)}), bf16[16,1,3]{2,1,0:T(2,128)(2,1)S(1)}, u32[]{:S(2)}, u32[]{:S(2)}) async-start(bf16[16,1,3]{2,1,0:T(2,128)(2,1)} %all_to_all.25), calls=%async_computation | async-start | bytes 16384 | tf_op jit(solution)/shard_map/all_to_all | solution.py:79
  79.0 0.0 reduce-scatter.2.cloned.1.call-start
  79.0 0.6 fusion.29
  80.3 5.0 %all-to-all-done = bf16[16,1,3]{2,1,0:T(2,128)(2,1)S(1)} async-done(((bf16[16,1,3]{2,1,0:T(2,128)(2,1)}), bf16[16,1,3]{2,1,0:T(2,128)(2,1)S(1)}, u32[]{:S(2)}, u32[]{:S(2)}) %all-to-all-start) | async-done | bytes 128 | tf_op jit(solution)/shard_map/all_to_all | solution.py:79
  85.3 0.1 reshape.143
  85.4 0.2 dynamic-update-slice
  85.7 4.9 %fusion.6 = f32[96,512]{1,0:T(8,128)S(1)} fusion(bf16[96,7168]{1,0:T(8,128)(2,1)} %all-gather.5.cloned.1.call-done, bf16[1,7168,512]{2,1,0:T(8,128)(2,1)} %param.11), kind=kOutput, calls=%fused_computation.15 | convolution fusion | flops 704643072 | bytes 8912896 | tf_op jit(solution)/shard_map/dot_general | solution.py:11
  90.6 4.4 %fusion.9 = f32[96,512]{1,0:T(8,128)S(1)} fusion(bf16[96,7168]{1,0:T(8,128)(2,1)S(1)} %copy-done.1, bf16[1,7168,512]{2,1,0:T(8,128)(2,1)} %param.12), kind=kOutput, calls=%fused_computation.18 | convolution fusion | flops 704643072 | bytes 8912896 | tf_op jit(solution)/shard_map/dot_general | solution.py:12
  94.9 2.8 %all-gather.3.cloned.1.call-done = bf16[96,7168]{1,0:T(8,128)(2,1)} async-done(((bf16[48,7168]{1,0:T(8,128)(2,1)}), bf16[96,7168]{1,0:T(8,128)(2,1)}) %all-gather.3.cloned.1.call-update) | async-done | bytes 1376272 | tf_op jit(solution)/shard_map/all_gather | solution.py:109
  97.7 6.0 %multiply_reduce_fusion = (bf16[96]{0:T(256)(128)(2,1)S(1)}, f32[96,512]{1,0:T(8,128)S(1)}) fusion(f32[96,512]{1,0:T(8,128)S(1)} %fusion.9, f32[96,512]{1,0:T(8,128)S(1)} %fusion.6, bf16[96,7168]{1,0:T(8,128)(2,1)} %all-gather.3.cloned.1.call-done, bf16[1,512,7168]{2,1,0:T(8,128)(2,1)} %param.13), kind=kOutput, calls=%fused_computation.32 | convolution fusion | flops 704987008 | bytes 9306304 | tf_op jit(solution)/shard_map/dot_general | solution.py:16
  103.8 4.9 %all-reduce.2 = (bf16[96]{0:T(256)(128)(2,1)S(1)}, bf16[96]{0:T(256)(128)(2,1)S(1)}) all-reduce(bf16[96]{0:T(256)(128)(2,1)S(1)} %dynamic-update-slice, bf16[96]{0:T(256)(128)(2,1)S(1)} %get-tuple-element.11), channel_id=1, replica_groups=mesh['exp'=16,'et'=2] {'et'}, use_global_device_ids=true, to_apply=%add | all-reduce | flops 192 | bytes 768
  108.7 0.1 multiply_convert_fusion.1
  108.9 5.6 %fusion.4 = f32[96,7168]{1,0:T(8,128)S(1)} fusion(bf16[96,512]{1,0:T(8,128)(2,1)S(1)} %get-tuple-element.8, bf16[1,7168,512]{2,1,0:T(8,128)(2,1)} %param.11), kind=kOutput, calls=%fused_computation.13 | convolution fusion | flops 704643072 | bytes 10190848 | tf_op jit(solution)/shard_map/dot_general | solution.py:25
  114.4 3.4 %fusion.3 = bf16[96,7168]{1,0:T(8,128)(2,1)} fusion(f32[96,7168]{1,0:T(8,128)S(1)} %fusion.4, bf16[96,512]{1,0:T(8,128)(2,1)S(1)} %get-tuple-element.7, bf16[1,7168,512]{2,1,0:T(8,128)(2,1)S(1)} %bitcast.51), kind=kOutput, calls=%fused_computation.12 | convolution fusion | flops 706019328 | bytes 11567104 | tf_op jit(solution)/shard_map/dot_general | solution.py:28
  118.5 0.1 dynamic-slice.2
  118.6 0.7 convert_element_type.74
  119.3 5.8 %all-to-all-start.4 = ((bf16[16,1,3]{2,1,0:T(2,128)(2,1)}), bf16[16,1,3]{2,1,0:T(2,128)(2,1)S(1)}, u32[]{:S(2)}, u32[]{:S(2)}) async-start(bf16[16,1,3]{2,1,0:T(2,128)(2,1)} %convert_element_type.74), calls=%async_computation.5 | async-start | bytes 16384 | tf_op jit(solution)/shard_map/all_to_all | solution.py:131
  125.1 16.8 %reduce-scatter.2.cloned.1.call-done = bf16[48,7168]{1,0:T(8,128)(2,1)} async-done(((bf16[96,7168]{1,0:T(8,128)(2,1)}), bf16[48,7168]{1,0:T(8,128)(2,1)}) %reduce-scatter.2.cloned.1.call-update) | async-done | bytes 688144 | tf_op jit(solution)/shard_map/reduce_scatter | solution.py:114
  142.0 2.2 %convert_element_type.63 = bf16[16,3,7168]{2,1,0:T(4,128)(2,1)} reshape(bf16[48,7168]{1,0:T(8,128)(2,1)} %reduce-scatter.2.cloned.1.call-done) | data formatting | bytes 1376256 | tf_op jit(solution)/shard_map/convert_element_type | solution.py:129
  144.1 5.6 %all-to-all-start.3 = ((bf16[16,3,7168]{2,1,0:T(4,128)(2,1)}), bf16[16,3,7168]{2,1,0:T(4,128)(2,1)S(1)}, u32[]{:S(2)}, u32[]{:S(2)}) async-start(bf16[16,3,7168]{2,1,0:T(4,128)(2,1)} %convert_element_type.63), calls=%async_computation.4 | async-start | bytes 1835008 | tf_op jit(solution)/shard_map/all_to_all | solution.py:128
  149.8 5.1 %fusion.1 = bf16[1,7168,512]{2,1,0:T(8,128)(2,1)} fusion(bf16[96,7168]{1,0:T(8,128)(2,1)S(1)} %copy-done.1, bf16[96,512]{1,0:T(8,128)(2,1)S(1)} %get-tuple-element.7), kind=kOutput, calls=%fused_computation.9 | convolution fusion | flops 708313088 | bytes 8814592 | tf_op jit(solution)/shard_map/dot_general | solution.py:34
  154.9 5.1 %fusion = bf16[1,7168,512]{2,1,0:T(8,128)(2,1)} fusion(bf16[96,7168]{1,0:T(8,128)(2,1)S(1)} %copy-done.1, bf16[96,512]{1,0:T(8,128)(2,1)S(1)} %get-tuple-element.8), kind=kOutput, calls=%fused_computation.8 | convolution fusion | flops 708313088 | bytes 8814592 | tf_op jit(solution)/shard_map/dot_general | solution.py:31
  160.1 5.2 %fusion.2 = bf16[1,512,7168]{2,1,0:T(8,128)(2,1)} fusion(bf16[96,7168]{1,0:T(8,128)(2,1)S(1)} %copy-done.2, f32[96]{0:T(128)S(1)} %convert_element_type.59, f32[96,512]{1,0:T(8,128)S(1)} %fusion.9, f32[96,512]{1,0:T(8,128)S(1)} %fusion.6), kind=kOutput, calls=%fused_computation.10 | convolution fusion | flops 708657152 | bytes 9109888 | tf_op jit(solution)/shard_map/dot_general | solution.py:37
  165.3 0.1 reshape.102
  165.4 0.8 gather_fusion.1
  166.2 0.7 reshape.99
  166.9 3.7 %all-to-all-done.3 = bf16[16,3,7168]{2,1,0:T(4,128)(2,1)S(1)} async-done(((bf16[16,3,7168]{2,1,0:T(4,128)(2,1)}), bf16[16,3,7168]{2,1,0:T(4,128)(2,1)S(1)}, u32[]{:S(2)}, u32[]{:S(2)}) %all-to-all-start.3) | async-done | bytes 688160 | tf_op jit(solution)/shard_map/all_to_all | solution.py:128
  170.6 0.5 reshape.101
  171.1 1.0 gather_fusion
  172.2 1.0 bitcast_reduce_fusion
  (29 shorter events, 0.2 us)
Async XLA Ops:
  7.2 1.9 %copy-start = (bf16[6,7168]{1,0:T(8,128)(2,1)S(1)}, bf16[6,7168]{1,0:T(8,128)(2,1)}, u32[]{:S(2)}) copy-start(bf16[6,7168]{1,0:T(8,128)(2,1)} %param.7) | copy-start | bytes 258052
  7.2 78.5 %all-gather.5.cloned.1.call-start = ((), (), s32[]{:S(2)}) async-start(), calls=%async_computation.7 | async-start | bytes 2064384 | tf_op jit(solution)/shard_map/all_gather | solution.py:108
  10.8 31.6 %copy-start.3 = (bf16[6,7168]{1,0:T(8,128)(2,1)S(1)}, bf16[6,7168]{1,0:T(8,128)(2,1)}, u32[]{:S(2)}) copy-start(bf16[6,7168]{1,0:T(8,128)(2,1)} %param.8) | copy-start | bytes 258052
  42.4 55.4 %all-gather.3.cloned.1.call-start = ((), (), s32[]{:S(2)}) async-start(), calls=%async_computation.6 | async-start | bytes 2064384 | tf_op jit(solution)/shard_map/all_gather | solution.py:109
  44.1 28.7 %copy-start.5 = (bf16[6,8]{1,0:T(8,128)(2,1)S(1)}, bf16[6,8]{1,0:T(8,128)(2,1)}, u32[]{:S(2)}) copy-start(bf16[6,8]{1,0:T(8,128)(2,1)} %param.9) | copy-start | bytes 292
  44.2 34.9 %copy-start.4 = (u32[32]{0:T(128)S(1)}, u32[32]{0:T(128)}, u32[]{:S(2)}) copy-start(u32[32]{0:T(128)} %constant.27) | copy-start | bytes 388
  74.5 10.8 %all-to-all-start = ((bf16[16,1,3]{2,1,0:T(2,128)(2,1)}), bf16[16,1,3]{2,1,0:T(2,128)(2,1)S(1)}, u32[]{:S(2)}, u32[]{:S(2)}) async-start(bf16[16,1,3]{2,1,0:T(2,128)(2,1)} %all_to_all.25), calls=%async_computation | async-start | bytes 16384 | tf_op jit(solution)/shard_map/all_to_all | solution.py:79
  79.0 63.0 %reduce-scatter.2.cloned.1.call-start = ((), (), s32[]{:S(2)}) async-start(), calls=%async_computation.8 | async-start | bytes 2064384 | tf_op jit(solution)/shard_map/reduce_scatter | solution.py:114
  85.7 4.9 %copy-start.1 = (bf16[96,7168]{1,0:T(8,128)(2,1)S(1)}, bf16[96,7168]{1,0:T(8,128)(2,1)}, u32[]{:S(2)}) copy-start(bf16[96,7168]{1,0:T(8,128)(2,1)} %all-gather.5.cloned.1.call-done) | copy-start | bytes 4128772
  108.7 5.7 %slice-start = ((s8[7340032]{0:T(1024)(128)(4,1)}), s8[4194304]{0:T(1024)(128)(4,1)S(1)}, s32[]{:S(2)}) async-start(s8[7340032]{0:T(1024)(128)(4,1)} %bitcast.50), calls=%async_computation.9 | async-start | bytes 8388608
  108.8 5.6 %slice-start.1 = ((s8[7340032]{0:T(1024)(128)(4,1)}), s8[3145728]{0:T(1024)(128)(4,1)S(1)}, s32[]{:S(2)}) async-start(s8[7340032]{0:T(1024)(128)(4,1)} %bitcast.50), calls=%async_computation.10 | async-start | bytes 6291456
  119.3 24.8 %all-to-all-start.4 = ((bf16[16,1,3]{2,1,0:T(2,128)(2,1)}), bf16[16,1,3]{2,1,0:T(2,128)(2,1)S(1)}, u32[]{:S(2)}, u32[]{:S(2)}) async-start(bf16[16,1,3]{2,1,0:T(2,128)(2,1)} %convert_element_type.74), calls=%async_computation.5 | async-start | bytes 16384 | tf_op jit(solution)/shard_map/all_to_all | solution.py:131
  144.1 26.4 %all-to-all-start.3 = ((bf16[16,3,7168]{2,1,0:T(4,128)(2,1)}), bf16[16,3,7168]{2,1,0:T(4,128)(2,1)S(1)}, u32[]{:S(2)}, u32[]{:S(2)}) async-start(bf16[16,3,7168]{2,1,0:T(4,128)(2,1)} %convert_element_type.63), calls=%async_computation.4 | async-start | bytes 1835008 | tf_op jit(solution)/shard_map/all_to_all | solution.py:128
  154.9 5.1 %copy-start.2 = (bf16[96,7168]{1,0:T(8,128)(2,1)S(1)}, bf16[96,7168]{1,0:T(8,128)(2,1)}, u32[]{:S(2)}) copy-start(bf16[96,7168]{1,0:T(8,128)(2,1)} %all-gather.3.cloned.1.call-done) | copy-start | bytes 4128772
Sparse Core Ops, SparseCore 0:
  42.5 24.7 all-gather.4
  72.9 24.7 all-gather.2
  118.0 23.9 reduce-scatter.1
where the time goes:
time: 181 us; the launch traced here: 180 us
  blocking collectives  61.5 us (34%)
  matrix products  39.7 us (22%)
  waiting for transfers between devices  28.4 us (16%)
  local copies, waits for them, and re-layouts  16.5 us (9%)
  starting transfers between devices  16 us (9%)
  between operations  15.3 us (8%)
  other arithmetic  2.21 us (1%)
    all_to_all x1, blocking collectives, on_device(): lax.all_to_all(buf_x, 'exp', split_axis=0, concat_axis=0, tiled=True)  29.7 us
    all_to_all x1, blocking collectives, on_device(): lax.all_to_all(buf_dy, 'exp', split_axis=0, concat_axis=0, tiled=True)  26.8 us
    reduce_scatter x1, waiting for transfers between devices, on_device(): lax.psum_scatter(folded[3].astype(jnp.bfloat16), 'et', scatter_dimension=...  16.8 us
    dot_general x1, matrix products, expert_terms(): lax.dot_general(rows_dy, w_down, (((1,), (1,)), ((), ())), preferred_elem...  6.01 us
    all_to_all x1, starting transfers between devices, on_device(): lax.all_to_all(score_all.astype(jnp.bfloat16), 'exp', split_axis=0, conca...  5.8 us
    all_to_all x1, starting transfers between devices, on_device(): lax.all_to_all(part_all.astype(jnp.bfloat16), 'exp', split_axis=0, concat...  5.62 us
    dot_general x1, matrix products, expert_terms(): lax.dot_general(grad_gate, w_gate, (((1,), (1,)), ((), ())), preferred_el...  5.55 us
    dot_general x1, matrix products, expert_terms(): lax.dot_general(weighted, rows_dy, (((0,), (0,)), ((), ())), preferred_el...  5.21 us
  transfers between devices with their start and end apart: 6, of which 4 were waited for; matrix products, arithmetic and copies ran while one was open for 19% of the time, Pallas kernels for 0%

commit v1 on v0

v1 whole, which is shorter than its diff:
```python
import functools

import jax
import jax.numpy as jnp
from jax import lax
from jax.experimental import pallas as pl
from jax.experimental.pallas import tpu as pltpu
from jax.sharding import PartitionSpec as P

LANES = 128
SPLIT = 4
AXES = ("exp", "et")
F32, BF16 = jnp.float32, jnp.bfloat16
MIB = 1 << 20
VMEM = pl.BlockSpec(memory_space=pltpu.VMEM)


def flips(mesh):
    n_exp, n_et = mesh.shape["exp"], mesh.shape["et"]

    def perm(far):
        pairs = []
        for e in range(n_exp):
            for t in range(n_et):
                e2, t2 = far(e, t)
                pairs.append((e * n_et + t, e2 * n_et + t2))
        return pairs

    def flip_y(e, t):
        return e ^ 2, t

    def flip_x(k):
        return lambda e, t: (e, t ^ k)

    def by_core(first, second):
        return perm(lambda e, t: first(e, t) if e % 2 == 0 else second(e, t))

    along = {"z": [perm(lambda e, t, k=k: (e ^ (4 * k), t)) for k in range(1, n_exp // 4)]}
    along["core"] = perm(lambda e, t: (e ^ 1, t))
    along["y"] = perm(flip_y)
    along["x"] = [perm(flip_x(k)) for k in range(1, n_et)]
    along["first"] = by_core(flip_y, flip_x(1))
    along["second"] = by_core(flip_x(1), flip_y)
    return along


def send(block, pairs):
    return lax.ppermute(block, AXES, pairs)


def params(limit=None):
    return pltpu.CompilerParams(vmem_limit_bytes=(limit or 48) * MIB)


def pack_kernel(x_ref, dy_ref, g_ref, id_ref, t_out, d_out):
    count, depth = x_ref.shape
    part = depth // SPLIT
    wide = t_out.shape[1] - part
    t_out[...] = jnp.zeros_like(t_out)
    for j in range(SPLIT):
        t_out[j * count : (j + 1) * count, :part] = x_ref[:, j * part : (j + 1) * part]
        d_out[j * count : (j + 1) * count, :] = dy_ref[:, j * part : (j + 1) * part]
    lane = lax.broadcasted_iota(jnp.int32, (count, wide), 1)
    total = jnp.zeros((count, wide), F32)
    for k in range(g_ref.shape[1]):
        total = total + jnp.where(id_ref[:, k : k + 1] == lane, g_ref[:, k : k + 1].astype(F32), 0.0)
    t_out[:count, part:] = total.astype(BF16)


def pack(tokens, grad_out, gates, expert_ids, wide):
    count, depth = tokens.shape
    part = depth // SPLIT
    return pl.pallas_call(
        pack_kernel,
        out_shape=(
            jax.ShapeDtypeStruct((SPLIT * count, part + wide), BF16),
            jax.ShapeDtypeStruct((SPLIT * count, part), BF16),
        ),
        in_specs=[VMEM] * 4,
        out_specs=(VMEM, VMEM),
        compiler_params=params(8),
        name="pack",
    )(tokens, grad_out, gates, expert_ids)


def unpack_kernel(count, part, *refs):
    out = refs[-1]
    for i, ref in enumerate(refs[:-1]):
        rows = slice(i * count, (i + 1) * count)
        for j in range(SPLIT):
            out[rows, j * part : (j + 1) * part] = ref[j * count : (j + 1) * count, :part]
        if ref.shape[1] > part:
            out[rows, SPLIT * part :] = ref[:count, part:]


def unpack(blocks, count, part):
    extra = blocks[0].shape[1] - part
    return pl.pallas_call(
        functools.partial(unpack_kernel, count, part),
        out_shape=jax.ShapeDtypeStruct((len(blocks) * count, SPLIT * part + extra), BF16),
        in_specs=[VMEM] * len(blocks),
        out_specs=VMEM,
        compiler_params=params(8),
        name="unpack",
    )(*blocks)


def dot(a, b, over):
    return lax.dot_general(a, b, ((over[:1], over[1:]), ((), ())), preferred_element_type=F32)


def in_kernel(n, depth, mine_ref, *refs):
    blocks, (wg, wu, x, act, sp, sq, wt, named, g_acc, u_acc) = refs[:n], refs[n:]
    step, steps = pl.program_id(0), pl.num_programs(0)
    size = wg.shape[0]
    rows = blocks[0].shape[0]
    cols = pl.ds(pl.multiple_of(step * size, LANES), size)
    for i, ref in enumerate(blocks):
        x[i * rows : (i + 1) * rows, cols] = ref[:, cols]

    @pl.when(step == 0)
    def _():
        g_acc[...] = jnp.zeros_like(g_acc)
        u_acc[...] = jnp.zeros_like(u_acc)

    piece = x[:, cols]
    g_acc[...] += dot(piece, wg[...], (1, 0))
    u_acc[...] += dot(piece, wu[...], (1, 0))

    @pl.when(step == steps - 1)
    def _():
        for i, ref in enumerate(blocks):
            span = slice(i * rows, (i + 1) * rows)
            gates = ref[:, depth:].astype(F32)
            at_mine = lax.broadcasted_iota(jnp.int32, gates.shape, 1) == mine_ref[0]
            gates = jnp.where(at_mine, gates, 0.0)
            named[span, :] = (gates != 0.0).astype(F32)
            scale = jnp.sum(gates, axis=1, keepdims=True)
            gate_pre, up_pre = g_acc[span, :], u_acc[span, :]
            sigma = jax.nn.sigmoid(gate_pre)
            silu = gate_pre * sigma
            hidden = silu * up_pre
            act[span, :] = hidden
            wt[span, :] = (scale * hidden).astype(BF16)
            sp[span, :] = scale * (up_pre * sigma * (1.0 + gate_pre * (1.0 - sigma)))
            sq[span, :] = scale * silu


def into_hidden(mine, blocks, w_gate, w_up, depth):
    n, rows = len(blocks), sum(b.shape[0] for b in blocks)
    ff = w_gate.shape[2]
    size = depth // 7 if depth % (7 * LANES) == 0 else depth // SPLIT
    weight = pl.BlockSpec((None, size, ff), lambda i: (0, i, 0))
    wide = jax.ShapeDtypeStruct((rows, ff), F32)
    return pl.pallas_call(
        functools.partial(in_kernel, n, depth),
        grid=(depth // size,),
        out_shape=(
            jax.ShapeDtypeStruct((rows, depth), BF16),
            wide,
            wide,
            wide,
            jax.ShapeDtypeStruct((rows, ff), BF16),
            jax.ShapeDtypeStruct((rows, blocks[0].shape[1] - depth), F32),
        ),
        in_specs=[pl.BlockSpec(memory_space=pltpu.SMEM)] + [VMEM] * n + [weight, weight],
        out_specs=(VMEM,) * 6,
        scratch_shapes=[pltpu.VMEM((rows, ff), F32)] * 2,
        compiler_params=params(),
        name="into_hidden",
    )(mine, *blocks, w_gate, w_up)


def back_kernel(n, *refs):
    blocks, (wd, act, sp, sq, named, dy, gg, gu, score, acc) = refs[:n], refs[n:]
    step, steps = pl.program_id(0), pl.num_programs(0)
    size = wd.shape[1]
    rows = blocks[0].shape[0]
    cols = pl.ds(pl.multiple_of(step * size, LANES), size)
    for i, ref in enumerate(blocks):
        dy[i * rows : (i + 1) * rows, cols] = ref[:, cols]

    @pl.when(step == 0)
    def _():
        acc[...] = jnp.zeros_like(acc)

    acc[...] += dot(dy[:, cols], wd[...], (1, 1))

    @pl.when(step == steps - 1)
    def _():
        back = acc[...]
        gg[...] = (back * sp[...]).astype(BF16)
        gu[...] = (back * sq[...]).astype(BF16)
        score[...] = (named[...] * jnp.sum(act[...] * back, axis=1, keepdims=True)).astype(BF16)


def back_hidden(blocks, w_down, act, sp, sq, named):
    n, rows = len(blocks), act.shape[0]
    ff, depth = w_down.shape[1:]
    size = depth // 7 if depth % (7 * LANES) == 0 else depth // SPLIT
    half = jax.ShapeDtypeStruct((rows, ff), BF16)
    return pl.pallas_call(
        functools.partial(back_kernel, n),
        grid=(depth // size,),
        out_shape=(
            jax.ShapeDtypeStruct((rows, depth), BF16),
            half,
            half,
            jax.ShapeDtypeStruct(named.shape, BF16),
        ),
        in_specs=[VMEM] * n + [pl.BlockSpec((None, ff, size), lambda i: (0, 0, i))] + [VMEM] * 4,
        out_specs=(VMEM,) * 4,
        scratch_shapes=[pltpu.VMEM((rows, ff), F32)],
        compiler_params=params(),
        name="back_hidden",
    )(*blocks, w_down, act, sp, sq, named)


def inward_kernel(gg, gu, wg, wu, out):
    out[...] = (dot(gg[...], wg[...], (1, 1)) + dot(gu[...], wu[...], (1, 1))).astype(BF16)


def inward(gg, gu, w_gate, w_up, start, stop):
    rows, ff = gg.shape
    size = 512
    first = start // size
    weight = pl.BlockSpec((None, size, ff), lambda i: (0, first + i, 0))
    return pl.pallas_call(
        inward_kernel,
        grid=((stop - start) // size,),
        out_shape=jax.ShapeDtypeStruct((rows, stop - start), BF16),
        in_specs=[VMEM, VMEM, weight, weight],
        out_specs=pl.BlockSpec((rows, size), lambda i: (0, i)),
        compiler_params=params(),
        name="inward",
    )(gg, gu, w_gate, w_up)


def outer_kernel(a, b, out):
    out[...] = dot(a[...], b[...], (0, 0)).astype(BF16)


def outer_tall(a, b):
    rows, depth = a.shape
    ff, size = b.shape[1], 1024
    return pl.pallas_call(
        outer_kernel,
        grid=(depth // size,),
        out_shape=jax.ShapeDtypeStruct((1, depth, ff), BF16),
        in_specs=[pl.BlockSpec((rows, size), lambda i: (0, i)), VMEM],
        out_specs=pl.BlockSpec((None, size, ff), lambda i: (0, i, 0)),
        compiler_params=params(),
        name="outer_tall",
    )(a, b)


def outer_wide(a, b):
    rows, depth = b.shape
    ff, size = a.shape[1], 1024
    return pl.pallas_call(
        outer_kernel,
        grid=(depth // size,),
        out_shape=jax.ShapeDtypeStruct((1, ff, depth), BF16),
        in_specs=[VMEM, pl.BlockSpec((rows, size), lambda i: (0, i))],
        out_specs=pl.BlockSpec((None, ff, size), lambda i: (0, 0, i)),
        compiler_params=params(),
        name="outer_wide",
    )(a, b)


def gather_rows(own, along, count, part):
    near = unpack([own] + [send(own, p) for p in along["z"]], count, part)
    first = send(near, along["first"])
    second = send(near, along["second"])
    both = send(first, along["second"])
    held = [near, first, second, both]
    return held + [send(b, along["core"]) for b in held]


def total_of(own, *parts):
    total = own.astype(F32)
    for part in parts:
        total = total + part.astype(F32)
    return total.astype(BF16)


def return_rows(partial, along):
    half = partial.shape[0] // 2
    partial = total_of(partial[:half], send(partial[half:], along["core"]))
    for way in ("second", "first"):
        half = partial.shape[0] // 2
        partial = total_of(partial[:half], send(partial[half:], along[way]))
    size = partial.shape[0] // (len(along["z"]) + 1)
    parts = [send(partial[(i + 1) * size : (i + 2) * size], p) for i, p in enumerate(along["z"])]
    return total_of(partial[:size], *parts)


def on_device(along, tokens, grad_out, gates, expert_ids, gate_weight, up_weight, down_weight):
    count, depth = tokens.shape
    n_exp = lax.axis_size("exp")
    mine = lax.axis_index("exp")
    wide = -(-n_exp // LANES) * LANES
    part = depth // SPLIT
    own_x, own_dy = pack(tokens, grad_out, gates, expert_ids, wide)
    blocks_x = gather_rows(own_x, along, count, part)
    blocks_dy = gather_rows(own_dy, along, count, part)
    x, act, sp, sq, wt, named = into_hidden(
        mine.reshape(1).astype(jnp.int32), blocks_x, gate_weight, up_weight, depth
    )
    dy, gg, gu, score = back_hidden(blocks_dy, down_weight, act, sp, sq, named)
    middle = depth // 2
    low = inward(gg, gu, gate_weight, up_weight, 0, middle)
    high = inward(gg, gu, gate_weight, up_weight, middle, depth)
    got_low = return_rows(low, along)
    got_high = return_rows(jnp.concatenate([high, score], axis=1), along)
    d_gate = outer_tall(x, gg)
    d_up = outer_tall(x, gu)
    d_down = outer_wide(wt, dy)
    input_grad = jnp.concatenate([got_low, got_high[:, : depth - middle]], axis=1)
    lane = jnp.arange(wide, dtype=jnp.int32)
    by_pair = jnp.where(expert_ids[:, :, None] == lane, got_high[:, None, depth - middle :].astype(F32), 0.0)
    return input_grad, jnp.sum(by_pair, axis=2), d_gate, d_up, d_down


def spread(block, stages):
    for stage in stages:
        block = jnp.concatenate([block] + [send(block, p) for p in stage], axis=0)
    return block


def collect(partial, stages):
    for stage in reversed(stages):
        own = partial.shape[0] // (len(stage) + 1)
        parts = [send(partial[(i + 1) * own : (i + 2) * own], p) for i, p in enumerate(stage)]
        partial = total_of(partial[:own], *parts)
    return partial


def on_device_large(along, tokens, grad_out, gates, expert_ids, gate_weight, up_weight, down_weight):
    stages = [along["z"], [along["y"]], along["x"], [along["core"]]]
    depth = tokens.shape[1]
    n_exp = lax.axis_size("exp")
    wide = -(-n_exp // LANES) * LANES
    named = expert_ids[:, :, None] == jnp.arange(wide, dtype=jnp.int32)
    by_expert = jnp.sum(jnp.where(named, gates.astype(F32)[:, :, None], 0.0), axis=1).astype(BF16)
    rows = spread(jnp.concatenate([tokens, by_expert], axis=1), stages)
    rows_dy = spread(grad_out, stages)
    rows_x, rows_g = rows[:, :depth], rows[:, depth:]
    w_gate, w_up, w_down = gate_weight[0], up_weight[0], down_weight[0]
    at_mine = jnp.arange(wide, dtype=jnp.int32)[None, :] == lax.axis_index("exp")
    scale = jnp.sum(jnp.where(at_mine, rows_g.astype(F32), 0.0), axis=1, keepdims=True)
    gate_pre = dot(rows_x, w_gate, (1, 0))
    up_pre = dot(rows_x, w_up, (1, 0))
    back = dot(rows_dy, w_down, (1, 1))
    sigma = jax.nn.sigmoid(gate_pre)
    silu_val = gate_pre * sigma
    act = silu_val * up_pre
    score = jnp.sum(act * back, axis=1, keepdims=True)
    weighted = (scale * act).astype(BF16)
    dact = scale * back
    grad_gate = (dact * up_pre * sigma * (1.0 + gate_pre * (1.0 - sigma))).astype(BF16)
    grad_up = (dact * silu_val).astype(BF16)
    back_in = dot(grad_gate, w_gate, (1, 1)) + dot(grad_up, w_up, (1, 1))
    scores = jnp.where(at_mine & (scale != 0.0), score, 0.0)
    got = collect(jnp.concatenate([back_in.astype(BF16), scores.astype(BF16)], axis=1), stages)
    d_gate = dot(rows_x, grad_gate, (0, 0)).astype(BF16)
    d_up = dot(rows_x, grad_up, (0, 0)).astype(BF16)
    d_down = dot(weighted, rows_dy, (0, 0)).astype(BF16)
    by_pair = jnp.where(named, got[:, None, depth:].astype(F32), 0.0)
    return got[:, :depth], jnp.sum(by_pair, axis=2), d_gate[None], d_up[None], d_down[None]


def solution(mesh):
    along = flips(mesh)
    small = mesh.shape["et"] == 2
    placed = (
        P(("exp", "et"), None),
        P(("exp", "et"), None),
        P(("exp", "et"), None),
        P(("exp", "et"), None),
        P("exp", None, "et"),
        P("exp", None, "et"),
        P("exp", "et", None),
    )
    return jax.shard_map(
        functools.partial(on_device if small else on_device_large, along),
        mesh=mesh,
        in_specs=placed,
        out_specs=(placed[0], placed[0], placed[4], placed[5], placed[6]),
        check_vma=False,
    )
```

time: 181 us -> 131 us (0.72)
  blocking collectives: 61.5 us -> 0 us
  Pallas kernels: 0 us -> 52 us
  matrix products: 39.7 us -> 0 us
  starting transfers between devices: 16 us -> 36.9 us
  between operations: 15.3 us -> 0.87 us
  local copies, waits for them, and re-layouts: 16.5 us -> 3.39 us
  waiting for transfers between devices: 28.4 us -> 34.7 us
    all_to_all x2 -> x0, blocking collectives: 56.6 us -> none  [the longest x1 29.7 us: on_device(): lax.all_to_all(buf_x, 'exp', split_axis=0, concat_axis=0, tiled=True)]
    pallas_call x0 -> x10, Pallas kernels: none -> 52 us  [the longest x2 14 us: inward(): pl.pallas_call(inward_kernel, grid=((stop - start) // size,), out_shape=j...]
    dot_general x8 -> x0, matrix products: 39.7 us -> none  [the longest x1 6.01 us: expert_terms(): lax.dot_general(rows_dy, w_down, (((1,), (1,)), ((), ())), preferred_elem...]
    ppermute x0 -> x32, starting transfers between devices: none -> 36.9 us  [send(): return lax.ppermute(block, AXES, pairs)]
    ppermute x0 -> x32, waiting for transfers between devices: none -> 34.7 us  [send(): return lax.ppermute(block, AXES, pairs)]
    reduce_scatter x1 -> x0, waiting for transfers between devices: 16.8 us -> none  [on_device(): lax.psum_scatter(folded[3].astype(jnp.bfloat16), 'et', scatter_dimension=...]
    all_to_all x3 -> x0, starting transfers between devices: 15.9 us -> none  [the longest x1 5.8 us: on_device(): lax.all_to_all(score_all.astype(jnp.bfloat16), 'exp', split_axis=0, conca...]
    all_to_all x3 -> x0, waiting for transfers between devices: 8.75 us -> none  [the longest x1 5.02 us: on_device(): lax.all_to_all(buf_g, 'exp', split_axis=0, concat_axis=0, tiled=True)]
  transfers between devices with their start and end apart: 6 -> 32, of which waited for: 4 -> 13; matrix products, arithmetic and copies ran while one was open for 19% -> 1% of each run, Pallas kernels for 0% -> 27%
where the time goes in v1:
time: 131 us; the launch traced here: 130 us
  Pallas kernels  52 us (40%)
  starting transfers between devices  36.9 us (28%)
  waiting for transfers between devices  34.7 us (26%)
  local copies, waits for them, and re-layouts  3.39 us (3%)
  other arithmetic  2.15 us (2%)
    ppermute x32, starting transfers between devices, send(): return lax.ppermute(block, AXES, pairs)  36.9 us
    ppermute x32, waiting for transfers between devices, send(): return lax.ppermute(block, AXES, pairs)  34.7 us
    pallas_call x2, Pallas kernels, inward(): pl.pallas_call(inward_kernel, grid=((stop - start) // size,), out_shape=j...  14 us
    pallas_call x2, Pallas kernels, outer_tall(): pl.pallas_call(outer_kernel, grid=(depth // size,), out_shape=jax.ShapeDt...  11.8 us
    pallas_call x1, Pallas kernels, into_hidden(): pl.pallas_call(functools.partial(in_kernel, n, depth), grid=(depth // siz...  10.6 us
    pallas_call x1, Pallas kernels, back_hidden(): pl.pallas_call(functools.partial(back_kernel, n), grid=(depth // size,),...  9.46 us
    pallas_call x1, Pallas kernels, outer_wide(): pl.pallas_call(outer_kernel, grid=(depth // size,), out_shape=jax.ShapeDt...  5.89 us
    unnamed x14, local copies, waits for them, and re-layouts  3.17 us
  transfers between devices with their start and end apart: 32, of which 13 were waited for; matrix products, arithmetic and copies ran while one was open for 1% of the time, Pallas kernels for 27%

profile of v1, /device:TPU:0, one launch (start us, length us, event | category | flops | bytes accessed | tf_op | source)
XLA Modules:
  0.0 130.0 jit_solution(2949207321689837018)
XLA Ops:
  0.6 0.9 copy-done.2
  1.5 0.9 copy-done.3
  2.4 0.7 copy-done.4
  3.1 0.7 copy-done.6
  3.9 5.1 %collective-permute-start.12 = (bf16[24,1920]{1,0:T(8,128)(2,1)S(1)}, bf16[24,1920]{1,0:T(8,128)(2,1)S(1)}, u32[]{:S(2)}, u32[]{:S(2)}) collective-permute-start(bf16[24,1920]{1,0:T(8,128)(2,1)S(1)} %get-tuple-element.18.refs_0_), channel_id=1, source_target_pairs={{0,24},{1,25},{2,26},{3,27},{4,28},{5,29},{6,30},{7,31},{8,16},{9,... | collective-permute-start | bytes 276488 | tf_op jit(solution)/shard_map/ppermute | solution.py:48
  9.0 0.6 collective-permute-start.10
  9.7 3.7 %collective-permute-start.2 = (bf16[24,1792]{1,0:T(8,128)(2,1)S(1)}, bf16[24,1792]{1,0:T(8,128)(2,1)S(1)}, u32[]{:S(2)}, u32[]{:S(2)}) collective-permute-start(bf16[24,1792]{1,0:T(8,128)(2,1)S(1)} %get-tuple-element.17.refs_0_), channel_id=1, source_target_pairs={{0,24},{1,25},{2,26},{3,27},{4,28},{5,29},{6,30},{7,31},{8,16},{9,... | collective-permute-start | bytes 258056 | tf_op jit(solution)/shard_map/ppermute | solution.py:48
  13.4 5.3 %collective-permute-start = (bf16[24,1792]{1,0:T(8,128)(2,1)S(1)}, bf16[24,1792]{1,0:T(8,128)(2,1)S(1)}, u32[]{:S(2)}, u32[]{:S(2)}) collective-permute-start(bf16[24,1792]{1,0:T(8,128)(2,1)S(1)} %get-tuple-element.17.refs_0_), channel_id=1, source_target_pairs={{0,8},{1,9},{2,10},{3,11},{4,12},{5,13},{6,14},{7,15},{8,0},{9,1},... | collective-permute-start | bytes 258056 | tf_op jit(solution)/shard_map/ppermute | solution.py:48
  18.8 2.7 %collective-permute-done.11.refs_2_ = bf16[24,1920]{1,0:T(8,128)(2,1)S(1)} collective-permute-done((bf16[24,1920]{1,0:T(8,128)(2,1)S(1)}, bf16[24,1920]{1,0:T(8,128)(2,1)S(1)}, u32[]{:S(2)}, u32[]{:S(2)}) %collective-permute-start.11) | collective-permute-done | bytes 92192 | tf_op jit(solution)/shard_map/ppermute | solution.py:48
  21.5 1.6 %collective-permute-start.13 = (bf16[24,7296]{1,0:T(8,128)(2,1)S(1)}, bf16[24,7296]{1,0:T(8,128)(2,1)S(1)}, u32[]{:S(2)}, u32[]{:S(2)}) collective-permute-start(bf16[24,7296]{1,0:T(8,128)(2,1)S(1)} %unpack.3.refs_0_), channel_id=1, source_target_pairs={{0,4},{1,5},{2,3},{3,2},{4,0},{5,1},{6,7},{7,6},{8,12},{9,13},{10,... | collective-permute-start | bytes 1050632 | tf_op jit(solution)/shard_map/ppermute | solution.py:48
  23.1 1.5 %collective-permute-start.14 = (bf16[24,7296]{1,0:T(8,128)(2,1)S(1)}, bf16[24,7296]{1,0:T(8,128)(2,1)S(1)}, u32[]{:S(2)}, u32[]{:S(2)}) collective-permute-start(bf16[24,7296]{1,0:T(8,128)(2,1)S(1)} %unpack.3.refs_0_), channel_id=1, source_target_pairs={{0,1},{1,0},{2,6},{3,7},{4,5},{5,4},{6,2},{7,3},{8,9},{9,8},{10,14... | collective-permute-start | bytes 1050632 | tf_op jit(solution)/shard_map/ppermute | solution.py:48
  24.7 1.1 collective-permute-start.4
  25.8 1.5 %collective-permute-start.3 = (bf16[24,7168]{1,0:T(8,128)(2,1)S(1)}, bf16[24,7168]{1,0:T(8,128)(2,1)}, u32[]{:S(2)}, u32[]{:S(2)}) collective-permute-start(bf16[24,7168]{1,0:T(8,128)(2,1)S(1)} %unpack.2.refs_0_), channel_id=1, source_target_pairs={{0,4},{1,5},{2,3},{3,2},{4,0},{5,1},{6,7},{7,6},{8,12},{9,13},{10,... | collective-permute-start | bytes 1032200 | tf_op jit(solution)/shard_map/ppermute | solution.py:48
  27.3 5.4 %collective-permute-done.13.refs_1_ = bf16[24,7296]{1,0:T(8,128)(2,1)S(1)} collective-permute-done((bf16[24,7296]{1,0:T(8,128)(2,1)S(1)}, bf16[24,7296]{1,0:T(8,128)(2,1)S(1)}, u32[]{:S(2)}, u32[]{:S(2)}) %collective-permute-start.13) | collective-permute-done | bytes 350240 | tf_op jit(solution)/shard_map/ppermute | solution.py:48
  32.7 0.9 collective-permute-start.15
  33.8 0.3 collective-permute-start.18
  34.2 3.6 %collective-permute-done.4.refs_2_ = bf16[24,7168]{1,0:T(8,128)(2,1)S(1)} collective-permute-done((bf16[24,7168]{1,0:T(8,128)(2,1)S(1)}, bf16[24,7168]{1,0:T(8,128)(2,1)S(1)}, u32[]{:S(2)}, u32[]{:S(2)}) %collective-permute-start.4) | collective-permute-done | bytes 344096 | tf_op jit(solution)/shard_map/ppermute | solution.py:48
  37.8 2.4 %collective-permute-done.3.refs_1_ = bf16[24,7168]{1,0:T(8,128)(2,1)} collective-permute-done((bf16[24,7168]{1,0:T(8,128)(2,1)S(1)}, bf16[24,7168]{1,0:T(8,128)(2,1)}, u32[]{:S(2)}, u32[]{:S(2)}) %collective-permute-start.3) | collective-permute-done | bytes 344096 | tf_op jit(solution)/shard_map/ppermute | solution.py:48
  40.2 0.9 collective-permute-start.5
  41.1 0.4 collective-permute-done.15.refs_3_
  41.5 0.5 collective-permute-start.6
  42.1 5.7 %collective-permute-done.5.refs_3_ = bf16[24,7168]{1,0:T(8,128)(2,1)} collective-permute-done((bf16[24,7168]{1,0:T(8,128)(2,1)}, bf16[24,7168]{1,0:T(8,128)(2,1)}, u32[]{:S(2)}, u32[]{:S(2)}) %collective-permute-start.5) | collective-permute-done | bytes 344096 | tf_op jit(solution)/shard_map/ppermute | solution.py:48
  47.8 0.5 collective-permute-start.8
  48.3 10.6 %into_hidden.1 = (bf16[192,7168]{1,0:T(8,128)(2,1)}, f32[192,512]{1,0:T(8,128)S(1)}, f32[192,512]{1,0:T(8,128)S(1)}, f32[192,512]{1,0:T(8,128)S(1)}, bf16[192,51...) custom-call(s32[1]{0:T(128)} %bitcast.mine_ref, bf16[24,7296]{1,0:T(8,128)(2,1)S(1)} %unpack.3.refs_0_, ...), custom_call_target="tpu_custom_call" | custom-call | tf_op jit(solution)/shard_map/into_hidden/pallas_call | solution.py:155
  58.9 9.5 %back_hidden.1 = (bf16[192,7168]{1,0:T(8,128)(2,1)}, bf16[192,512]{1,0:T(8,128)(2,1)S(1)}, bf16[192,512]{1,0:T(8,128)(2,1)S(1)}, bf16[192,128]{1,0:T(8,128)(2,1)S(1)}) custom-call(bf16[24,7168]{1,0:T(8,128)(2,1)S(1)} %unpack.2.refs_0_, bf16[24,7168]{1,0:T(8,128)(2,1)} %collective-permute-done.3.refs_1_, bf16[24,7168]{1,0:T(8,128)(2,1)S(1)} %collective-permute-done.4.refs_2_, ...), custom_call_target="tpu_custom_call" | custom-call | tf_op jit(solution)/shard_map/back_hidden/pallas_call | solution.py:202
  68.4 6.9 %inward.2 = bf16[192,3584]{1,0:T(8,128)(2,1)S(1)} custom-call(bf16[192,512]{1,0:T(8,128)(2,1)S(1)} %get-tuple-element.23.gg.b, bf16[192,512]{1,0:T(8,128)(2,1)S(1)} %get-tuple-element.24.gu.b, bf16[1,7168,512]{2,1,0:T(8,128)(2,1)} %wg.3, bf16[1,7168,512]{2,1,0:T(8,128)(2,1)} %wu.3), custom_call_target="tpu_custom_call" | custom-call | tf_op jit(solution)/shard_map/inward/pallas_call | solution.py:228
  75.3 0.5 collective-permute-start.20
  75.8 7.1 %inward.3 = bf16[192,3584]{1,0:T(8,128)(2,1)S(1)} custom-call(bf16[192,512]{1,0:T(8,128)(2,1)S(1)} %get-tuple-element.23.gg.b, bf16[192,512]{1,0:T(8,128)(2,1)S(1)} %get-tuple-element.24.gu.b, bf16[1,7168,512]{2,1,0:T(8,128)(2,1)} %wg.3, bf16[1,7168,512]{2,1,0:T(8,128)(2,1)} %wu.3), custom_call_target="tpu_custom_call" | custom-call | tf_op jit(solution)/shard_map/inward/pallas_call | solution.py:228
  82.9 5.9 %outer_tall.3 = bf16[1,7168,512]{2,1,0:T(8,128)(2,1)} custom-call(bf16[192,7168]{1,0:T(8,128)(2,1)S(1)} %copy-done, bf16[192,512]{1,0:T(8,128)(2,1)S(1)} %get-tuple-element.24.gu.b), custom_call_target="tpu_custom_call" | custom-call | tf_op jit(solution)/shard_map/outer_tall/pallas_call | solution.py:246
  88.8 5.9 %outer_tall.2 = bf16[1,7168,512]{2,1,0:T(8,128)(2,1)} custom-call(bf16[192,7168]{1,0:T(8,128)(2,1)S(1)} %copy-done, bf16[192,512]{1,0:T(8,128)(2,1)S(1)} %get-tuple-element.23.gg.b), custom_call_target="tpu_custom_call" | custom-call | tf_op jit(solution)/shard_map/outer_tall/pallas_call | solution.py:246
  95.0 5.9 %outer_wide.1 = bf16[1,512,7168]{2,1,0:T(8,128)(2,1)} custom-call(bf16[192,512]{1,0:T(8,128)(2,1)S(1)} %get-tuple-element.27.a, bf16[192,7168]{1,0:T(8,128)(2,1)S(1)} %copy-done.1), custom_call_target="tpu_custom_call" | custom-call | tf_op jit(solution)/shard_map/outer_wide/pallas_call | solution.py:260
  101.1 1.0 collective-permute-start.21
  102.3 1.2 collective-permute-start.27
  103.4 5.0 %collective-permute-done.21 = bf16[48,3584]{1,0:T(8,128)(2,1)S(1)} collective-permute-done((bf16[48,3584]{1,0:T(8,128)(2,1)S(1)}, bf16[48,3584]{1,0:T(8,128)(2,1)S(1)}, u32[]{:S(2)}, u32[]{:S(2)}) %collective-permute-start.21) | collective-permute-done | bytes 344096 | tf_op jit(solution)/shard_map/ppermute | solution.py:48
  108.5 1.6 %collective-permute-start.22 = (bf16[24,3584]{1,0:T(8,128)(2,1)S(1)}, bf16[24,3584]{1,0:T(8,128)(2,1)S(1)}, u32[]{:S(2)}, u32[]{:S(2)}) collective-permute-start(bf16[24,3584]{1,0:T(8,128)(2,1)S(1)} %slice.93), channel_id=1, source_target_pairs={{0,4},{1,5},{2,3},{3,2},{4,0},{5,1},{6,7},{7,6},{8,12},{9,13},{10,... | collective-permute-start | bytes 516104 | tf_op jit(solution)/shard_map/ppermute | solution.py:48
  110.1 3.5 %collective-permute-done.27 = bf16[48,3712]{1,0:T(8,128)(2,1)S(1)} collective-permute-done((bf16[48,3712]{1,0:T(8,128)(2,1)S(1)}, bf16[48,3712]{1,0:T(8,128)(2,1)S(1)}, u32[]{:S(2)}, u32[]{:S(2)}) %collective-permute-start.27) | collective-permute-done | bytes 356384 | tf_op jit(solution)/shard_map/ppermute | solution.py:48
  113.7 1.6 %collective-permute-start.28 = (bf16[24,3712]{1,0:T(8,128)(2,1)S(1)}, bf16[24,3712]{1,0:T(8,128)(2,1)S(1)}, u32[]{:S(2)}, u32[]{:S(2)}) collective-permute-start(bf16[24,3712]{1,0:T(8,128)(2,1)S(1)} %slice.103), channel_id=1, source_target_pairs={{0,4},{1,5},{2,3},{3,2},{4,0},{5,1},{6,7},{7,6},{8,12},{9,13},{10,... | collective-permute-start | bytes 534536 | tf_op jit(solution)/shard_map/ppermute | solution.py:48
  115.5 2.2 %collective-permute-start.25 = (bf16[6,3584]{1,0:T(8,128)(2,1)S(1)}, bf16[6,3584]{1,0:T(8,128)(2,1)S(1)}, u32[]{:S(2)}, u32[]{:S(2)}) collective-permute-start(bf16[6,3584]{1,0:T(8,128)(2,1)S(1)} %get-tuple-element.33), channel_id=1, source_target_pairs={{0,24},{1,25},{2,26},{3,27},{4,28},{5,29},{6,30},{7,31},{8,16},{9,... | collective-permute-start | bytes 129032 | tf_op jit(solution)/shard_map/ppermute | solution.py:48
  117.7 1.2 collective-permute-start.24
  119.0 0.3 collective-permute-done.28
  119.4 0.8 collective-permute-start.29
  120.1 2.2 %collective-permute-start.31 = (bf16[6,3712]{1,0:T(8,128)(2,1)S(1)}, bf16[6,3712]{1,0:T(8,128)(2,1)S(1)}, u32[]{:S(2)}, u32[]{:S(2)}) collective-permute-start(bf16[6,3712]{1,0:T(8,128)(2,1)S(1)} %get-tuple-element.30), channel_id=1, source_target_pairs={{0,24},{1,25},{2,26},{3,27},{4,28},{5,29},{6,30},{7,31},{8,16},{9,... | collective-permute-start | bytes 133640 | tf_op jit(solution)/shard_map/ppermute | solution.py:48
  122.3 0.6 collective-permute-start.30
  122.9 2.7 %collective-permute-done.24 = bf16[6,3584]{1,0:T(8,128)(2,1)S(1)} collective-permute-done((bf16[6,3584]{1,0:T(8,128)(2,1)S(1)}, bf16[6,3584]{1,0:T(8,128)(2,1)S(1)}, u32[]{:S(2)}, u32[]{:S(2)}) %collective-permute-start.24) | collective-permute-done | bytes 43040 | tf_op jit(solution)/shard_map/ppermute | solution.py:48
  125.7 0.6 collective-permute-done.31
  126.2 2.3 %collective-permute-done.30 = bf16[6,3712]{1,0:T(8,128)(2,1)S(1)} collective-permute-done((bf16[6,3712]{1,0:T(8,128)(2,1)S(1)}, bf16[6,3712]{1,0:T(8,128)(2,1)S(1)}, u32[]{:S(2)}, u32[]{:S(2)}) %collective-permute-start.30) | collective-permute-done | bytes 44576 | tf_op jit(solution)/shard_map/ppermute | solution.py:48
  128.6 0.7 select_reduce_fusion
  129.3 0.7 pad_maximum_fusion.1
  (60 shorter events, 1.8 us)
Async XLA Ops:
  0.6 0.9 copy-start.2
  1.5 0.9 copy-start.3
  2.4 0.7 copy-start.4
  3.1 0.7 copy-start.6
  3.9 9.5 %collective-permute-start.12 = (bf16[24,1920]{1,0:T(8,128)(2,1)S(1)}, bf16[24,1920]{1,0:T(8,128)(2,1)S(1)}, u32[]{:S(2)}, u32[]{:S(2)}) collective-permute-start(bf16[24,1920]{1,0:T(8,128)(2,1)S(1)} %get-tuple-element.18.refs_0_), channel_id=1, source_target_pairs={{0,24},{1,25},{2,26},{3,27},{4,28},{5,29},{6,30},{7,31},{8,16},{9,... | collective-permute-start | bytes 276488 | tf_op jit(solution)/shard_map/ppermute | solution.py:48
  9.0 12.4 %collective-permute-start.11 = (bf16[24,1920]{1,0:T(8,128)(2,1)S(1)}, bf16[24,1920]{1,0:T(8,128)(2,1)S(1)}, u32[]{:S(2)}, u32[]{:S(2)}) collective-permute-start(bf16[24,1920]{1,0:T(8,128)(2,1)S(1)} %get-tuple-element.18.refs_0_), channel_id=1, source_target_pairs={{0,16},{1,17},{2,18},{3,19},{4,20},{5,21},{6,22},{7,23},{8,24},{9,... | collective-permute-start | bytes 276488 | tf_op jit(solution)/shard_map/ppermute | solution.py:48
  9.0 12.4 %collective-permute-start.10 = (bf16[24,1920]{1,0:T(8,128)(2,1)S(1)}, bf16[24,1920]{1,0:T(8,128)(2,1)S(1)}, u32[]{:S(2)}, u32[]{:S(2)}) collective-permute-start(bf16[24,1920]{1,0:T(8,128)(2,1)S(1)} %get-tuple-element.18.refs_0_), channel_id=1, source_target_pairs={{0,8},{1,9},{2,10},{3,11},{4,12},{5,13},{6,14},{7,15},{8,0},{9,1},... | collective-permute-start | bytes 276488 | tf_op jit(solution)/shard_map/ppermute | solution.py:48
  9.7 14.9 %collective-permute-start.2 = (bf16[24,1792]{1,0:T(8,128)(2,1)S(1)}, bf16[24,1792]{1,0:T(8,128)(2,1)S(1)}, u32[]{:S(2)}, u32[]{:S(2)}) collective-permute-start(bf16[24,1792]{1,0:T(8,128)(2,1)S(1)} %get-tuple-element.17.refs_0_), channel_id=1, source_target_pairs={{0,24},{1,25},{2,26},{3,27},{4,28},{5,29},{6,30},{7,31},{8,16},{9,... | collective-permute-start | bytes 258056 | tf_op jit(solution)/shard_map/ppermute | solution.py:48
  13.4 11.2 %collective-permute-start.1 = (bf16[24,1792]{1,0:T(8,128)(2,1)S(1)}, bf16[24,1792]{1,0:T(8,128)(2,1)S(1)}, u32[]{:S(2)}, u32[]{:S(2)}) collective-permute-start(bf16[24,1792]{1,0:T(8,128)(2,1)S(1)} %get-tuple-element.17.refs_0_), channel_id=1, source_target_pairs={{0,16},{1,17},{2,18},{3,19},{4,20},{5,21},{6,22},{7,23},{8,24},{9,... | collective-permute-start | bytes 258056 | tf_op jit(solution)/shard_map/ppermute | solution.py:48
  13.4 11.2 %collective-permute-start = (bf16[24,1792]{1,0:T(8,128)(2,1)S(1)}, bf16[24,1792]{1,0:T(8,128)(2,1)S(1)}, u32[]{:S(2)}, u32[]{:S(2)}) collective-permute-start(bf16[24,1792]{1,0:T(8,128)(2,1)S(1)} %get-tuple-element.17.refs_0_), channel_id=1, source_target_pairs={{0,8},{1,9},{2,10},{3,11},{4,12},{5,13},{6,14},{7,15},{8,0},{9,1},... | collective-permute-start | bytes 258056 | tf_op jit(solution)/shard_map/ppermute | solution.py:48
  21.5 11.2 %collective-permute-start.13 = (bf16[24,7296]{1,0:T(8,128)(2,1)S(1)}, bf16[24,7296]{1,0:T(8,128)(2,1)S(1)}, u32[]{:S(2)}, u32[]{:S(2)}) collective-permute-start(bf16[24,7296]{1,0:T(8,128)(2,1)S(1)} %unpack.3.refs_0_), channel_id=1, source_target_pairs={{0,4},{1,5},{2,3},{3,2},{4,0},{5,1},{6,7},{7,6},{8,12},{9,13},{10,... | collective-permute-start | bytes 1050632 | tf_op jit(solution)/shard_map/ppermute | solution.py:48
  23.1 10.7 %collective-permute-start.14 = (bf16[24,7296]{1,0:T(8,128)(2,1)S(1)}, bf16[24,7296]{1,0:T(8,128)(2,1)S(1)}, u32[]{:S(2)}, u32[]{:S(2)}) collective-permute-start(bf16[24,7296]{1,0:T(8,128)(2,1)S(1)} %unpack.3.refs_0_), channel_id=1, source_target_pairs={{0,1},{1,0},{2,6},{3,7},{4,5},{5,4},{6,2},{7,3},{8,9},{9,8},{10,14... | collective-permute-start | bytes 1050632 | tf_op jit(solution)/shard_map/ppermute | solution.py:48
  24.7 13.1 %collective-permute-start.4 = (bf16[24,7168]{1,0:T(8,128)(2,1)S(1)}, bf16[24,7168]{1,0:T(8,128)(2,1)S(1)}, u32[]{:S(2)}, u32[]{:S(2)}) collective-permute-start(bf16[24,7168]{1,0:T(8,128)(2,1)S(1)} %unpack.2.refs_0_), channel_id=1, source_target_pairs={{0,1},{1,0},{2,6},{3,7},{4,5},{5,4},{6,2},{7,3},{8,9},{9,8},{10,14... | collective-permute-start | bytes 1032200 | tf_op jit(solution)/shard_map/ppermute | solution.py:48
  25.8 14.4 %collective-permute-start.3 = (bf16[24,7168]{1,0:T(8,128)(2,1)S(1)}, bf16[24,7168]{1,0:T(8,128)(2,1)}, u32[]{:S(2)}, u32[]{:S(2)}) collective-permute-start(bf16[24,7168]{1,0:T(8,128)(2,1)S(1)} %unpack.2.refs_0_), channel_id=1, source_target_pairs={{0,4},{1,5},{2,3},{3,2},{4,0},{5,1},{6,7},{7,6},{8,12},{9,13},{10,... | collective-permute-start | bytes 1032200 | tf_op jit(solution)/shard_map/ppermute | solution.py:48
  32.7 8.8 %collective-permute-start.15 = (bf16[24,7296]{1,0:T(8,128)(2,1)S(1)}, bf16[24,7296]{1,0:T(8,128)(2,1)S(1)}, u32[]{:S(2)}, u32[]{:S(2)}) collective-permute-start(bf16[24,7296]{1,0:T(8,128)(2,1)S(1)} %collective-permute-done.13.refs_1_), channel_id=1, source_target_pairs={{0,1},{1,0},{2,6},{3,7},{4,5},{5,4},{6,2},{7,3},{8,9},{9,8},{10,14... | collective-permute-start | bytes 1050632 | tf_op jit(solution)/shard_map/ppermute | solution.py:48
  33.6 7.9 %collective-permute-start.16 = (bf16[24,7296]{1,0:T(8,128)(2,1)S(1)}, bf16[24,7296]{1,0:T(8,128)(2,1)S(1)}, u32[]{:S(2)}, u32[]{:S(2)}) collective-permute-start(bf16[24,7296]{1,0:T(8,128)(2,1)S(1)} %unpack.3.refs_0_), channel_id=1, source_target_pairs={{0,2},{1,3},{2,0},{3,1},{4,6},{5,7},{6,4},{7,5},{8,10},{9,11},{10,... | collective-permute-start | bytes 1050632 | tf_op jit(solution)/shard_map/ppermute | solution.py:48
  33.8 13.9 %collective-permute-start.18 = (bf16[24,7296]{1,0:T(8,128)(2,1)S(1)}, bf16[24,7296]{1,0:T(8,128)(2,1)S(1)}, u32[]{:S(2)}, u32[]{:S(2)}) collective-permute-start(bf16[24,7296]{1,0:T(8,128)(2,1)S(1)} %collective-permute-done.14.refs_2_), channel_id=1, source_target_pairs={{0,2},{1,3},{2,0},{3,1},{4,6},{5,7},{6,4},{7,5},{8,10},{9,11},{10,... | collective-permute-start | bytes 1050632 | tf_op jit(solution)/shard_map/ppermute | solution.py:48
  37.8 10.5 %collective-permute-start.17 = (bf16[24,7296]{1,0:T(8,128)(2,1)S(1)}, bf16[24,7296]{1,0:T(8,128)(2,1)S(1)}, u32[]{:S(2)}, u32[]{:S(2)}) collective-permute-start(bf16[24,7296]{1,0:T(8,128)(2,1)S(1)} %collective-permute-done.13.refs_1_), channel_id=1, source_target_pairs={{0,2},{1,3},{2,0},{3,1},{4,6},{5,7},{6,4},{7,5},{8,10},{9,11},{10,... | collective-permute-start | bytes 1050632 | tf_op jit(solution)/shard_map/ppermute | solution.py:48
  40.2 7.6 %collective-permute-start.5 = (bf16[24,7168]{1,0:T(8,128)(2,1)}, bf16[24,7168]{1,0:T(8,128)(2,1)}, u32[]{:S(2)}, u32[]{:S(2)}) collective-permute-start(bf16[24,7168]{1,0:T(8,128)(2,1)} %collective-permute-done.3.refs_1_), channel_id=1, source_target_pairs={{0,1},{1,0},{2,6},{3,7},{4,5},{5,4},{6,2},{7,3},{8,9},{9,8},{10,14... | collective-permute-start | bytes 1032200 | tf_op jit(solution)/shard_map/ppermute | solution.py:48
  41.5 6.8 %collective-permute-start.19 = (bf16[24,7296]{1,0:T(8,128)(2,1)S(1)}, bf16[24,7296]{1,0:T(8,128)(2,1)S(1)}, u32[]{:S(2)}, u32[]{:S(2)}) collective-permute-start(bf16[24,7296]{1,0:T(8,128)(2,1)S(1)} %collective-permute-done.15.refs_3_), channel_id=1, source_target_pairs={{0,2},{1,3},{2,0},{3,1},{4,6},{5,7},{6,4},{7,5},{8,10},{9,11},{10,... | collective-permute-start | bytes 1050632 | tf_op jit(solution)/shard_map/ppermute | solution.py:48
  41.5 17.4 %collective-permute-start.6 = (bf16[24,7168]{1,0:T(8,128)(2,1)S(1)}, bf16[24,7168]{1,0:T(8,128)(2,1)}, u32[]{:S(2)}, u32[]{:S(2)}) collective-permute-start(bf16[24,7168]{1,0:T(8,128)(2,1)S(1)} %unpack.2.refs_0_), channel_id=1, source_target_pairs={{0,2},{1,3},{2,0},{3,1},{4,6},{5,7},{6,4},{7,5},{8,10},{9,11},{10,... | collective-permute-start | bytes 1032200 | tf_op jit(solution)/shard_map/ppermute | solution.py:48
  47.8 11.2 %collective-permute-start.7 = (bf16[24,7168]{1,0:T(8,128)(2,1)}, bf16[24,7168]{1,0:T(8,128)(2,1)}, u32[]{:S(2)}, u32[]{:S(2)}) collective-permute-start(bf16[24,7168]{1,0:T(8,128)(2,1)} %collective-permute-done.3.refs_1_), channel_id=1, source_target_pairs={{0,2},{1,3},{2,0},{3,1},{4,6},{5,7},{6,4},{7,5},{8,10},{9,11},{10,... | collective-permute-start | bytes 1032200 | tf_op jit(solution)/shard_map/ppermute | solution.py:48
  47.8 11.1 %collective-permute-start.8 = (bf16[24,7168]{1,0:T(8,128)(2,1)S(1)}, bf16[24,7168]{1,0:T(8,128)(2,1)}, u32[]{:S(2)}, u32[]{:S(2)}) collective-permute-start(bf16[24,7168]{1,0:T(8,128)(2,1)S(1)} %collective-permute-done.4.refs_2_), channel_id=1, source_target_pairs={{0,2},{1,3},{2,0},{3,1},{4,6},{5,7},{6,4},{7,5},{8,10},{9,11},{10,... | collective-permute-start | bytes 1032200 | tf_op jit(solution)/shard_map/ppermute | solution.py:48
  48.3 10.7 %collective-permute-start.9 = (bf16[24,7168]{1,0:T(8,128)(2,1)}, bf16[24,7168]{1,0:T(8,128)(2,1)}, u32[]{:S(2)}, u32[]{:S(2)}) collective-permute-start(bf16[24,7168]{1,0:T(8,128)(2,1)} %collective-permute-done.5.refs_3_), channel_id=1, source_target_pairs={{0,2},{1,3},{2,0},{3,1},{4,6},{5,7},{6,4},{7,5},{8,10},{9,11},{10,... | collective-permute-start | bytes 1032200 | tf_op jit(solution)/shard_map/ppermute | solution.py:48
  75.3 25.5 %collective-permute-start.20 = (bf16[96,3584]{1,0:T(8,128)(2,1)S(1)}, bf16[96,3584]{1,0:T(8,128)(2,1)S(1)}, u32[]{:S(2)}, u32[]{:S(2)}) collective-permute-start(bf16[96,3584]{1,0:T(8,128)(2,1)S(1)} %slice.89), channel_id=1, source_target_pairs={{0,2},{1,3},{2,0},{3,1},{4,6},{5,7},{6,4},{7,5},{8,10},{9,11},{10,... | collective-permute-start | bytes 2064392 | tf_op jit(solution)/shard_map/ppermute | solution.py:48
  75.8 7.1 %copy-start = (bf16[192,7168]{1,0:T(8,128)(2,1)S(1)}, bf16[192,7168]{1,0:T(8,128)(2,1)}, u32[]{:S(2)}) copy-start(bf16[192,7168]{1,0:T(8,128)(2,1)} %get-tuple-element.26.a) | copy-start | bytes 8257540
  88.8 6.1 %copy-start.1 = (bf16[192,7168]{1,0:T(8,128)(2,1)S(1)}, bf16[192,7168]{1,0:T(8,128)(2,1)}, u32[]{:S(2)}) copy-start(bf16[192,7168]{1,0:T(8,128)(2,1)} %get-tuple-element.28.b) | copy-start | bytes 8257540
  94.8 7.2 %collective-permute-start.26 = (bf16[96,3712]{1,0:T(8,128)(2,1)S(1)}, bf16[96,3712]{1,0:T(8,128)(2,1)S(1)}, u32[]{:S(2)}, u32[]{:S(2)}) collective-permute-start(bf16[96,3712]{1,0:T(8,128)(2,1)S(1)} %pad_maximum_fusion), channel_id=1, source_target_pairs={{0,2},{1,3},{2,0},{3,1},{4,6},{5,7},{6,4},{7,5},{8,10},{9,11},{10,... | collective-permute-start | bytes 2138120 | tf_op jit(solution)/shard_map/ppermute | solution.py:48
  101.1 7.3 %collective-permute-start.21 = (bf16[48,3584]{1,0:T(8,128)(2,1)S(1)}, bf16[48,3584]{1,0:T(8,128)(2,1)S(1)}, u32[]{:S(2)}, u32[]{:S(2)}) collective-permute-start(bf16[48,3584]{1,0:T(8,128)(2,1)S(1)} %slice.91), channel_id=1, source_target_pairs={{0,1},{1,0},{2,6},{3,7},{4,5},{5,4},{6,2},{7,3},{8,9},{9,8},{10,14... | collective-permute-start | bytes 1032200 | tf_op jit(solution)/shard_map/ppermute | solution.py:48
  102.3 11.3 %collective-permute-start.27 = (bf16[48,3712]{1,0:T(8,128)(2,1)S(1)}, bf16[48,3712]{1,0:T(8,128)(2,1)S(1)}, u32[]{:S(2)}, u32[]{:S(2)}) collective-permute-start(bf16[48,3712]{1,0:T(8,128)(2,1)S(1)} %slice.101), channel_id=1, source_target_pairs={{0,1},{1,0},{2,6},{3,7},{4,5},{5,4},{6,2},{7,3},{8,9},{9,8},{10,14... | collective-permute-start | bytes 1069064 | tf_op jit(solution)/shard_map/ppermute | solution.py:48
  108.5 6.8 %collective-permute-start.22 = (bf16[24,3584]{1,0:T(8,128)(2,1)S(1)}, bf16[24,3584]{1,0:T(8,128)(2,1)S(1)}, u32[]{:S(2)}, u32[]{:S(2)}) collective-permute-start(bf16[24,3584]{1,0:T(8,128)(2,1)S(1)} %slice.93), channel_id=1, source_target_pairs={{0,4},{1,5},{2,3},{3,2},{4,0},{5,1},{6,7},{7,6},{8,12},{9,13},{10,... | collective-permute-start | bytes 516104 | tf_op jit(solution)/shard_map/ppermute | solution.py:48
  113.7 14.9 %copy-start.5 = (s32[6,8]{1,0:T(8,128)S(1)}, s32[6,8]{1,0:T(8,128)}, u32[]{:S(2)}) copy-start(s32[6,8]{1,0:T(8,128)} %id_ref.1) | copy-start | bytes 580
  113.7 5.5 %collective-permute-start.28 = (bf16[24,3712]{1,0:T(8,128)(2,1)S(1)}, bf16[24,3712]{1,0:T(8,128)(2,1)S(1)}, u32[]{:S(2)}, u32[]{:S(2)}) collective-permute-start(bf16[24,3712]{1,0:T(8,128)(2,1)S(1)} %slice.103), channel_id=1, source_target_pairs={{0,4},{1,5},{2,3},{3,2},{4,0},{5,1},{6,7},{7,6},{8,12},{9,13},{10,... | collective-permute-start | bytes 534536 | tf_op jit(solution)/shard_map/ppermute | solution.py:48
  115.4 6.9 %collective-permute-start.23 = (bf16[6,3584]{1,0:T(8,128)(2,1)S(1)}, bf16[6,3584]{1,0:T(8,128)(2,1)S(1)}, u32[]{:S(2)}, u32[]{:S(2)}) collective-permute-start(bf16[6,3584]{1,0:T(8,128)(2,1)S(1)} %get-tuple-element.32), channel_id=1, source_target_pairs={{0,8},{1,9},{2,10},{3,11},{4,12},{5,13},{6,14},{7,15},{8,0},{9,1},... | collective-permute-start | bytes 129032 | tf_op jit(solution)/shard_map/ppermute | solution.py:48
  115.5 7.4 %collective-permute-start.25 = (bf16[6,3584]{1,0:T(8,128)(2,1)S(1)}, bf16[6,3584]{1,0:T(8,128)(2,1)S(1)}, u32[]{:S(2)}, u32[]{:S(2)}) collective-permute-start(bf16[6,3584]{1,0:T(8,128)(2,1)S(1)} %get-tuple-element.33), channel_id=1, source_target_pairs={{0,24},{1,25},{2,26},{3,27},{4,28},{5,29},{6,30},{7,31},{8,16},{9,... | collective-permute-start | bytes 129032 | tf_op jit(solution)/shard_map/ppermute | solution.py:48
  117.7 7.9 %collective-permute-start.24 = (bf16[6,3584]{1,0:T(8,128)(2,1)S(1)}, bf16[6,3584]{1,0:T(8,128)(2,1)S(1)}, u32[]{:S(2)}, u32[]{:S(2)}) collective-permute-start(bf16[6,3584]{1,0:T(8,128)(2,1)S(1)} %get-tuple-element.34), channel_id=1, source_target_pairs={{0,16},{1,17},{2,18},{3,19},{4,20},{5,21},{6,22},{7,23},{8,24},{9,... | collective-permute-start | bytes 129032 | tf_op jit(solution)/shard_map/ppermute | solution.py:48
  119.4 6.3 %collective-permute-start.29 = (bf16[6,3712]{1,0:T(8,128)(2,1)S(1)}, bf16[6,3712]{1,0:T(8,128)(2,1)S(1)}, u32[]{:S(2)}, u32[]{:S(2)}) collective-permute-start(bf16[6,3712]{1,0:T(8,128)(2,1)S(1)} %get-tuple-element.29), channel_id=1, source_target_pairs={{0,8},{1,9},{2,10},{3,11},{4,12},{5,13},{6,14},{7,15},{8,0},{9,1},... | collective-permute-start | bytes 133640 | tf_op jit(solution)/shard_map/ppermute | solution.py:48
  120.1 6.1 %collective-permute-start.31 = (bf16[6,3712]{1,0:T(8,128)(2,1)S(1)}, bf16[6,3712]{1,0:T(8,128)(2,1)S(1)}, u32[]{:S(2)}, u32[]{:S(2)}) collective-permute-start(bf16[6,3712]{1,0:T(8,128)(2,1)S(1)} %get-tuple-element.30), channel_id=1, source_target_pairs={{0,24},{1,25},{2,26},{3,27},{4,28},{5,29},{6,30},{7,31},{8,16},{9,... | collective-permute-start | bytes 133640 | tf_op jit(solution)/shard_map/ppermute | solution.py:48
  122.3 6.2 %collective-permute-start.30 = (bf16[6,3712]{1,0:T(8,128)(2,1)S(1)}, bf16[6,3712]{1,0:T(8,128)(2,1)S(1)}, u32[]{:S(2)}, u32[]{:S(2)}) collective-permute-start(bf16[6,3712]{1,0:T(8,128)(2,1)S(1)} %get-tuple-element.31), channel_id=1, source_target_pairs={{0,16},{1,17},{2,18},{3,19},{4,20},{5,21},{6,22},{7,23},{8,24},{9,... | collective-permute-start | bytes 133640 | tf_op jit(solution)/shard_map/ppermute | solution.py:48

commit v2 on v1

v2 whole, which is shorter than its diff:
```python
import functools

import jax
import jax.numpy as jnp
from jax import lax
from jax.experimental import pallas as pl
from jax.experimental.pallas import tpu as pltpu
from jax.sharding import PartitionSpec as P

LANES = 128
SPLIT = 4
AXES = ("exp", "et")
F32, BF16 = jnp.float32, jnp.bfloat16
MIB = 1 << 20
HIDDEN_LIMIT = 36
INWARD_LIMIT = 52
VMEM = pl.BlockSpec(memory_space=pltpu.VMEM)
HBM = pl.BlockSpec(memory_space=pltpu.HBM)
ANY = pl.BlockSpec(memory_space=pl.ANY)


def flips(mesh):
    n_exp, n_et = mesh.shape["exp"], mesh.shape["et"]

    def perm(far):
        pairs = []
        for e in range(n_exp):
            for t in range(n_et):
                e2, t2 = far(e, t)
                pairs.append((e * n_et + t, e2 * n_et + t2))
        return pairs

    def flip_y(e, t):
        return e ^ 2, t

    def flip_x(k):
        return lambda e, t: (e, t ^ k)

    def by_core(first, second):
        return perm(lambda e, t: first(e, t) if e % 2 == 0 else second(e, t))

    along = {"z": [perm(lambda e, t, k=k: (e ^ (4 * k), t)) for k in range(1, n_exp // 4)]}
    along["core"] = perm(lambda e, t: (e ^ 1, t))
    along["y"] = perm(flip_y)
    along["x"] = [perm(flip_x(k)) for k in range(1, n_et)]
    along["first"] = by_core(flip_y, flip_x(1))
    along["second"] = by_core(flip_x(1), flip_y)
    return along


def send(block, pairs):
    return lax.ppermute(block, AXES, pairs)


def params(limit=None):
    return pltpu.CompilerParams(vmem_limit_bytes=(limit or 48) * MIB)


def cost(flops, bytes_accessed=0):
    return pl.CostEstimate(flops=flops, bytes_accessed=bytes_accessed, transcendentals=0)


def pack_kernel(x_hbm, dy_hbm, g_hbm, id_hbm, out, x, dy, g, ids, sem):
    copies = [pltpu.make_async_copy(*pair, sem.at[i]) for i, pair in enumerate(
        ((x_hbm, x), (dy_hbm, dy), (g_hbm, g), (id_hbm, ids)))]
    for copy in copies:
        copy.start()
    count, depth = x.shape
    part = depth // SPLIT
    wide = out.shape[1] - part
    out[:, part:] = jnp.zeros((out.shape[0], wide), BF16)
    for copy in copies:
        copy.wait()
    for kind, rows in enumerate((x, dy)):
        for j in range(SPLIT):
            top = (kind * SPLIT + j) * count
            out[top : top + count, :part] = rows[:, j * part : (j + 1) * part]
    lane = lax.broadcasted_iota(jnp.int32, (count, wide), 1)
    total = jnp.zeros((count, wide), F32)
    for k in range(g.shape[1]):
        total = total + jnp.where(ids[:, k : k + 1] == lane, g[:, k : k + 1].astype(F32), 0.0)
    out[:count, part:] = total.astype(BF16)


def pack(*args, wide):
    count, depth = args[0].shape
    return pl.pallas_call(
        pack_kernel,
        out_shape=pltpu.VMEM((2 * SPLIT * count, depth // SPLIT + wide), BF16),
        in_specs=[HBM] * 4,
        out_specs=VMEM,
        scratch_shapes=[pltpu.VMEM(v.shape, v.dtype) for v in args] + [pltpu.SemaphoreType.DMA((4,))],
        compiler_params=params(56),
        name="pack",
    )(*args)


def pair_kernel(count, part, a, b, out):
    for d, ref in enumerate((a, b)):
        for kind in range(2):
            for j in range(SPLIT):
                low = (kind * SPLIT + j) * count
                top = (2 * kind + j // 2) * 2 * count + d * count
                out[top : top + count, (j % 2) * part : (j % 2 + 1) * part] = ref[low : low + count, :part]
        out[d * count : (d + 1) * count, 2 * part :] = ref[:count, part:]


def pair(a, b, count, part):
    return pl.pallas_call(
        functools.partial(pair_kernel, count, part),
        out_shape=jax.ShapeDtypeStruct((2 * SPLIT * count, a.shape[1] + part), BF16),
        in_specs=[VMEM] * 2,
        out_specs=VMEM,
        compiler_params=params(4),
        name="pair",
    )(a, b)


def dot(a, b, over):
    return lax.dot_general(a, b, ((over[:1], over[1:]), ((), ())), preferred_element_type=F32)


def blocks_of(refs, height):
    return [(ref, top) for ref in refs for top in range(0, ref.shape[0], height)]


def assemble(out, near, far, height, kind):
    half = out.shape[1] // 2
    rows = height // 4
    for i, ((a, a_top), (b, b_top)) in enumerate(zip(blocks_of(near, height), blocks_of(far, height), strict=True)):
        for j in range(2):
            top = (2 * kind + j) * rows
            low, high = a[a_top + top : a_top + top + rows, :half], b[b_top + top : b_top + top + rows, :half]
            out[2 * i * rows : 2 * (i + 1) * rows, j * half : (j + 1) * half] = jnp.concatenate([low, high], axis=0)


def scales(near, far, height, first, mine):
    rows = height // 4
    ends = zip(blocks_of(near, height), blocks_of(far, height), strict=True)
    gates = [ref[top : top + rows, first:].astype(F32) for pair in ends for ref, top in pair]
    gates = jnp.concatenate(gates, axis=0)
    gates = jnp.where(lax.broadcasted_iota(jnp.int32, gates.shape, 1) == mine, gates, 0.0)
    return jnp.sum(gates, axis=1, keepdims=True), (gates != 0.0).astype(F32)


def hidden_kernel(n, height, size, mine_ref, *refs):
    near, far, refs = refs[:n], refs[n : 2 * n], refs[2 * n :]
    (wg_hbm, wu_hbm, wd_hbm), (x, dy, wt, gg, gu, score, low), refs = refs[:3], refs[3:10], refs[10:]
    wg, wu, wd, gate_acc, up_acc, sem = refs
    depth, ff = wg.shape
    parts = depth // size
    halves = [pl.ds(i * (ff // 2), ff // 2) for i in range(2)]
    steps = [pl.ds(i * size, size) for i in range(parts)]
    downs = [pltpu.make_async_copy(wd_hbm.at[0, h], wd.at[h], sem.at[i]) for i, h in enumerate(halves)]
    gates = [pltpu.make_async_copy(wg_hbm.at[0, c], wg.at[c], sem.at[2 + i]) for i, c in enumerate(steps)]
    ups = [pltpu.make_async_copy(wu_hbm.at[0, c], wu.at[c], sem.at[2 + parts + i]) for i, c in enumerate(steps)]
    for copy in downs:
        copy.start()
    for pair in zip(gates, ups, strict=True):
        for copy in pair:
            copy.start()
    assemble(dy, near, far, height, 1)
    assemble(x, near, far, height, 0)
    back = []
    for copy, h in zip(downs, halves, strict=True):
        copy.wait()
        back.append(dot(dy[...], wd[h, :], (1, 1)))
    back = jnp.concatenate(back, axis=1)
    for i, c in enumerate(steps):
        gates[i].wait()
        ups[i].wait()
        gate, up = dot(x[:, c], wg[c, :], (1, 0)), dot(x[:, c], wu[c, :], (1, 0))
        gate_acc[...] = gate if i == 0 else gate_acc[...] + gate
        up_acc[...] = up if i == 0 else up_acc[...] + up
    gate_pre, up_pre = gate_acc[...], up_acc[...]
    scale, named = scales(near, far, height, depth // 2, mine_ref[0])
    sigma = jax.nn.sigmoid(gate_pre)
    silu = gate_pre * sigma
    act = silu * up_pre
    wt[...] = (scale * act).astype(BF16)
    score[...] = (named * jnp.sum(act * back, axis=1, keepdims=True)).astype(BF16)
    dact = scale * back
    gg[...] = (dact * up_pre * sigma * (1.0 + gate_pre * (1.0 - sigma))).astype(BF16)
    gu[...] = (dact * silu).astype(BF16)
    for first in range(0, low.shape[1], 512):
        c = pl.ds(first, 512)
        low[:, c] = (dot(gg[...], wg[c, :], (1, 1)) + dot(gu[...], wu[c, :], (1, 1))).astype(BF16)


def hidden(mine, near, far, height, w_gate, w_up, w_down, wide):
    n = len(near)
    rows = sum(b.shape[0] for b in far) // 2
    depth, ff = w_gate.shape[1:]
    size = 1024
    full, half = jax.ShapeDtypeStruct((rows, depth), BF16), jax.ShapeDtypeStruct((rows, ff), BF16)
    return pl.pallas_call(
        functools.partial(hidden_kernel, n, height, size),
        out_shape=(
            full,
            full,
            half,
            half,
            half,
            jax.ShapeDtypeStruct((rows, wide), BF16),
            jax.ShapeDtypeStruct((rows, depth // 2), BF16),
        ),
        in_specs=[pl.BlockSpec(memory_space=pltpu.SMEM)] + [VMEM] * (2 * n) + [ANY] * 3,
        out_specs=(VMEM,) * 7,
        scratch_shapes=[
            pltpu.VMEM((depth, ff), BF16),
            pltpu.VMEM((depth, ff), BF16),
            pltpu.VMEM((ff, depth), BF16),
            pltpu.VMEM((rows, ff), F32),
            pltpu.VMEM((rows, ff), F32),
            pltpu.SemaphoreType.DMA((2 + 2 * (depth // size),)),
        ],
        compiler_params=params(HIDDEN_LIMIT),
        cost_estimate=cost(8 * rows * depth * ff, 6 * depth * ff),
        name="hidden",
    )(mine, *near, *far, w_gate, w_up, w_down)


def inward_kernel(start, size, gg, gu, score, wg_hbm, wu_hbm, out, wg, wu, sem):
    parts = [pl.ds(first, size) for first in range(0, wg.shape[0], size)]
    copies = []
    for i, c in enumerate(parts):
        there = pl.ds(start + i * size, size)
        pair = (
            pltpu.make_async_copy(wg_hbm.at[0, there], wg.at[c], sem.at[2 * i]),
            pltpu.make_async_copy(wu_hbm.at[0, there], wu.at[c], sem.at[2 * i + 1]),
        )
        for copy in pair:
            copy.start()
        copies.append(pair)
    out[:, wg.shape[0] :] = score[...]
    for pair, c in zip(copies, parts, strict=True):
        for copy in pair:
            copy.wait()
        out[:, c] = (dot(gg[...], wg[c, :], (1, 1)) + dot(gu[...], wu[c, :], (1, 1))).astype(BF16)


def inward(gg, gu, score, w_gate, w_up, start):
    rows, ff = gg.shape
    width, size = w_gate.shape[1] - start, 512
    return pl.pallas_call(
        functools.partial(inward_kernel, start, size),
        out_shape=jax.ShapeDtypeStruct((rows, width + score.shape[1]), BF16),
        in_specs=[VMEM] * 3 + [ANY] * 2,
        out_specs=VMEM,
        scratch_shapes=[pltpu.VMEM((width, ff), BF16)] * 2 + [pltpu.SemaphoreType.DMA((2 * (width // size),))],
        compiler_params=params(INWARD_LIMIT),
        cost_estimate=cost(4 * rows * width * ff, 4 * width * ff),
        name="inward",
    )(gg, gu, score, w_gate, w_up)


def outer_kernel(tall, size, a, b, after, out, done, sem):
    copies = []
    for i in range((a if tall else b).shape[1] // size):
        part = pl.ds(i * size, size)
        here = (part, slice(None)) if tall else (slice(None), part)
        left, right = (a[:, part], b[...]) if tall else (a[...], b[:, part])
        done[here] = dot(left, right, (0, 0)).astype(BF16)
        copies.append(pltpu.make_async_copy(done.at[here], out.at[(0, *here)], sem.at[i]))
        copies[-1].start()
    for copy in copies:
        copy.wait()


def outer(a, b, after):
    rows = a.shape[0]
    tall = a.shape[1] > b.shape[1]
    size = 1024
    shape = a.shape[1], b.shape[1]
    return pl.pallas_call(
        functools.partial(outer_kernel, tall, size),
        out_shape=jax.ShapeDtypeStruct((1, *shape), BF16),
        in_specs=[VMEM, VMEM, ANY],
        out_specs=ANY,
        scratch_shapes=[pltpu.VMEM(shape, BF16), pltpu.SemaphoreType.DMA((max(shape) // size,))],
        compiler_params=params(20),
        cost_estimate=cost(2 * rows * shape[0] * shape[1], 2 * shape[0] * shape[1]),
        name="outer",
    )(a, b, after)


def around(near, along):
    first = send(near, along["first"])
    held = [near, first, send(near, along["second"]), send(first, along["second"])]
    return held + [send(b, along["core"]) for b in held]


def total_of(own, *parts):
    total = own.astype(F32)
    for part in parts:
        total = total + part.astype(F32)
    return total.astype(BF16)


def fold(partial, pairs):
    half = partial.shape[0] // 2
    return total_of(partial[:half], send(partial[half:], pairs))


def return_rows(partial, along):
    size = partial.shape[0] // (len(along["z"]) + 1)
    parts = [send(partial[(i + 1) * size : (i + 2) * size], p) for i, p in enumerate(along["z"])]
    return total_of(partial[:size], *parts)


def on_device(along, tokens, grad_out, gates, expert_ids, gate_weight, up_weight, down_weight):
    count, depth = tokens.shape
    n_exp = lax.axis_size("exp")
    mine = lax.axis_index("exp")
    wide = -(-n_exp // LANES) * LANES
    part = depth // SPLIT
    own = pack(tokens, grad_out, gates, expert_ids, wide=wide)
    z1, z2, z3 = along["z"]
    near = pair(own, send(own, z1), count, part)
    height = near.shape[0]
    near = around(near, along)
    far = pair(send(own, z2), send(own, z3), count, part)
    far = around(far, along)
    mine = mine.reshape(1).astype(jnp.int32)
    x, dy, wt, gg, gu, score, low = hidden(mine, near, far, height, gate_weight, up_weight, down_weight, wide)
    middle = depth // 2
    high = inward(gg, gu, score, gate_weight, up_weight, middle)
    low = fold(low, along["core"])
    high = fold(high, along["core"])
    d_gate = outer(x, gg, low)
    low = fold(low, along["second"])
    d_up = outer(x, gu, low)
    high = fold(high, along["second"])
    low = fold(low, along["first"])
    d_down = outer(wt, dy, low)
    high = fold(high, along["first"])
    got_low = return_rows(low, along)
    got_high = return_rows(high, along)
    input_grad = jnp.concatenate([got_low, got_high[:, : depth - middle]], axis=1)
    lane = jnp.arange(wide, dtype=jnp.int32)
    by_pair = jnp.where(expert_ids[:, :, None] == lane, got_high[:, None, depth - middle :].astype(F32), 0.0)
    return input_grad, jnp.sum(by_pair, axis=2), d_gate, d_up, d_down


def spread(block, stages):
    for stage in stages:
        block = jnp.concatenate([block] + [send(block, p) for p in stage], axis=0)
    return block


def collect(partial, stages):
    for stage in reversed(stages):
        own = partial.shape[0] // (len(stage) + 1)
        parts = [send(partial[(i + 1) * own : (i + 2) * own], p) for i, p in enumerate(stage)]
        partial = total_of(partial[:own], *parts)
    return partial


def on_device_large(along, tokens, grad_out, gates, expert_ids, gate_weight, up_weight, down_weight):
    stages = [along["z"], [along["y"]], along["x"], [along["core"]]]
    depth = tokens.shape[1]
    n_exp = lax.axis_size("exp")
    wide = -(-n_exp // LANES) * LANES
    named = expert_ids[:, :, None] == jnp.arange(wide, dtype=jnp.int32)
    by_expert = jnp.sum(jnp.where(named, gates.astype(F32)[:, :, None], 0.0), axis=1).astype(BF16)
    rows = spread(jnp.concatenate([tokens, by_expert], axis=1), stages)
    rows_dy = spread(grad_out, stages)
    rows_x, rows_g = rows[:, :depth], rows[:, depth:]
    w_gate, w_up, w_down = gate_weight[0], up_weight[0], down_weight[0]
    at_mine = jnp.arange(wide, dtype=jnp.int32)[None, :] == lax.axis_index("exp")
    scale = jnp.sum(jnp.where(at_mine, rows_g.astype(F32), 0.0), axis=1, keepdims=True)
    gate_pre = dot(rows_x, w_gate, (1, 0))
    up_pre = dot(rows_x, w_up, (1, 0))
    back = dot(rows_dy, w_down, (1, 1))
    sigma = jax.nn.sigmoid(gate_pre)
    silu_val = gate_pre * sigma
    act = silu_val * up_pre
    score = jnp.sum(act * back, axis=1, keepdims=True)
    weighted = (scale * act).astype(BF16)
    dact = scale * back
    grad_gate = (dact * up_pre * sigma * (1.0 + gate_pre * (1.0 - sigma))).astype(BF16)
    grad_up = (dact * silu_val).astype(BF16)
    back_in = dot(grad_gate, w_gate, (1, 1)) + dot(grad_up, w_up, (1, 1))
    scores = jnp.where(at_mine & (scale != 0.0), score, 0.0)
    got = collect(jnp.concatenate([back_in.astype(BF16), scores.astype(BF16)], axis=1), stages)
    d_gate = dot(rows_x, grad_gate, (0, 0)).astype(BF16)
    d_up = dot(rows_x, grad_up, (0, 0)).astype(BF16)
    d_down = dot(weighted, rows_dy, (0, 0)).astype(BF16)
    by_pair = jnp.where(named, got[:, None, depth:].astype(F32), 0.0)
    return got[:, :depth], jnp.sum(by_pair, axis=2), d_gate[None], d_up[None], d_down[None]


def solution(mesh):
    along = flips(mesh)
    small = mesh.shape["et"] == 2
    placed = (
        P(("exp", "et"), None),
        P(("exp", "et"), None),
        P(("exp", "et"), None),
        P(("exp", "et"), None),
        P("exp", None, "et"),
        P("exp", None, "et"),
        P("exp", "et", None),
    )
    return jax.shard_map(
        functools.partial(on_device if small else on_device_large, along),
        mesh=mesh,
        in_specs=placed,
        out_specs=(placed[0], placed[0], placed[4], placed[5], placed[6]),
        check_vma=False,
    )
```

time: 131 us -> 97.5 us (0.74)
  Pallas kernels: 52 us -> 30.4 us
  starting transfers between devices: 36.9 us -> 30.7 us
  waiting for transfers between devices: 34.7 us -> 31.3 us
  local copies, waits for them, and re-layouts: 3.39 us -> 1.99 us
    pallas_call x10 -> x8, Pallas kernels: 52 us -> 30.4 us  [the longest x1 13.8 us: hidden(): pl.pallas_call(functools.partial(hidden_kernel, n, height, size), out_sha...]
    ppermute x32 -> x29, starting transfers between devices: 36.9 us -> 30.7 us  [send(): return lax.ppermute(block, AXES, pairs)]
    ppermute x32 -> x29, waiting for transfers between devices: 34.7 us -> 31.3 us  [send(): return lax.ppermute(block, AXES, pairs)]
    unnamed x14 -> x6, local copies, waits for them, and re-layouts: 3.17 us -> 1.72 us
  transfers between devices with their start and end apart: 32 -> 29, of which waited for: 13 -> 10; matrix products, arithmetic and copies ran while one was open for 1% -> 1% of each run, Pallas kernels for 27% -> 16%
where the time goes in v2:
time: 97.5 us; the launch traced here: 97.3 us
  waiting for transfers between devices  31.3 us (32%)
  starting transfers between devices  30.7 us (31%)
  Pallas kernels  30.4 us (31%)
  other arithmetic  2.08 us (2%)
  local copies, waits for them, and re-layouts  1.99 us (2%)
    ppermute x29, waiting for transfers between devices, send(): return lax.ppermute(block, AXES, pairs)  31.3 us
    ppermute x29, starting transfers between devices, send(): return lax.ppermute(block, AXES, pairs)  30.7 us
    pallas_call x1, Pallas kernels, hidden(): pl.pallas_call(functools.partial(hidden_kernel, n, height, size), out_sha...  13.8 us
    pallas_call x3, Pallas kernels, outer(): pl.pallas_call(functools.partial(outer_kernel, tall, size), out_shape=jax...  10.6 us
    pallas_call x1, Pallas kernels, inward(): pl.pallas_call(functools.partial(inward_kernel, start, size), out_shape=j...  4.8 us
  transfers between devices with their start and end apart: 29, of which 10 were waited for; matrix products, arithmetic and copies ran while one was open for 1% of the time, Pallas kernels for 16%

profile of v2, /device:TPU:0, one launch (start us, length us, event | category | flops | bytes accessed | tf_op | source)
XLA Modules:
  0.0 97.3 jit_solution(6952962077445886843)
XLA Ops:
  0.6 1.1 %pack.1.a = bf16[48,1920]{1,0:T(8,128)(2,1)S(1)} custom-call(bf16[6,7168]{1,0:T(8,128)(2,1)} %x_hbm.1, bf16[6,7168]{1,0:T(8,128)(2,1)} %dy_hbm.1, bf16[6,8]{1,0:T(8,128)(2,1)} %g_hbm.1, s32[6,8]{1,0:T(8,128)} %id_hbm.1), custom_call_target="tpu_custom_call" | custom-call | tf_op jit(solution)/shard_map/pack/pallas_call | solution.py:87
  1.8 3.1 %collective-permute-start = (bf16[48,1920]{1,0:T(8,128)(2,1)S(1)}, bf16[48,1920]{1,0:T(8,128)(2,1)S(1)}, u32[]{:S(2)}, u32[]{:S(2)}) collective-permute-start(bf16[48,1920]{1,0:T(8,128)(2,1)S(1)} %pack.1.a), channel_id=1, source_target_pairs={{0,8},{1,9},{2,10},{3,11},{4,12},{5,13},{6,14},{7,15},{8,0},{9,1},... | collective-permute-start | bytes 552968 | tf_op jit(solution)/shard_map/ppermute | solution.py:52
  4.8 2.6 %collective-permute-start.8 = (bf16[48,1920]{1,0:T(8,128)(2,1)S(1)}, bf16[48,1920]{1,0:T(8,128)(2,1)S(1)}, u32[]{:S(2)}, u32[]{:S(2)}) collective-permute-start(bf16[48,1920]{1,0:T(8,128)(2,1)S(1)} %pack.1.a), channel_id=1, source_target_pairs={{0,16},{1,17},{2,18},{3,19},{4,20},{5,21},{6,22},{7,23},{8,24},{9,... | collective-permute-start | bytes 552968 | tf_op jit(solution)/shard_map/ppermute | solution.py:52
  7.4 5.1 %collective-permute-done.b = bf16[48,1920]{1,0:T(8,128)(2,1)S(1)} collective-permute-done((bf16[48,1920]{1,0:T(8,128)(2,1)S(1)}, bf16[48,1920]{1,0:T(8,128)(2,1)S(1)}, u32[]{:S(2)}, u32[]{:S(2)}) %collective-permute-start) | collective-permute-done | bytes 184352 | tf_op jit(solution)/shard_map/ppermute | solution.py:52
  12.5 0.1 pair.2.refs_0_
  12.6 1.8 %collective-permute-start.1 = (bf16[48,3712]{1,0:T(8,128)(2,1)S(1)}, bf16[48,3712]{1,0:T(8,128)(2,1)S(1)}, u32[]{:S(2)}, u32[]{:S(2)}) collective-permute-start(bf16[48,3712]{1,0:T(8,128)(2,1)S(1)} %pair.2.refs_0_), channel_id=1, source_target_pairs={{0,4},{1,5},{2,3},{3,2},{4,0},{5,1},{6,7},{7,6},{8,12},{9,13},{10,... | collective-permute-start | bytes 1069064 | tf_op jit(solution)/shard_map/ppermute | solution.py:52
  14.4 1.5 %collective-permute-start.2 = (bf16[48,3712]{1,0:T(8,128)(2,1)S(1)}, bf16[48,3712]{1,0:T(8,128)(2,1)S(1)}, u32[]{:S(2)}, u32[]{:S(2)}) collective-permute-start(bf16[48,3712]{1,0:T(8,128)(2,1)S(1)} %pair.2.refs_0_), channel_id=1, source_target_pairs={{0,1},{1,0},{2,6},{3,7},{4,5},{5,4},{6,2},{7,3},{8,9},{9,8},{10,14... | collective-permute-start | bytes 1069064 | tf_op jit(solution)/shard_map/ppermute | solution.py:52
  15.9 5.3 %collective-permute-done.8.a = bf16[48,1920]{1,0:T(8,128)(2,1)S(1)} collective-permute-done((bf16[48,1920]{1,0:T(8,128)(2,1)S(1)}, bf16[48,1920]{1,0:T(8,128)(2,1)S(1)}, u32[]{:S(2)}, u32[]{:S(2)}) %collective-permute-start.8) | collective-permute-done | bytes 184352 | tf_op jit(solution)/shard_map/ppermute | solution.py:52
  21.3 1.6 %collective-permute-start.10 = (bf16[48,3712]{1,0:T(8,128)(2,1)S(1)}, bf16[48,3712]{1,0:T(8,128)(2,1)S(1)}, u32[]{:S(2)}, u32[]{:S(2)}) collective-permute-start(bf16[48,3712]{1,0:T(8,128)(2,1)S(1)} %pair.3.refs_8_), channel_id=1, source_target_pairs={{0,4},{1,5},{2,3},{3,2},{4,0},{5,1},{6,7},{7,6},{8,12},{9,13},{10,... | collective-permute-start | bytes 1069064 | tf_op jit(solution)/shard_map/ppermute | solution.py:52
  22.9 1.5 %collective-permute-start.11 = (bf16[48,3712]{1,0:T(8,128)(2,1)S(1)}, bf16[48,3712]{1,0:T(8,128)(2,1)S(1)}, u32[]{:S(2)}, u32[]{:S(2)}) collective-permute-start(bf16[48,3712]{1,0:T(8,128)(2,1)S(1)} %pair.3.refs_8_), channel_id=1, source_target_pairs={{0,1},{1,0},{2,6},{3,7},{4,5},{5,4},{6,2},{7,3},{8,9},{9,8},{10,14... | collective-permute-start | bytes 1069064 | tf_op jit(solution)/shard_map/ppermute | solution.py:52
  24.4 0.6 collective-permute-start.3
  25.0 0.1 collective-permute-start.5
  25.1 7.5 %collective-permute-done.10.refs_9_ = bf16[48,3712]{1,0:T(8,128)(2,1)S(1)} collective-permute-done((bf16[48,3712]{1,0:T(8,128)(2,1)S(1)}, bf16[48,3712]{1,0:T(8,128)(2,1)S(1)}, u32[]{:S(2)}, u32[]{:S(2)}) %collective-permute-start.10) | collective-permute-done | bytes 356384 | tf_op jit(solution)/shard_map/ppermute | solution.py:52
  32.6 1.5 %collective-permute-start.12 = (bf16[48,3712]{1,0:T(8,128)(2,1)S(1)}, bf16[48,3712]{1,0:T(8,128)(2,1)}, u32[]{:S(2)}, u32[]{:S(2)}) collective-permute-start(bf16[48,3712]{1,0:T(8,128)(2,1)S(1)} %collective-permute-done.10.refs_9_), channel_id=1, source_target_pairs={{0,1},{1,0},{2,6},{3,7},{4,5},{5,4},{6,2},{7,3},{8,9},{9,8},{10,14... | collective-permute-start | bytes 1069064 | tf_op jit(solution)/shard_map/ppermute | solution.py:52
  34.1 0.5 collective-permute-start.6
  34.7 0.7 copy-done
  35.4 0.4 collective-permute-start.7
  35.9 4.2 %collective-permute-done.12.refs_11_ = bf16[48,3712]{1,0:T(8,128)(2,1)} collective-permute-done((bf16[48,3712]{1,0:T(8,128)(2,1)S(1)}, bf16[48,3712]{1,0:T(8,128)(2,1)}, u32[]{:S(2)}, u32[]{:S(2)}) %collective-permute-start.12) | collective-permute-done | bytes 356384 | tf_op jit(solution)/shard_map/ppermute | solution.py:52
  40.1 2.0 %collective-permute-done.16.refs_15_ = bf16[48,3712]{1,0:T(8,128)(2,1)} collective-permute-done((bf16[48,3712]{1,0:T(8,128)(2,1)}, bf16[48,3712]{1,0:T(8,128)(2,1)}, u32[]{:S(2)}, u32[]{:S(2)}) %collective-permute-start.16) | collective-permute-done | bytes 356384 | tf_op jit(solution)/shard_map/ppermute | solution.py:52
  42.1 1.0 %copy-done.1 = bf16[48,3712]{1,0:T(8,128)(2,1)S(1)} copy-done((bf16[48,3712]{1,0:T(8,128)(2,1)S(1)}, bf16[48,3712]{1,0:T(8,128)(2,1)}, u32[]{:S(2)}) %copy-start.1) | copy-done | bytes 356376
  43.1 13.8 %hidden.1 = (bf16[192,7168]{1,0:T(8,128)(2,1)S(1)}, bf16[192,7168]{1,0:T(8,128)(2,1)S(1)}, bf16[192,512]{1,0:T(8,128)(2,1)S(1)}, bf16[192,512]{1,0:T(8,128)(2,1)...) custom-call(s32[1]{0:T(128)} %bitcast.mine_ref, ...), custom_call_target="tpu_custom_call" | custom-call | flops 5637144576 | bytes 22020096 | tf_op jit(solution)/shard_map/hidden/pallas_call | solution.py:196
  57.0 0.2 collective-permute-start.17
  57.2 4.8 %inward.1 = bf16[192,3712]{1,0:T(8,128)(2,1)S(1)} custom-call(bf16[192,512]{1,0:T(8,128)(2,1)S(1)} %get-tuple-element.13.gg.b, bf16[192,512]{1,0:T(8,128)(2,1)S(1)} %get-tuple-element.14.gu.b, bf16[192,128]{1,0:T(8,128)(2,1)S(1)} %get-tuple-element.15.score, bf16[1,7168,512]{2,1,0:T(8,128)(2,1)} %wg_hbm.1, bf16[1,7168,512]{2,1,0:T(8,128)(2,1)} %wu_hbm.1), custom_call_target="tpu_custom_call" | custom-call | flops 1409286144 | bytes 7340032 | tf_op jit(solution)/shard_map/inward/pallas_call | solution.py:245
  62.0 0.4 collective-permute-start.23
  62.5 0.2 add_convert_fusion.1.after
  62.7 1.6 %collective-permute-start.18 = (bf16[48,3584]{1,0:T(8,128)(2,1)S(1)}, bf16[48,3584]{1,0:T(8,128)(2,1)S(1)}, u32[]{:S(2)}, u32[]{:S(2)}) collective-permute-start(bf16[48,3584]{1,0:T(8,128)(2,1)S(1)} %slice.89), channel_id=1, source_target_pairs={{0,1},{1,0},{2,6},{3,7},{4,5},{5,4},{6,2},{7,3},{8,9},{9,8},{10,14... | collective-permute-start | bytes 1032200 | tf_op jit(solution)/shard_map/ppermute | solution.py:52
  64.2 3.5 %outer.3 = bf16[1,7168,512]{2,1,0:T(8,128)(2,1)} custom-call(bf16[192,7168]{1,0:T(8,128)(2,1)S(1)} %get-tuple-element.16.a, bf16[192,512]{1,0:T(8,128)(2,1)S(1)} %get-tuple-element.13.gg.b, bf16[96,3584]{1,0:T(8,128)(2,1)S(1)} %add_convert_fusion.1.after), custom_call_target="tpu_custom_call" | custom-call | flops 1409286144 | bytes 7340032 | tf_op jit(solution)/shard_map/outer/pallas_call | solution.py:275
  67.8 0.2 add_convert_fusion
  68.0 0.6 collective-permute-start.24
  68.6 1.4 %collective-permute-done.18 = bf16[48,3584]{1,0:T(8,128)(2,1)S(1)} collective-permute-done((bf16[48,3584]{1,0:T(8,128)(2,1)S(1)}, bf16[48,3584]{1,0:T(8,128)(2,1)S(1)}, u32[]{:S(2)}, u32[]{:S(2)}) %collective-permute-start.18) | collective-permute-done | bytes 344096 | tf_op jit(solution)/shard_map/ppermute | solution.py:52
  70.0 0.1 add_convert_fusion.3.after
  70.1 1.6 %collective-permute-start.19 = (bf16[24,3584]{1,0:T(8,128)(2,1)S(1)}, bf16[24,3584]{1,0:T(8,128)(2,1)S(1)}, u32[]{:S(2)}, u32[]{:S(2)}) collective-permute-start(bf16[24,3584]{1,0:T(8,128)(2,1)S(1)} %slice.91), channel_id=1, source_target_pairs={{0,4},{1,5},{2,3},{3,2},{4,0},{5,1},{6,7},{7,6},{8,12},{9,13},{10,... | collective-permute-start | bytes 516104 | tf_op jit(solution)/shard_map/ppermute | solution.py:52
  71.7 3.5 %outer.4 = bf16[1,7168,512]{2,1,0:T(8,128)(2,1)} custom-call(bf16[192,7168]{1,0:T(8,128)(2,1)S(1)} %get-tuple-element.16.a, bf16[192,512]{1,0:T(8,128)(2,1)S(1)} %get-tuple-element.14.gu.b, bf16[48,3584]{1,0:T(8,128)(2,1)S(1)} %add_convert_fusion.3.after), custom_call_target="tpu_custom_call" | custom-call | flops 1409286144 | bytes 7340032 | tf_op jit(solution)/shard_map/outer/pallas_call | solution.py:275
  75.2 2.1 %collective-permute-done.24 = bf16[48,3712]{1,0:T(8,128)(2,1)S(1)} collective-permute-done((bf16[48,3712]{1,0:T(8,128)(2,1)S(1)}, bf16[48,3712]{1,0:T(8,128)(2,1)S(1)}, u32[]{:S(2)}, u32[]{:S(2)}) %collective-permute-start.24) | collective-permute-done | bytes 356384 | tf_op jit(solution)/shard_map/ppermute | solution.py:52
  77.3 0.1 add_convert_fusion.2
  77.4 1.8 %collective-permute-start.25 = (bf16[24,3712]{1,0:T(8,128)(2,1)S(1)}, bf16[24,3712]{1,0:T(8,128)(2,1)S(1)}, u32[]{:S(2)}, u32[]{:S(2)}) collective-permute-start(bf16[24,3712]{1,0:T(8,128)(2,1)S(1)} %slice.101), channel_id=1, source_target_pairs={{0,4},{1,5},{2,3},{3,2},{4,0},{5,1},{6,7},{7,6},{8,12},{9,13},{10,... | collective-permute-start | bytes 534536 | tf_op jit(solution)/shard_map/ppermute | solution.py:52
  79.3 2.5 %collective-permute-start.22 = (bf16[6,3584]{1,0:T(8,128)(2,1)S(1)}, bf16[6,3584]{1,0:T(8,128)(2,1)S(1)}, u32[]{:S(2)}, u32[]{:S(2)}) collective-permute-start(bf16[6,3584]{1,0:T(8,128)(2,1)S(1)} %get-tuple-element.23), channel_id=1, source_target_pairs={{0,24},{1,25},{2,26},{3,27},{4,28},{5,29},{6,30},{7,31},{8,16},{9,... | collective-permute-start | bytes 129032 | tf_op jit(solution)/shard_map/ppermute | solution.py:52
  81.9 2.1 %collective-permute-start.21 = (bf16[6,3584]{1,0:T(8,128)(2,1)S(1)}, bf16[6,3584]{1,0:T(8,128)(2,1)S(1)}, u32[]{:S(2)}, u32[]{:S(2)}) collective-permute-start(bf16[6,3584]{1,0:T(8,128)(2,1)S(1)} %get-tuple-element.24), channel_id=1, source_target_pairs={{0,16},{1,17},{2,18},{3,19},{4,20},{5,21},{6,22},{7,23},{8,24},{9,... | collective-permute-start | bytes 129032 | tf_op jit(solution)/shard_map/ppermute | solution.py:52
  83.9 0.1 collective-permute-start.20
  84.0 3.5 %outer.5 = bf16[1,512,7168]{2,1,0:T(8,128)(2,1)} custom-call(bf16[192,512]{1,0:T(8,128)(2,1)S(1)} %get-tuple-element.17.a, bf16[192,7168]{1,0:T(8,128)(2,1)S(1)} %get-tuple-element.18.b, bf16[24,3584]{1,0:T(8,128)(2,1)S(1)} %add_convert_fusion.5.after), custom_call_target="tpu_custom_call" | custom-call | flops 1409286144 | bytes 7340032 | tf_op jit(solution)/shard_map/outer/pallas_call | solution.py:275
  87.7 2.4 %collective-permute-start.28 = (bf16[6,3712]{1,0:T(8,128)(2,1)S(1)}, bf16[6,3712]{1,0:T(8,128)(2,1)S(1)}, u32[]{:S(2)}, u32[]{:S(2)}) collective-permute-start(bf16[6,3712]{1,0:T(8,128)(2,1)S(1)} %get-tuple-element.20), channel_id=1, source_target_pairs={{0,24},{1,25},{2,26},{3,27},{4,28},{5,29},{6,30},{7,31},{8,16},{9,... | collective-permute-start | bytes 133640 | tf_op jit(solution)/shard_map/ppermute | solution.py:52
  90.1 1.0 %collective-permute-start.27 = (bf16[6,3712]{1,0:T(8,128)(2,1)S(1)}, bf16[6,3712]{1,0:T(8,128)(2,1)S(1)}, u32[]{:S(2)}, u32[]{:S(2)}) collective-permute-start(bf16[6,3712]{1,0:T(8,128)(2,1)S(1)} %get-tuple-element.21), channel_id=1, source_target_pairs={{0,16},{1,17},{2,18},{3,19},{4,20},{5,21},{6,22},{7,23},{8,24},{9,... | collective-permute-start | bytes 133640 | tf_op jit(solution)/shard_map/ppermute | solution.py:52
  91.1 1.0 %collective-permute-start.26 = (bf16[6,3712]{1,0:T(8,128)(2,1)S(1)}, bf16[6,3712]{1,0:T(8,128)(2,1)S(1)}, u32[]{:S(2)}, u32[]{:S(2)}) collective-permute-start(bf16[6,3712]{1,0:T(8,128)(2,1)S(1)} %get-tuple-element.19), channel_id=1, source_target_pairs={{0,8},{1,9},{2,10},{3,11},{4,12},{5,13},{6,14},{7,15},{8,0},{9,1},... | collective-permute-start | bytes 133640 | tf_op jit(solution)/shard_map/ppermute | solution.py:52
  92.2 1.7 %collective-permute-done.28 = bf16[6,3712]{1,0:T(8,128)(2,1)S(1)} collective-permute-done((bf16[6,3712]{1,0:T(8,128)(2,1)S(1)}, bf16[6,3712]{1,0:T(8,128)(2,1)S(1)}, u32[]{:S(2)}, u32[]{:S(2)}) %collective-permute-start.28) | collective-permute-done | bytes 44576 | tf_op jit(solution)/shard_map/ppermute | solution.py:52
  93.9 1.4 %collective-permute-done.27 = bf16[6,3712]{1,0:T(8,128)(2,1)S(1)} collective-permute-done((bf16[6,3712]{1,0:T(8,128)(2,1)S(1)}, bf16[6,3712]{1,0:T(8,128)(2,1)S(1)}, u32[]{:S(2)}, u32[]{:S(2)}) %collective-permute-start.27) | collective-permute-done | bytes 44576 | tf_op jit(solution)/shard_map/ppermute | solution.py:52
  95.3 0.6 collective-permute-done.26
  95.9 0.7 select_reduce_fusion
  96.7 0.7 pad_maximum_fusion
  (44 shorter events, 0.7 us)
Async XLA Ops:
  1.8 10.8 %collective-permute-start = (bf16[48,1920]{1,0:T(8,128)(2,1)S(1)}, bf16[48,1920]{1,0:T(8,128)(2,1)S(1)}, u32[]{:S(2)}, u32[]{:S(2)}) collective-permute-start(bf16[48,1920]{1,0:T(8,128)(2,1)S(1)} %pack.1.a), channel_id=1, source_target_pairs={{0,8},{1,9},{2,10},{3,11},{4,12},{5,13},{6,14},{7,15},{8,0},{9,1},... | collective-permute-start | bytes 552968 | tf_op jit(solution)/shard_map/ppermute | solution.py:52
  4.8 16.4 %collective-permute-start.8 = (bf16[48,1920]{1,0:T(8,128)(2,1)S(1)}, bf16[48,1920]{1,0:T(8,128)(2,1)S(1)}, u32[]{:S(2)}, u32[]{:S(2)}) collective-permute-start(bf16[48,1920]{1,0:T(8,128)(2,1)S(1)} %pack.1.a), channel_id=1, source_target_pairs={{0,16},{1,17},{2,18},{3,19},{4,20},{5,21},{6,22},{7,23},{8,24},{9,... | collective-permute-start | bytes 552968 | tf_op jit(solution)/shard_map/ppermute | solution.py:52
  7.4 13.8 %collective-permute-start.9 = (bf16[48,1920]{1,0:T(8,128)(2,1)S(1)}, bf16[48,1920]{1,0:T(8,128)(2,1)S(1)}, u32[]{:S(2)}, u32[]{:S(2)}) collective-permute-start(bf16[48,1920]{1,0:T(8,128)(2,1)S(1)} %pack.1.a), channel_id=1, source_target_pairs={{0,24},{1,25},{2,26},{3,27},{4,28},{5,29},{6,30},{7,31},{8,16},{9,... | collective-permute-start | bytes 552968 | tf_op jit(solution)/shard_map/ppermute | solution.py:52
  12.6 11.8 %collective-permute-start.1 = (bf16[48,3712]{1,0:T(8,128)(2,1)S(1)}, bf16[48,3712]{1,0:T(8,128)(2,1)S(1)}, u32[]{:S(2)}, u32[]{:S(2)}) collective-permute-start(bf16[48,3712]{1,0:T(8,128)(2,1)S(1)} %pair.2.refs_0_), channel_id=1, source_target_pairs={{0,4},{1,5},{2,3},{3,2},{4,0},{5,1},{6,7},{7,6},{8,12},{9,13},{10,... | collective-permute-start | bytes 1069064 | tf_op jit(solution)/shard_map/ppermute | solution.py:52
  14.4 10.0 %collective-permute-start.2 = (bf16[48,3712]{1,0:T(8,128)(2,1)S(1)}, bf16[48,3712]{1,0:T(8,128)(2,1)S(1)}, u32[]{:S(2)}, u32[]{:S(2)}) collective-permute-start(bf16[48,3712]{1,0:T(8,128)(2,1)S(1)} %pair.2.refs_0_), channel_id=1, source_target_pairs={{0,1},{1,0},{2,6},{3,7},{4,5},{5,4},{6,2},{7,3},{8,9},{9,8},{10,14... | collective-permute-start | bytes 1069064 | tf_op jit(solution)/shard_map/ppermute | solution.py:52
  15.9 9.1 %collective-permute-start.4 = (bf16[48,3712]{1,0:T(8,128)(2,1)S(1)}, bf16[48,3712]{1,0:T(8,128)(2,1)S(1)}, u32[]{:S(2)}, u32[]{:S(2)}) collective-permute-start(bf16[48,3712]{1,0:T(8,128)(2,1)S(1)} %pair.2.refs_0_), channel_id=1, source_target_pairs={{0,2},{1,3},{2,0},{3,1},{4,6},{5,7},{6,4},{7,5},{8,10},{9,11},{10,... | collective-permute-start | bytes 1069064 | tf_op jit(solution)/shard_map/ppermute | solution.py:52
  21.3 11.3 %collective-permute-start.10 = (bf16[48,3712]{1,0:T(8,128)(2,1)S(1)}, bf16[48,3712]{1,0:T(8,128)(2,1)S(1)}, u32[]{:S(2)}, u32[]{:S(2)}) collective-permute-start(bf16[48,3712]{1,0:T(8,128)(2,1)S(1)} %pair.3.refs_8_), channel_id=1, source_target_pairs={{0,4},{1,5},{2,3},{3,2},{4,0},{5,1},{6,7},{7,6},{8,12},{9,13},{10,... | collective-permute-start | bytes 1069064 | tf_op jit(solution)/shard_map/ppermute | solution.py:52
  22.9 11.2 %collective-permute-start.11 = (bf16[48,3712]{1,0:T(8,128)(2,1)S(1)}, bf16[48,3712]{1,0:T(8,128)(2,1)S(1)}, u32[]{:S(2)}, u32[]{:S(2)}) collective-permute-start(bf16[48,3712]{1,0:T(8,128)(2,1)S(1)} %pair.3.refs_8_), channel_id=1, source_target_pairs={{0,1},{1,0},{2,6},{3,7},{4,5},{5,4},{6,2},{7,3},{8,9},{9,8},{10,14... | collective-permute-start | bytes 1069064 | tf_op jit(solution)/shard_map/ppermute | solution.py:52
  24.4 9.7 %collective-permute-start.13 = (bf16[48,3712]{1,0:T(8,128)(2,1)S(1)}, bf16[48,3712]{1,0:T(8,128)(2,1)S(1)}, u32[]{:S(2)}, u32[]{:S(2)}) collective-permute-start(bf16[48,3712]{1,0:T(8,128)(2,1)S(1)} %pair.3.refs_8_), channel_id=1, source_target_pairs={{0,2},{1,3},{2,0},{3,1},{4,6},{5,7},{6,4},{7,5},{8,10},{9,11},{10,... | collective-permute-start | bytes 1069064 | tf_op jit(solution)/shard_map/ppermute | solution.py:52
  24.4 10.3 %collective-permute-start.3 = (bf16[48,3712]{1,0:T(8,128)(2,1)S(1)}, bf16[48,3712]{1,0:T(8,128)(2,1)S(1)}, u32[]{:S(2)}, u32[]{:S(2)}) collective-permute-start(bf16[48,3712]{1,0:T(8,128)(2,1)S(1)} %collective-permute-done.1.refs_1_), channel_id=1, source_target_pairs={{0,1},{1,0},{2,6},{3,7},{4,5},{5,4},{6,2},{7,3},{8,9},{9,8},{10,14... | collective-permute-start | bytes 1069064 | tf_op jit(solution)/shard_map/ppermute | solution.py:52
  25.0 9.7 %collective-permute-start.5 = (bf16[48,3712]{1,0:T(8,128)(2,1)S(1)}, bf16[48,3712]{1,0:T(8,128)(2,1)S(1)}, u32[]{:S(2)}, u32[]{:S(2)}) collective-permute-start(bf16[48,3712]{1,0:T(8,128)(2,1)S(1)} %collective-permute-done.1.refs_1_), channel_id=1, source_target_pairs={{0,2},{1,3},{2,0},{3,1},{4,6},{5,7},{6,4},{7,5},{8,10},{9,11},{10,... | collective-permute-start | bytes 1069064 | tf_op jit(solution)/shard_map/ppermute | solution.py:52
  32.6 7.5 %collective-permute-start.12 = (bf16[48,3712]{1,0:T(8,128)(2,1)S(1)}, bf16[48,3712]{1,0:T(8,128)(2,1)}, u32[]{:S(2)}, u32[]{:S(2)}) collective-permute-start(bf16[48,3712]{1,0:T(8,128)(2,1)S(1)} %collective-permute-done.10.refs_9_), channel_id=1, source_target_pairs={{0,1},{1,0},{2,6},{3,7},{4,5},{5,4},{6,2},{7,3},{8,9},{9,8},{10,14... | collective-permute-start | bytes 1069064 | tf_op jit(solution)/shard_map/ppermute | solution.py:52
  34.1 6.0 %collective-permute-start.14 = (bf16[48,3712]{1,0:T(8,128)(2,1)S(1)}, bf16[48,3712]{1,0:T(8,128)(2,1)}, u32[]{:S(2)}, u32[]{:S(2)}) collective-permute-start(bf16[48,3712]{1,0:T(8,128)(2,1)S(1)} %collective-permute-done.10.refs_9_), channel_id=1, source_target_pairs={{0,2},{1,3},{2,0},{3,1},{4,6},{5,7},{6,4},{7,5},{8,10},{9,11},{10,... | collective-permute-start | bytes 1069064 | tf_op jit(solution)/shard_map/ppermute | solution.py:52
  34.1 6.0 %collective-permute-start.6 = (bf16[48,3712]{1,0:T(8,128)(2,1)S(1)}, bf16[48,3712]{1,0:T(8,128)(2,1)}, u32[]{:S(2)}, u32[]{:S(2)}) collective-permute-start(bf16[48,3712]{1,0:T(8,128)(2,1)S(1)} %collective-permute-done.2.refs_2_), channel_id=1, source_target_pairs={{0,2},{1,3},{2,0},{3,1},{4,6},{5,7},{6,4},{7,5},{8,10},{9,11},{10,... | collective-permute-start | bytes 1069064 | tf_op jit(solution)/shard_map/ppermute | solution.py:52
  34.6 5.5 %collective-permute-start.15 = (bf16[48,3712]{1,0:T(8,128)(2,1)S(1)}, bf16[48,3712]{1,0:T(8,128)(2,1)}, u32[]{:S(2)}, u32[]{:S(2)}) collective-permute-start(bf16[48,3712]{1,0:T(8,128)(2,1)S(1)} %collective-permute-done.11.refs_10_), channel_id=1, source_target_pairs={{0,2},{1,3},{2,0},{3,1},{4,6},{5,7},{6,4},{7,5},{8,10},{9,11},{10,... | collective-permute-start | bytes 1069064 | tf_op jit(solution)/shard_map/ppermute | solution.py:52
  34.7 0.7 copy-start
  35.4 4.7 %collective-permute-start.7 = (bf16[48,3712]{1,0:T(8,128)(2,1)S(1)}, bf16[48,3712]{1,0:T(8,128)(2,1)}, u32[]{:S(2)}, u32[]{:S(2)}) collective-permute-start(bf16[48,3712]{1,0:T(8,128)(2,1)S(1)} %collective-permute-done.3.refs_3_), channel_id=1, source_target_pairs={{0,2},{1,3},{2,0},{3,1},{4,6},{5,7},{6,4},{7,5},{8,10},{9,11},{10,... | collective-permute-start | bytes 1069064 | tf_op jit(solution)/shard_map/ppermute | solution.py:52
  40.1 2.0 %collective-permute-start.16 = (bf16[48,3712]{1,0:T(8,128)(2,1)}, bf16[48,3712]{1,0:T(8,128)(2,1)}, u32[]{:S(2)}, u32[]{:S(2)}) collective-permute-start(bf16[48,3712]{1,0:T(8,128)(2,1)} %collective-permute-done.12.refs_11_), channel_id=1, source_target_pairs={{0,2},{1,3},{2,0},{3,1},{4,6},{5,7},{6,4},{7,5},{8,10},{9,11},{10,... | collective-permute-start | bytes 1069064 | tf_op jit(solution)/shard_map/ppermute | solution.py:52
  42.1 1.0 %copy-start.1 = (bf16[48,3712]{1,0:T(8,128)(2,1)S(1)}, bf16[48,3712]{1,0:T(8,128)(2,1)}, u32[]{:S(2)}) copy-start(bf16[48,3712]{1,0:T(8,128)(2,1)} %copy-done) | copy-start | bytes 1069060
  57.0 5.5 %collective-permute-start.17 = (bf16[96,3584]{1,0:T(8,128)(2,1)S(1)}, bf16[96,3584]{1,0:T(8,128)(2,1)S(1)}, u32[]{:S(2)}, u32[]{:S(2)}) collective-permute-start(bf16[96,3584]{1,0:T(8,128)(2,1)S(1)} %slice.67), channel_id=1, source_target_pairs={{0,2},{1,3},{2,0},{3,1},{4,6},{5,7},{6,4},{7,5},{8,10},{9,11},{10,... | collective-permute-start | bytes 2064392 | tf_op jit(solution)/shard_map/ppermute | solution.py:52
  62.0 5.7 %collective-permute-start.23 = (bf16[96,3712]{1,0:T(8,128)(2,1)S(1)}, bf16[96,3712]{1,0:T(8,128)(2,1)S(1)}, u32[]{:S(2)}, u32[]{:S(2)}) collective-permute-start(bf16[96,3712]{1,0:T(8,128)(2,1)S(1)} %slice.97), channel_id=1, source_target_pairs={{0,2},{1,3},{2,0},{3,1},{4,6},{5,7},{6,4},{7,5},{8,10},{9,11},{10,... | collective-permute-start | bytes 2138120 | tf_op jit(solution)/shard_map/ppermute | solution.py:52
  62.7 7.3 %collective-permute-start.18 = (bf16[48,3584]{1,0:T(8,128)(2,1)S(1)}, bf16[48,3584]{1,0:T(8,128)(2,1)S(1)}, u32[]{:S(2)}, u32[]{:S(2)}) collective-permute-start(bf16[48,3584]{1,0:T(8,128)(2,1)S(1)} %slice.89), channel_id=1, source_target_pairs={{0,1},{1,0},{2,6},{3,7},{4,5},{5,4},{6,2},{7,3},{8,9},{9,8},{10,14... | collective-permute-start | bytes 1032200 | tf_op jit(solution)/shard_map/ppermute | solution.py:52
  68.0 9.3 %collective-permute-start.24 = (bf16[48,3712]{1,0:T(8,128)(2,1)S(1)}, bf16[48,3712]{1,0:T(8,128)(2,1)S(1)}, u32[]{:S(2)}, u32[]{:S(2)}) collective-permute-start(bf16[48,3712]{1,0:T(8,128)(2,1)S(1)} %slice.99), channel_id=1, source_target_pairs={{0,1},{1,0},{2,6},{3,7},{4,5},{5,4},{6,2},{7,3},{8,9},{9,8},{10,14... | collective-permute-start | bytes 1069064 | tf_op jit(solution)/shard_map/ppermute | solution.py:52
  70.1 9.1 %collective-permute-start.19 = (bf16[24,3584]{1,0:T(8,128)(2,1)S(1)}, bf16[24,3584]{1,0:T(8,128)(2,1)S(1)}, u32[]{:S(2)}, u32[]{:S(2)}) collective-permute-start(bf16[24,3584]{1,0:T(8,128)(2,1)S(1)} %slice.91), channel_id=1, source_target_pairs={{0,4},{1,5},{2,3},{3,2},{4,0},{5,1},{6,7},{7,6},{8,12},{9,13},{10,... | collective-permute-start | bytes 516104 | tf_op jit(solution)/shard_map/ppermute | solution.py:52
  77.4 10.2 %collective-permute-start.25 = (bf16[24,3712]{1,0:T(8,128)(2,1)S(1)}, bf16[24,3712]{1,0:T(8,128)(2,1)S(1)}, u32[]{:S(2)}, u32[]{:S(2)}) collective-permute-start(bf16[24,3712]{1,0:T(8,128)(2,1)S(1)} %slice.101), channel_id=1, source_target_pairs={{0,4},{1,5},{2,3},{3,2},{4,0},{5,1},{6,7},{7,6},{8,12},{9,13},{10,... | collective-permute-start | bytes 534536 | tf_op jit(solution)/shard_map/ppermute | solution.py:52
  79.3 11.8 %collective-permute-start.22 = (bf16[6,3584]{1,0:T(8,128)(2,1)S(1)}, bf16[6,3584]{1,0:T(8,128)(2,1)S(1)}, u32[]{:S(2)}, u32[]{:S(2)}) collective-permute-start(bf16[6,3584]{1,0:T(8,128)(2,1)S(1)} %get-tuple-element.23), channel_id=1, source_target_pairs={{0,24},{1,25},{2,26},{3,27},{4,28},{5,29},{6,30},{7,31},{8,16},{9,... | collective-permute-start | bytes 129032 | tf_op jit(solution)/shard_map/ppermute | solution.py:52
  81.9 10.3 %collective-permute-start.21 = (bf16[6,3584]{1,0:T(8,128)(2,1)S(1)}, bf16[6,3584]{1,0:T(8,128)(2,1)S(1)}, u32[]{:S(2)}, u32[]{:S(2)}) collective-permute-start(bf16[6,3584]{1,0:T(8,128)(2,1)S(1)} %get-tuple-element.24), channel_id=1, source_target_pairs={{0,16},{1,17},{2,18},{3,19},{4,20},{5,21},{6,22},{7,23},{8,24},{9,... | collective-permute-start | bytes 129032 | tf_op jit(solution)/shard_map/ppermute | solution.py:52
  83.9 8.2 %collective-permute-start.20 = (bf16[6,3584]{1,0:T(8,128)(2,1)S(1)}, bf16[6,3584]{1,0:T(8,128)(2,1)S(1)}, u32[]{:S(2)}, u32[]{:S(2)}) collective-permute-start(bf16[6,3584]{1,0:T(8,128)(2,1)S(1)} %get-tuple-element.22), channel_id=1, source_target_pairs={{0,8},{1,9},{2,10},{3,11},{4,12},{5,13},{6,14},{7,15},{8,0},{9,1},... | collective-permute-start | bytes 129032 | tf_op jit(solution)/shard_map/ppermute | solution.py:52
  87.6 8.4 %copy-start.2 = (s32[6,8]{1,0:T(8,128)S(1)}, s32[6,8]{1,0:T(8,128)}, u32[]{:S(2)}) copy-start(s32[6,8]{1,0:T(8,128)} %id_hbm.1) | copy-start | bytes 580
  87.7 6.2 %collective-permute-start.28 = (bf16[6,3712]{1,0:T(8,128)(2,1)S(1)}, bf16[6,3712]{1,0:T(8,128)(2,1)S(1)}, u32[]{:S(2)}, u32[]{:S(2)}) collective-permute-start(bf16[6,3712]{1,0:T(8,128)(2,1)S(1)} %get-tuple-element.20), channel_id=1, source_target_pairs={{0,24},{1,25},{2,26},{3,27},{4,28},{5,29},{6,30},{7,31},{8,16},{9,... | collective-permute-start | bytes 133640 | tf_op jit(solution)/shard_map/ppermute | solution.py:52
  90.1 5.2 %collective-permute-start.27 = (bf16[6,3712]{1,0:T(8,128)(2,1)S(1)}, bf16[6,3712]{1,0:T(8,128)(2,1)S(1)}, u32[]{:S(2)}, u32[]{:S(2)}) collective-permute-start(bf16[6,3712]{1,0:T(8,128)(2,1)S(1)} %get-tuple-element.21), channel_id=1, source_target_pairs={{0,16},{1,17},{2,18},{3,19},{4,20},{5,21},{6,22},{7,23},{8,24},{9,... | collective-permute-start | bytes 133640 | tf_op jit(solution)/shard_map/ppermute | solution.py:52
  91.1 4.7 %collective-permute-start.26 = (bf16[6,3712]{1,0:T(8,128)(2,1)S(1)}, bf16[6,3712]{1,0:T(8,128)(2,1)S(1)}, u32[]{:S(2)}, u32[]{:S(2)}) collective-permute-start(bf16[6,3712]{1,0:T(8,128)(2,1)S(1)} %get-tuple-element.19), channel_id=1, source_target_pairs={{0,8},{1,9},{2,10},{3,11},{4,12},{5,13},{6,14},{7,15},{8,0},{9,1},... | collective-permute-start | bytes 133640 | tf_op jit(solution)/shard_map/ppermute | solution.py:52

commit v3 on v2

--- a/solution.py
+++ b/solution.py
@@ -13,7 +13,6 @@
 F32, BF16 = jnp.float32, jnp.bfloat16
 MIB = 1 << 20
 HIDDEN_LIMIT = 36
-INWARD_LIMIT = 52
 VMEM = pl.BlockSpec(memory_space=pltpu.VMEM)
 HBM = pl.BlockSpec(memory_space=pltpu.HBM)
 ANY = pl.BlockSpec(memory_space=pl.ANY)
@@ -124,20 +123,19 @@
     return [(ref, top) for ref in refs for top in range(0, ref.shape[0], height)]
 
 
-def assemble(out, near, far, height, kind):
+def assemble(out, first, refs, height, kind):
     half = out.shape[1] // 2
     rows = height // 4
-    for i, ((a, a_top), (b, b_top)) in enumerate(zip(blocks_of(near, height), blocks_of(far, height), strict=True)):
+    blocks = blocks_of(refs, height)
+    for i in range(0, len(blocks), 2):
         for j in range(2):
             top = (2 * kind + j) * rows
-            low, high = a[a_top + top : a_top + top + rows, :half], b[b_top + top : b_top + top + rows, :half]
-            out[2 * i * rows : 2 * (i + 1) * rows, j * half : (j + 1) * half] = jnp.concatenate([low, high], axis=0)
-
-
-def scales(near, far, height, first, mine):
-    rows = height // 4
-    ends = zip(blocks_of(near, height), blocks_of(far, height), strict=True)
-    gates = [ref[top : top + rows, first:].astype(F32) for pair in ends for ref, top in pair]
+            both = [ref[at + top : at + top + rows, :half] for ref, at in blocks[i : i + 2]]
+            out[first + i * rows : first + (i + 2) * rows, j * half : (j + 1) * half] = jnp.concatenate(both, axis=0)
+
+
+def scales(refs, height, first, mine):
+    gates = [ref[at : at + height // 4, first:].astype(F32) for ref, at in blocks_of(refs, height)]
     gates = jnp.concatenate(gates, axis=0)
     gates = jnp.where(lax.broadcasted_iota(jnp.int32, gates.shape, 1) == mine, gates, 0.0)
     return jnp.sum(gates, axis=1, keepdims=True), (gates != 0.0).astype(F32)
@@ -145,7 +143,7 @@
 
 def hidden_kernel(n, height, size, mine_ref, *refs):
     near, far, refs = refs[:n], refs[n : 2 * n], refs[2 * n :]
-    (wg_hbm, wu_hbm, wd_hbm), (x, dy, wt, gg, gu, score, low), refs = refs[:3], refs[3:10], refs[10:]
+    (wg_hbm, wu_hbm, wd_hbm), (x, dy, wt, gg, gu, near_in, far_in), refs = refs[:3], refs[3:10], refs[10:]
     wg, wu, wd, gate_acc, up_acc, sem = refs
     depth, ff = wg.shape
     parts = depth // size
@@ -159,8 +157,10 @@
     for pair in zip(gates, ups, strict=True):
         for copy in pair:
             copy.start()
-    assemble(dy, near, far, height, 1)
-    assemble(x, near, far, height, 0)
+    middle = x.shape[0] // 2
+    for out, kind in ((dy, 1), (x, 0)):
+        assemble(out, 0, near, height, kind)
+        assemble(out, middle, far, height, kind)
     back = []
     for copy, h in zip(downs, halves, strict=True):
         copy.wait()
@@ -173,18 +173,22 @@
         gate_acc[...] = gate if i == 0 else gate_acc[...] + gate
         up_acc[...] = up if i == 0 else up_acc[...] + up
     gate_pre, up_pre = gate_acc[...], up_acc[...]
-    scale, named = scales(near, far, height, depth // 2, mine_ref[0])
+    scale, named = scales(near + far, height, depth // 2, mine_ref[0])
     sigma = jax.nn.sigmoid(gate_pre)
     silu = gate_pre * sigma
     act = silu * up_pre
     wt[...] = (scale * act).astype(BF16)
-    score[...] = (named * jnp.sum(act * back, axis=1, keepdims=True)).astype(BF16)
+    score = (named * jnp.sum(act * back, axis=1, keepdims=True)).astype(BF16)
     dact = scale * back
     gg[...] = (dact * up_pre * sigma * (1.0 + gate_pre * (1.0 - sigma))).astype(BF16)
     gu[...] = (dact * silu).astype(BF16)
-    for first in range(0, low.shape[1], 512):
+    near_in[:, depth:] = score[:middle]
+    far_in[:, depth:] = score[middle:]
+    for first in range(0, depth, 512):
         c = pl.ds(first, 512)
-        low[:, c] = (dot(gg[...], wg[c, :], (1, 1)) + dot(gu[...], wu[c, :], (1, 1))).astype(BF16)
+        total = (dot(gg[...], wg[c, :], (1, 1)) + dot(gu[...], wu[c, :], (1, 1))).astype(BF16)
+        near_in[:, c] = total[:middle]
+        far_in[:, c] = total[middle:]
 
 
 def hidden(mine, near, far, height, w_gate, w_up, w_down, wide):
@@ -201,8 +205,8 @@
             half,
             half,
             half,
-            jax.ShapeDtypeStruct((rows, wide), BF16),
-            jax.ShapeDtypeStruct((rows, depth // 2), BF16),
+            jax.ShapeDtypeStruct((rows // 2, depth + wide), BF16),
+            jax.ShapeDtypeStruct((rows // 2, depth + wide), BF16),
         ),
         in_specs=[pl.BlockSpec(memory_space=pltpu.SMEM)] + [VMEM] * (2 * n) + [ANY] * 3,
         out_specs=(VMEM,) * 7,
@@ -220,41 +224,69 @@
     )(mine, *near, *far, w_gate, w_up, w_down)
 
 
-def inward_kernel(start, size, gg, gu, score, wg_hbm, wu_hbm, out, wg, wu, sem):
-    parts = [pl.ds(first, size) for first in range(0, wg.shape[0], size)]
-    copies = []
-    for i, c in enumerate(parts):
-        there = pl.ds(start + i * size, size)
-        pair = (
-            pltpu.make_async_copy(wg_hbm.at[0, there], wg.at[c], sem.at[2 * i]),
-            pltpu.make_async_copy(wu_hbm.at[0, there], wu.at[c], sem.at[2 * i + 1]),
-        )
-        for copy in pair:
-            copy.start()
-        copies.append(pair)
-    out[:, wg.shape[0] :] = score[...]
-    for pair, c in zip(copies, parts, strict=True):
-        for copy in pair:
-            copy.wait()
-        out[:, c] = (dot(gg[...], wg[c, :], (1, 1)) + dot(gu[...], wu[c, :], (1, 1))).astype(BF16)
-
-
-def inward(gg, gu, score, w_gate, w_up, start):
-    rows, ff = gg.shape
-    width, size = w_gate.shape[1] - start, 512
-    return pl.pallas_call(
-        functools.partial(inward_kernel, start, size),
-        out_shape=jax.ShapeDtypeStruct((rows, width + score.shape[1]), BF16),
-        in_specs=[VMEM] * 3 + [ANY] * 2,
+def fold_kernel(own, other, after, out):
+    out[...] = (own[: out.shape[0], :].astype(F32) + other[...].astype(F32)).astype(BF16)
+
+
+def fold_after(partial, pairs, after):
+    half = partial.shape[0] // 2
+    return pl.pallas_call(
+        fold_kernel,
+        out_shape=jax.ShapeDtypeStruct((half, partial.shape[1]), BF16),
+        in_specs=[VMEM, VMEM, ANY],
         out_specs=VMEM,
-        scratch_shapes=[pltpu.VMEM((width, ff), BF16)] * 2 + [pltpu.SemaphoreType.DMA((2 * (width // size),))],
-        compiler_params=params(INWARD_LIMIT),
-        cost_estimate=cost(4 * rows * width * ff, 4 * width * ff),
-        name="inward",
-    )(gg, gu, score, w_gate, w_up)
-
-
-def outer_kernel(tall, size, a, b, after, out, done, sem):
+        compiler_params=params(6),
+        name="fold",
+    )(partial, send(partial[half:], pairs), after)
+
+
+def split_kernel(count, part, own, other, first, second):
+    total = (own[: 2 * count, :].astype(F32) + other[...].astype(F32)).astype(BF16)
+    for d, out in enumerate((first, second)):
+        rows = total[d * count : (d + 1) * count]
+        for j in range(SPLIT):
+            out[j * count : (j + 1) * count, :part] = rows[:, j * part : (j + 1) * part]
+        out[:count, part:] = rows[:, SPLIT * part :]
+        out[count:, part:] = jnp.zeros_like(out[count:, part:])
+
+
+def split(own, other, count, part):
+    wide = own.shape[1] - SPLIT * part
+    shape = jax.ShapeDtypeStruct((SPLIT * count, part + wide), BF16)
+    return pl.pallas_call(
+        functools.partial(split_kernel, count, part),
+        out_shape=(shape, shape),
+        in_specs=[VMEM] * 2,
+        out_specs=(VMEM,) * 2,
+        compiler_params=params(6),
+        name="split",
+    )(own, other)
+
+
+def finish_kernel(part, ids, a, b, c, d, grad, gates):
+    count = ids.shape[0]
+    total = a[...].astype(F32) + b[...].astype(F32) + c[...].astype(F32) + d[...].astype(F32)
+    for j in range(SPLIT):
+        grad[:, j * part : (j + 1) * part] = total[j * count : (j + 1) * count, :part].astype(BF16)
+    score = total[:count, part:]
+    lane = lax.broadcasted_iota(jnp.int32, score.shape, 1)
+    for k in range(ids.shape[1]):
+        gates[:, k : k + 1] = jnp.sum(jnp.where(lane == ids[:, k : k + 1], score, 0.0), axis=1, keepdims=True)
+
+
+def finish(ids, parts, part):
+    count, top = ids.shape
+    return pl.pallas_call(
+        functools.partial(finish_kernel, part),
+        out_shape=(jax.ShapeDtypeStruct((count, SPLIT * part), BF16), jax.ShapeDtypeStruct((count, top), F32)),
+        in_specs=[VMEM] * 5,
+        out_specs=(VMEM,) * 2,
+        compiler_params=params(6),
+        name="finish",
+    )(ids, *parts)
+
+
+def outer_kernel(tall, size, a, b, after, out, ended, done, sem):
     copies = []
     for i in range((a if tall else b).shape[1] // size):
         part = pl.ds(i * size, size)
@@ -263,6 +295,7 @@
         done[here] = dot(left, right, (0, 0)).astype(BF16)
         copies.append(pltpu.make_async_copy(done.at[here], out.at[(0, *here)], sem.at[i]))
         copies[-1].start()
+    ended[...] = jnp.zeros_like(ended)
     for copy in copies:
         copy.wait()
 
@@ -274,9 +307,9 @@
     shape = a.shape[1], b.shape[1]
     return pl.pallas_call(
         functools.partial(outer_kernel, tall, size),
-        out_shape=jax.ShapeDtypeStruct((1, *shape), BF16),
+        out_shape=(jax.ShapeDtypeStruct((1, *shape), BF16), jax.ShapeDtypeStruct((8, LANES), F32)),
         in_specs=[VMEM, VMEM, ANY],
-        out_specs=ANY,
+        out_specs=(ANY, VMEM),
         scratch_shapes=[pltpu.VMEM(shape, BF16), pltpu.SemaphoreType.DMA((max(shape) // size,))],
         compiler_params=params(20),
         cost_estimate=cost(2 * rows * shape[0] * shape[1], 2 * shape[0] * shape[1]),
@@ -300,12 +333,6 @@
 def fold(partial, pairs):
     half = partial.shape[0] // 2
     return total_of(partial[:half], send(partial[half:], pairs))
-
-
-def return_rows(partial, along):
-    size = partial.shape[0] // (len(along["z"]) + 1)
-    parts = [send(partial[(i + 1) * size : (i + 2) * size], p) for i, p in enumerate(along["z"])]
-    return total_of(partial[:size], *parts)
 
 
 def on_device(along, tokens, grad_out, gates, expert_ids, gate_weight, up_weight, down_weight):
@@ -322,24 +349,19 @@
     far = pair(send(own, z2), send(own, z3), count, part)
     far = around(far, along)
     mine = mine.reshape(1).astype(jnp.int32)
-    x, dy, wt, gg, gu, score, low = hidden(mine, near, far, height, gate_weight, up_weight, down_weight, wide)
-    middle = depth // 2
-    high = inward(gg, gu, score, gate_weight, up_weight, middle)
-    low = fold(low, along["core"])
-    high = fold(high, along["core"])
-    d_gate = outer(x, gg, low)
-    low = fold(low, along["second"])
-    d_up = outer(x, gu, low)
-    high = fold(high, along["second"])
-    low = fold(low, along["first"])
-    d_down = outer(wt, dy, low)
-    high = fold(high, along["first"])
-    got_low = return_rows(low, along)
-    got_high = return_rows(high, along)
-    input_grad = jnp.concatenate([got_low, got_high[:, : depth - middle]], axis=1)
-    lane = jnp.arange(wide, dtype=jnp.int32)
-    by_pair = jnp.where(expert_ids[:, :, None] == lane, got_high[:, None, depth - middle :].astype(F32), 0.0)
-    return input_grad, jnp.sum(by_pair, axis=2), d_gate, d_up, d_down
+    x, dy, wt, gg, gu, near, far = hidden(mine, near, far, height, gate_weight, up_weight, down_weight, wide)
+    far = fold(far, along["core"])
+    near = fold(near, along["core"])
+    d_gate, ended = outer(x, gg, near)
+    far = fold_after(far, along["second"], ended)
+    d_up, ended = outer(x, gu, far)
+    near = fold_after(near, along["second"], ended)
+    far_2, far_3 = split(far, send(far[2 * count :], along["first"]), count, part)
+    d_down, _ = outer(wt, dy, far_2)
+    own, near_1 = split(near, send(near[2 * count :], along["first"]), count, part)
+    parts = [own, send(near_1, z1), send(far_2, z2), send(far_3, z3)]
+    input_grad, gate_grad = finish(expert_ids, parts, part)
+    return input_grad, gate_grad, d_gate, d_up, d_down
 
 
 def spread(block, stages):

time: 97.5 us -> 89.2 us (0.915)
  starting transfers between devices: 30.7 us -> 27.2 us
  other arithmetic: 2.08 us -> 0.34 us
  local copies, waits for them, and re-layouts: 1.99 us -> 0.26 us
    ppermute x29 -> x26, starting transfers between devices: 30.7 us -> 27.2 us  [send(): return lax.ppermute(block, AXES, pairs)]
    pallas_call x4 -> x8, Pallas kernels: 15.4 us -> 12.4 us  [the longest x3 11.3 us: outer(): pl.pallas_call(functools.partial(outer_kernel, tall, size), out_shape=(ja...]
    pallas_call x1, Pallas kernels: 13.8 us -> 16.3 us  [hidden(): pl.pallas_call(functools.partial(hidden_kernel, n, height, size), out_sha...]
    unnamed x6 -> x2, local copies, waits for them, and re-layouts: 1.72 us -> 0.01 us
    ppermute x29 -> x26, waiting for transfers between devices: 31.3 us -> 30.4 us  [send(): return lax.ppermute(block, AXES, pairs)]
  transfers between devices with their start and end apart: 29 -> 26, of which waited for: 10 -> 12; matrix products, arithmetic and copies ran while one was open for 1% -> 1% of each run, Pallas kernels for 16% -> 13%
where the time goes in v3:
time: 89.2 us; the launch traced here: 89 us
  waiting for transfers between devices  30.4 us (34%)
  Pallas kernels  30 us (34%)
  starting transfers between devices  27.2 us (30%)
    ppermute x26, waiting for transfers between devices, send(): return lax.ppermute(block, AXES, pairs)  30.4 us
    ppermute x26, starting transfers between devices, send(): return lax.ppermute(block, AXES, pairs)  27.2 us
    pallas_call x1, Pallas kernels, hidden(): pl.pallas_call(functools.partial(hidden_kernel, n, height, size), out_sha...  16.3 us
    pallas_call x3, Pallas kernels, outer(): pl.pallas_call(functools.partial(outer_kernel, tall, size), out_shape=(ja...  11.3 us
  transfers between devices with their start and end apart: 26, of which 12 were waited for; matrix products, arithmetic and copies ran while one was open for 1% of the time, Pallas kernels for 13%

profile of v3, /device:TPU:0, one launch (start us, length us, event | category | flops | bytes accessed | tf_op | source)
XLA Modules:
  0.0 89.0 jit_solution(6707072135652168926)
XLA Ops:
  0.6 1.1 %pack.1.a = bf16[48,1920]{1,0:T(8,128)(2,1)S(1)} custom-call(bf16[6,7168]{1,0:T(8,128)(2,1)} %x_hbm.1, bf16[6,7168]{1,0:T(8,128)(2,1)} %dy_hbm.1, bf16[6,8]{1,0:T(8,128)(2,1)} %g_hbm.1, s32[6,8]{1,0:T(8,128)} %ids.1), custom_call_target="tpu_custom_call" | custom-call | tf_op jit(solution)/shard_map/pack/pallas_call | solution.py:86
  1.8 3.1 %collective-permute-start = (bf16[48,1920]{1,0:T(8,128)(2,1)S(1)}, bf16[48,1920]{1,0:T(8,128)(2,1)S(1)}, u32[]{:S(2)}, u32[]{:S(2)}) collective-permute-start(bf16[48,1920]{1,0:T(8,128)(2,1)S(1)} %pack.1.a), channel_id=1, source_target_pairs={{0,8},{1,9},{2,10},{3,11},{4,12},{5,13},{6,14},{7,15},{8,0},{9,1},... | collective-permute-start | bytes 552968 | tf_op jit(solution)/shard_map/ppermute | solution.py:51
  4.8 2.5 %collective-permute-start.9 = (bf16[48,1920]{1,0:T(8,128)(2,1)S(1)}, bf16[48,1920]{1,0:T(8,128)(2,1)S(1)}, u32[]{:S(2)}, u32[]{:S(2)}) collective-permute-start(bf16[48,1920]{1,0:T(8,128)(2,1)S(1)} %pack.1.a), channel_id=1, source_target_pairs={{0,24},{1,25},{2,26},{3,27},{4,28},{5,29},{6,30},{7,31},{8,16},{9,... | collective-permute-start | bytes 552968 | tf_op jit(solution)/shard_map/ppermute | solution.py:51
  7.3 0.1 collective-permute-start.8
  7.4 2.5 %collective-permute-done.b = bf16[48,1920]{1,0:T(8,128)(2,1)S(1)} collective-permute-done((bf16[48,1920]{1,0:T(8,128)(2,1)S(1)}, bf16[48,1920]{1,0:T(8,128)(2,1)S(1)}, u32[]{:S(2)}, u32[]{:S(2)}) %collective-permute-start) | collective-permute-done | bytes 184352 | tf_op jit(solution)/shard_map/ppermute | solution.py:51
  9.9 0.1 pair.2.refs_0_
  10.0 0.1 collective-permute-start.4
  10.0 1.6 %collective-permute-start.2 = (bf16[48,3712]{1,0:T(8,128)(2,1)S(1)}, bf16[48,3712]{1,0:T(8,128)(2,1)S(1)}, u32[]{:S(2)}, u32[]{:S(2)}) collective-permute-start(bf16[48,3712]{1,0:T(8,128)(2,1)S(1)} %pair.2.refs_0_), channel_id=1, source_target_pairs={{0,1},{1,0},{2,6},{3,7},{4,5},{5,4},{6,2},{7,3},{8,9},{9,8},{10,14... | collective-permute-start | bytes 1069064 | tf_op jit(solution)/shard_map/ppermute | solution.py:51
  11.6 1.5 %collective-permute-start.1 = (bf16[48,3712]{1,0:T(8,128)(2,1)S(1)}, bf16[48,3712]{1,0:T(8,128)(2,1)S(1)}, u32[]{:S(2)}, u32[]{:S(2)}) collective-permute-start(bf16[48,3712]{1,0:T(8,128)(2,1)S(1)} %pair.2.refs_0_), channel_id=1, source_target_pairs={{0,4},{1,5},{2,3},{3,2},{4,0},{5,1},{6,7},{7,6},{8,12},{9,13},{10,... | collective-permute-start | bytes 1069064 | tf_op jit(solution)/shard_map/ppermute | solution.py:51
  13.1 3.7 %collective-permute-done.9.b = bf16[48,1920]{1,0:T(8,128)(2,1)S(1)} collective-permute-done((bf16[48,1920]{1,0:T(8,128)(2,1)S(1)}, bf16[48,1920]{1,0:T(8,128)(2,1)S(1)}, u32[]{:S(2)}, u32[]{:S(2)}) %collective-permute-start.9) | collective-permute-done | bytes 184352 | tf_op jit(solution)/shard_map/ppermute | solution.py:51
  16.9 6.8 %collective-permute-done.8.a = bf16[48,1920]{1,0:T(8,128)(2,1)S(1)} collective-permute-done((bf16[48,1920]{1,0:T(8,128)(2,1)S(1)}, bf16[48,1920]{1,0:T(8,128)(2,1)S(1)}, u32[]{:S(2)}, u32[]{:S(2)}) %collective-permute-start.8) | collective-permute-done | bytes 184352 | tf_op jit(solution)/shard_map/ppermute | solution.py:51
  23.6 0.1 pair.3.refs_8_
  23.7 1.6 %collective-permute-start.10 = (bf16[48,3712]{1,0:T(8,128)(2,1)S(1)}, bf16[48,3712]{1,0:T(8,128)(2,1)S(1)}, u32[]{:S(2)}, u32[]{:S(2)}) collective-permute-start(bf16[48,3712]{1,0:T(8,128)(2,1)S(1)} %pair.3.refs_8_), channel_id=1, source_target_pairs={{0,4},{1,5},{2,3},{3,2},{4,0},{5,1},{6,7},{7,6},{8,12},{9,13},{10,... | collective-permute-start | bytes 1069064 | tf_op jit(solution)/shard_map/ppermute | solution.py:51
  25.3 1.5 %collective-permute-start.11 = (bf16[48,3712]{1,0:T(8,128)(2,1)S(1)}, bf16[48,3712]{1,0:T(8,128)(2,1)S(1)}, u32[]{:S(2)}, u32[]{:S(2)}) collective-permute-start(bf16[48,3712]{1,0:T(8,128)(2,1)S(1)} %pair.3.refs_8_), channel_id=1, source_target_pairs={{0,1},{1,0},{2,6},{3,7},{4,5},{5,4},{6,2},{7,3},{8,9},{9,8},{10,14... | collective-permute-start | bytes 1069064 | tf_op jit(solution)/shard_map/ppermute | solution.py:51
  26.8 0.7 collective-permute-start.3
  27.5 6.4 %collective-permute-done.10.refs_9_ = bf16[48,3712]{1,0:T(8,128)(2,1)S(1)} collective-permute-done((bf16[48,3712]{1,0:T(8,128)(2,1)S(1)}, bf16[48,3712]{1,0:T(8,128)(2,1)S(1)}, u32[]{:S(2)}, u32[]{:S(2)}) %collective-permute-start.10) | collective-permute-done | bytes 356384 | tf_op jit(solution)/shard_map/ppermute | solution.py:51
  34.0 1.5 %collective-permute-start.12 = (bf16[48,3712]{1,0:T(8,128)(2,1)S(1)}, bf16[48,3712]{1,0:T(8,128)(2,1)}, u32[]{:S(2)}, u32[]{:S(2)}) collective-permute-start(bf16[48,3712]{1,0:T(8,128)(2,1)S(1)} %collective-permute-done.10.refs_9_), channel_id=1, source_target_pairs={{0,1},{1,0},{2,6},{3,7},{4,5},{5,4},{6,2},{7,3},{8,9},{9,8},{10,14... | collective-permute-start | bytes 1069064 | tf_op jit(solution)/shard_map/ppermute | solution.py:51
  35.5 0.5 collective-permute-start.14
  36.0 0.1 collective-permute-start.15
  36.1 0.8 collective-permute-done.3.refs_3_
  36.9 2.1 %collective-permute-start.7 = (bf16[48,3712]{1,0:T(8,128)(2,1)}, bf16[48,3712]{1,0:T(8,128)(2,1)}, u32[]{:S(2)}, u32[]{:S(2)}) collective-permute-start(bf16[48,3712]{1,0:T(8,128)(2,1)} %collective-permute-done.3.refs_3_), channel_id=1, source_target_pairs={{0,2},{1,3},{2,0},{3,1},{4,6},{5,7},{6,4},{7,5},{8,10},{9,11},{10,... | collective-permute-start | bytes 1069064 | tf_op jit(solution)/shard_map/ppermute | solution.py:51
  39.0 2.4 %collective-permute-done.12.refs_11_ = bf16[48,3712]{1,0:T(8,128)(2,1)} collective-permute-done((bf16[48,3712]{1,0:T(8,128)(2,1)S(1)}, bf16[48,3712]{1,0:T(8,128)(2,1)}, u32[]{:S(2)}, u32[]{:S(2)}) %collective-permute-start.12) | collective-permute-done | bytes 356384 | tf_op jit(solution)/shard_map/ppermute | solution.py:51
  41.5 1.1 %collective-permute-start.16 = (bf16[48,3712]{1,0:T(8,128)(2,1)}, bf16[48,3712]{1,0:T(8,128)(2,1)}, u32[]{:S(2)}, u32[]{:S(2)}) collective-permute-start(bf16[48,3712]{1,0:T(8,128)(2,1)} %collective-permute-done.12.refs_11_), channel_id=1, source_target_pairs={{0,2},{1,3},{2,0},{3,1},{4,6},{5,7},{6,4},{7,5},{8,10},{9,11},{10,... | collective-permute-start | bytes 1069064 | tf_op jit(solution)/shard_map/ppermute | solution.py:51
  42.6 1.6 %collective-permute-done.16.refs_15_ = bf16[48,3712]{1,0:T(8,128)(2,1)} collective-permute-done((bf16[48,3712]{1,0:T(8,128)(2,1)}, bf16[48,3712]{1,0:T(8,128)(2,1)}, u32[]{:S(2)}, u32[]{:S(2)}) %collective-permute-start.16) | collective-permute-done | bytes 356384 | tf_op jit(solution)/shard_map/ppermute | solution.py:51
  44.2 16.3 %hidden.1 = (bf16[192,7168]{1,0:T(8,128)(2,1)S(1)}, bf16[192,7168]{1,0:T(8,128)(2,1)S(1)}, bf16[192,512]{1,0:T(8,128)(2,1)S(1)}, bf16[192,512]{1,0:T(8,128)(2,1)...) custom-call(s32[1]{0:T(128)} %bitcast.mine_ref, ...), custom_call_target="tpu_custom_call" | custom-call | flops 5637144576 | bytes 22020096 | tf_op jit(solution)/shard_map/hidden/pallas_call | solution.py:200
  60.5 0.4 collective-permute-start.19
  61.0 0.2 collective-permute-start.17
  61.2 1.5 %collective-permute-done.19 = bf16[48,7296]{1,0:T(8,128)(2,1)S(1)} collective-permute-done((bf16[48,7296]{1,0:T(8,128)(2,1)S(1)}, bf16[48,7296]{1,0:T(8,128)(2,1)S(1)}, u32[]{:S(2)}, u32[]{:S(2)}) %collective-permute-start.19) | collective-permute-done | bytes 700448 | tf_op jit(solution)/shard_map/ppermute | solution.py:51
  62.7 0.2 add_convert_fusion.own
  62.9 1.6 %collective-permute-start.20 = (bf16[24,7296]{1,0:T(8,128)(2,1)S(1)}, bf16[24,7296]{1,0:T(8,128)(2,1)S(1)}, u32[]{:S(2)}, u32[]{:S(2)}) collective-permute-start(bf16[24,7296]{1,0:T(8,128)(2,1)S(1)} %slice.33), channel_id=1, source_target_pairs={{0,1},{1,0},{2,6},{3,7},{4,5},{5,4},{6,2},{7,3},{8,9},{9,8},{10,14... | collective-permute-start | bytes 1050632 | tf_op jit(solution)/shard_map/ppermute | solution.py:51
  64.5 0.2 add_convert_fusion.1.after.own
  64.7 0.8 collective-permute-start.18
  65.5 3.7 %outer.3 = (bf16[1,7168,512]{2,1,0:T(8,128)(2,1)}, f32[8,128]{1,0:T(8,128)S(1)}) custom-call(bf16[192,7168]{1,0:T(8,128)(2,1)S(1)} %get-tuple-element.24.a, bf16[192,512]{1,0:T(8,128)(2,1)S(1)} %get-tuple-element.27.b, bf16[48,7296]{1,0:T(8,128)(2,1)S(1)} %add_convert_fusion.1.after.own), custom_call_target="tpu_custom_call" | custom-call | flops 1409286144 | bytes 7340032 | tf_op jit(solution)/shard_map/outer/pallas_call | solution.py:308
  69.2 1.1 %collective-permute-done.20.other = bf16[24,7296]{1,0:T(8,128)(2,1)S(1)} collective-permute-done((bf16[24,7296]{1,0:T(8,128)(2,1)S(1)}, bf16[24,7296]{1,0:T(8,128)(2,1)S(1)}, u32[]{:S(2)}, u32[]{:S(2)}) %collective-permute-start.20) | collective-permute-done | bytes 350240 | tf_op jit(solution)/shard_map/ppermute | solution.py:51
  70.3 0.1 fold.2.after.own
  70.5 1.8 %collective-permute-start.23 = (bf16[12,7296]{1,0:T(8,128)(2,1)S(1)}, bf16[12,7296]{1,0:T(8,128)(2,1)S(1)}, u32[]{:S(2)}, u32[]{:S(2)}) collective-permute-start(bf16[12,7296]{1,0:T(8,128)(2,1)S(1)} %slice.35), channel_id=1, source_target_pairs={{0,4},{1,5},{2,3},{3,2},{4,0},{5,1},{6,7},{7,6},{8,12},{9,13},{10,... | collective-permute-start | bytes 525320 | tf_op jit(solution)/shard_map/ppermute | solution.py:51
  72.3 3.5 %outer.4 = (bf16[1,7168,512]{2,1,0:T(8,128)(2,1)}, f32[8,128]{1,0:T(8,128)S(1)}) custom-call(bf16[192,7168]{1,0:T(8,128)(2,1)S(1)} %get-tuple-element.24.a, bf16[192,512]{1,0:T(8,128)(2,1)S(1)} %get-tuple-element.25.b, bf16[24,7296]{1,0:T(8,128)(2,1)S(1)} %fold.2.after.own), custom_call_target="tpu_custom_call" | custom-call | flops 1409286144 | bytes 7340032 | tf_op jit(solution)/shard_map/outer/pallas_call | solution.py:308
  75.8 0.1 fold.3.own
  76.0 1.6 %collective-permute-start.21 = (bf16[12,7296]{1,0:T(8,128)(2,1)S(1)}, bf16[12,7296]{1,0:T(8,128)(2,1)S(1)}, u32[]{:S(2)}, u32[]{:S(2)}) collective-permute-start(bf16[12,7296]{1,0:T(8,128)(2,1)S(1)} %slice.34), channel_id=1, source_target_pairs={{0,4},{1,5},{2,3},{3,2},{4,0},{5,1},{6,7},{7,6},{8,12},{9,13},{10,... | collective-permute-start | bytes 525320 | tf_op jit(solution)/shard_map/ppermute | solution.py:51
  77.6 0.1 split.3
  77.7 2.7 %collective-permute-start.25 = (bf16[24,1920]{1,0:T(8,128)(2,1)S(1)}, bf16[24,1920]{1,0:T(8,128)(2,1)S(1)}, u32[]{:S(2)}, u32[]{:S(2)}) collective-permute-start(bf16[24,1920]{1,0:T(8,128)(2,1)S(1)} %get-tuple-element.33), channel_id=1, source_target_pairs={{0,24},{1,25},{2,26},{3,27},{4,28},{5,29},{6,30},{7,31},{8,16},{9,... | collective-permute-start | bytes 276488 | tf_op jit(solution)/shard_map/ppermute | solution.py:51
  80.5 1.7 %collective-permute-done.21.other = bf16[12,7296]{1,0:T(8,128)(2,1)S(1)} collective-permute-done((bf16[12,7296]{1,0:T(8,128)(2,1)S(1)}, bf16[12,7296]{1,0:T(8,128)(2,1)S(1)}, u32[]{:S(2)}, u32[]{:S(2)}) %collective-permute-start.21) | collective-permute-done | bytes 175136 | tf_op jit(solution)/shard_map/ppermute | solution.py:51
  82.1 0.1 split.2
  82.2 0.1 collective-permute-start.22
  82.3 4.1 %outer.5 = (bf16[1,512,7168]{2,1,0:T(8,128)(2,1)}, f32[8,128]{1,0:T(8,128)}) custom-call(bf16[192,512]{1,0:T(8,128)(2,1)S(1)} %get-tuple-element.38.a, bf16[192,7168]{1,0:T(8,128)(2,1)S(1)} %get-tuple-element.39.b, bf16[24,1920]{1,0:T(8,128)(2,1)S(1)} %get-tuple-element.32.after), custom_call_target="tpu_custom_call" | custom-call | flops 1409286144 | bytes 7340032 | tf_op jit(solution)/shard_map/outer/pallas_call | solution.py:308
  86.4 1.1 %collective-permute-done.24.c = bf16[24,1920]{1,0:T(8,128)(2,1)S(1)} collective-permute-done((bf16[24,1920]{1,0:T(8,128)(2,1)S(1)}, bf16[24,1920]{1,0:T(8,128)(2,1)S(1)}, u32[]{:S(2)}, u32[]{:S(2)}) %collective-permute-start.24) | collective-permute-done | bytes 92192 | tf_op jit(solution)/shard_map/ppermute | solution.py:51
  87.6 0.6 collective-permute-done.22.b
  88.2 0.8 finish.1
  (26 shorter events, 0.3 us)
Async XLA Ops:
  1.8 8.1 %collective-permute-start = (bf16[48,1920]{1,0:T(8,128)(2,1)S(1)}, bf16[48,1920]{1,0:T(8,128)(2,1)S(1)}, u32[]{:S(2)}, u32[]{:S(2)}) collective-permute-start(bf16[48,1920]{1,0:T(8,128)(2,1)S(1)} %pack.1.a), channel_id=1, source_target_pairs={{0,8},{1,9},{2,10},{3,11},{4,12},{5,13},{6,14},{7,15},{8,0},{9,1},... | collective-permute-start | bytes 552968 | tf_op jit(solution)/shard_map/ppermute | solution.py:51
  4.8 12.0 %collective-permute-start.9 = (bf16[48,1920]{1,0:T(8,128)(2,1)S(1)}, bf16[48,1920]{1,0:T(8,128)(2,1)S(1)}, u32[]{:S(2)}, u32[]{:S(2)}) collective-permute-start(bf16[48,1920]{1,0:T(8,128)(2,1)S(1)} %pack.1.a), channel_id=1, source_target_pairs={{0,24},{1,25},{2,26},{3,27},{4,28},{5,29},{6,30},{7,31},{8,16},{9,... | collective-permute-start | bytes 552968 | tf_op jit(solution)/shard_map/ppermute | solution.py:51
  7.3 16.3 %collective-permute-start.8 = (bf16[48,1920]{1,0:T(8,128)(2,1)S(1)}, bf16[48,1920]{1,0:T(8,128)(2,1)S(1)}, u32[]{:S(2)}, u32[]{:S(2)}) collective-permute-start(bf16[48,1920]{1,0:T(8,128)(2,1)S(1)} %pack.1.a), channel_id=1, source_target_pairs={{0,16},{1,17},{2,18},{3,19},{4,20},{5,21},{6,22},{7,23},{8,24},{9,... | collective-permute-start | bytes 552968 | tf_op jit(solution)/shard_map/ppermute | solution.py:51
  10.0 15.3 %collective-permute-start.4 = (bf16[48,3712]{1,0:T(8,128)(2,1)S(1)}, bf16[48,3712]{1,0:T(8,128)(2,1)S(1)}, u32[]{:S(2)}, u32[]{:S(2)}) collective-permute-start(bf16[48,3712]{1,0:T(8,128)(2,1)S(1)} %pair.2.refs_0_), channel_id=1, source_target_pairs={{0,2},{1,3},{2,0},{3,1},{4,6},{5,7},{6,4},{7,5},{8,10},{9,11},{10,... | collective-permute-start | bytes 1069064 | tf_op jit(solution)/shard_map/ppermute | solution.py:51
  10.0 16.8 %collective-permute-start.2 = (bf16[48,3712]{1,0:T(8,128)(2,1)S(1)}, bf16[48,3712]{1,0:T(8,128)(2,1)S(1)}, u32[]{:S(2)}, u32[]{:S(2)}) collective-permute-start(bf16[48,3712]{1,0:T(8,128)(2,1)S(1)} %pair.2.refs_0_), channel_id=1, source_target_pairs={{0,1},{1,0},{2,6},{3,7},{4,5},{5,4},{6,2},{7,3},{8,9},{9,8},{10,14... | collective-permute-start | bytes 1069064 | tf_op jit(solution)/shard_map/ppermute | solution.py:51
  11.6 15.2 %collective-permute-start.1 = (bf16[48,3712]{1,0:T(8,128)(2,1)S(1)}, bf16[48,3712]{1,0:T(8,128)(2,1)S(1)}, u32[]{:S(2)}, u32[]{:S(2)}) collective-permute-start(bf16[48,3712]{1,0:T(8,128)(2,1)S(1)} %pair.2.refs_0_), channel_id=1, source_target_pairs={{0,4},{1,5},{2,3},{3,2},{4,0},{5,1},{6,7},{7,6},{8,12},{9,13},{10,... | collective-permute-start | bytes 1069064 | tf_op jit(solution)/shard_map/ppermute | solution.py:51
  23.7 10.2 %collective-permute-start.10 = (bf16[48,3712]{1,0:T(8,128)(2,1)S(1)}, bf16[48,3712]{1,0:T(8,128)(2,1)S(1)}, u32[]{:S(2)}, u32[]{:S(2)}) collective-permute-start(bf16[48,3712]{1,0:T(8,128)(2,1)S(1)} %pair.3.refs_8_), channel_id=1, source_target_pairs={{0,4},{1,5},{2,3},{3,2},{4,0},{5,1},{6,7},{7,6},{8,12},{9,13},{10,... | collective-permute-start | bytes 1069064 | tf_op jit(solution)/shard_map/ppermute | solution.py:51
  25.3 10.2 %collective-permute-start.13 = (bf16[48,3712]{1,0:T(8,128)(2,1)S(1)}, bf16[48,3712]{1,0:T(8,128)(2,1)S(1)}, u32[]{:S(2)}, u32[]{:S(2)}) collective-permute-start(bf16[48,3712]{1,0:T(8,128)(2,1)S(1)} %pair.3.refs_8_), channel_id=1, source_target_pairs={{0,2},{1,3},{2,0},{3,1},{4,6},{5,7},{6,4},{7,5},{8,10},{9,11},{10,... | collective-permute-start | bytes 1069064 | tf_op jit(solution)/shard_map/ppermute | solution.py:51
  25.3 10.2 %collective-permute-start.11 = (bf16[48,3712]{1,0:T(8,128)(2,1)S(1)}, bf16[48,3712]{1,0:T(8,128)(2,1)S(1)}, u32[]{:S(2)}, u32[]{:S(2)}) collective-permute-start(bf16[48,3712]{1,0:T(8,128)(2,1)S(1)} %pair.3.refs_8_), channel_id=1, source_target_pairs={{0,1},{1,0},{2,6},{3,7},{4,5},{5,4},{6,2},{7,3},{8,9},{9,8},{10,14... | collective-permute-start | bytes 1069064 | tf_op jit(solution)/shard_map/ppermute | solution.py:51
  26.8 9.2 %collective-permute-start.6 = (bf16[48,3712]{1,0:T(8,128)(2,1)S(1)}, bf16[48,3712]{1,0:T(8,128)(2,1)S(1)}, u32[]{:S(2)}, u32[]{:S(2)}) collective-permute-start(bf16[48,3712]{1,0:T(8,128)(2,1)S(1)} %collective-permute-done.2.refs_2_), channel_id=1, source_target_pairs={{0,2},{1,3},{2,0},{3,1},{4,6},{5,7},{6,4},{7,5},{8,10},{9,11},{10,... | collective-permute-start | bytes 1069064 | tf_op jit(solution)/shard_map/ppermute | solution.py:51
  26.8 10.1 %collective-permute-start.3 = (bf16[48,3712]{1,0:T(8,128)(2,1)S(1)}, bf16[48,3712]{1,0:T(8,128)(2,1)}, u32[]{:S(2)}, u32[]{:S(2)}) collective-permute-start(bf16[48,3712]{1,0:T(8,128)(2,1)S(1)} %collective-permute-done.1.refs_1_), channel_id=1, source_target_pairs={{0,1},{1,0},{2,6},{3,7},{4,5},{5,4},{6,2},{7,3},{8,9},{9,8},{10,14... | collective-permute-start | bytes 1069064 | tf_op jit(solution)/shard_map/ppermute | solution.py:51
  34.0 7.5 %collective-permute-start.12 = (bf16[48,3712]{1,0:T(8,128)(2,1)S(1)}, bf16[48,3712]{1,0:T(8,128)(2,1)}, u32[]{:S(2)}, u32[]{:S(2)}) collective-permute-start(bf16[48,3712]{1,0:T(8,128)(2,1)S(1)} %collective-permute-done.10.refs_9_), channel_id=1, source_target_pairs={{0,1},{1,0},{2,6},{3,7},{4,5},{5,4},{6,2},{7,3},{8,9},{9,8},{10,14... | collective-permute-start | bytes 1069064 | tf_op jit(solution)/shard_map/ppermute | solution.py:51
  35.5 7.1 %collective-permute-start.5 = (bf16[48,3712]{1,0:T(8,128)(2,1)S(1)}, bf16[48,3712]{1,0:T(8,128)(2,1)}, u32[]{:S(2)}, u32[]{:S(2)}) collective-permute-start(bf16[48,3712]{1,0:T(8,128)(2,1)S(1)} %collective-permute-done.1.refs_1_), channel_id=1, source_target_pairs={{0,2},{1,3},{2,0},{3,1},{4,6},{5,7},{6,4},{7,5},{8,10},{9,11},{10,... | collective-permute-start | bytes 1069064 | tf_op jit(solution)/shard_map/ppermute | solution.py:51
  35.5 7.1 %collective-permute-start.14 = (bf16[48,3712]{1,0:T(8,128)(2,1)S(1)}, bf16[48,3712]{1,0:T(8,128)(2,1)}, u32[]{:S(2)}, u32[]{:S(2)}) collective-permute-start(bf16[48,3712]{1,0:T(8,128)(2,1)S(1)} %collective-permute-done.10.refs_9_), channel_id=1, source_target_pairs={{0,2},{1,3},{2,0},{3,1},{4,6},{5,7},{6,4},{7,5},{8,10},{9,11},{10,... | collective-permute-start | bytes 1069064 | tf_op jit(solution)/shard_map/ppermute | solution.py:51
  36.0 6.6 %collective-permute-start.15 = (bf16[48,3712]{1,0:T(8,128)(2,1)S(1)}, bf16[48,3712]{1,0:T(8,128)(2,1)}, u32[]{:S(2)}, u32[]{:S(2)}) collective-permute-start(bf16[48,3712]{1,0:T(8,128)(2,1)S(1)} %collective-permute-done.11.refs_10_), channel_id=1, source_target_pairs={{0,2},{1,3},{2,0},{3,1},{4,6},{5,7},{6,4},{7,5},{8,10},{9,11},{10,... | collective-permute-start | bytes 1069064 | tf_op jit(solution)/shard_map/ppermute | solution.py:51
  36.9 5.7 %collective-permute-start.7 = (bf16[48,3712]{1,0:T(8,128)(2,1)}, bf16[48,3712]{1,0:T(8,128)(2,1)}, u32[]{:S(2)}, u32[]{:S(2)}) collective-permute-start(bf16[48,3712]{1,0:T(8,128)(2,1)} %collective-permute-done.3.refs_3_), channel_id=1, source_target_pairs={{0,2},{1,3},{2,0},{3,1},{4,6},{5,7},{6,4},{7,5},{8,10},{9,11},{10,... | collective-permute-start | bytes 1069064 | tf_op jit(solution)/shard_map/ppermute | solution.py:51
  41.5 2.7 %collective-permute-start.16 = (bf16[48,3712]{1,0:T(8,128)(2,1)}, bf16[48,3712]{1,0:T(8,128)(2,1)}, u32[]{:S(2)}, u32[]{:S(2)}) collective-permute-start(bf16[48,3712]{1,0:T(8,128)(2,1)} %collective-permute-done.12.refs_11_), channel_id=1, source_target_pairs={{0,2},{1,3},{2,0},{3,1},{4,6},{5,7},{6,4},{7,5},{8,10},{9,11},{10,... | collective-permute-start | bytes 1069064 | tf_op jit(solution)/shard_map/ppermute | solution.py:51
  60.5 2.2 %collective-permute-start.19 = (bf16[48,7296]{1,0:T(8,128)(2,1)S(1)}, bf16[48,7296]{1,0:T(8,128)(2,1)S(1)}, u32[]{:S(2)}, u32[]{:S(2)}) collective-permute-start(bf16[48,7296]{1,0:T(8,128)(2,1)S(1)} %slice.28), channel_id=1, source_target_pairs={{0,2},{1,3},{2,0},{3,1},{4,6},{5,7},{6,4},{7,5},{8,10},{9,11},{10,... | collective-permute-start | bytes 2101256 | tf_op jit(solution)/shard_map/ppermute | solution.py:51
  61.0 3.5 %collective-permute-start.17 = (bf16[48,7296]{1,0:T(8,128)(2,1)S(1)}, bf16[48,7296]{1,0:T(8,128)(2,1)S(1)}, u32[]{:S(2)}, u32[]{:S(2)}) collective-permute-start(bf16[48,7296]{1,0:T(8,128)(2,1)S(1)} %slice.25), channel_id=1, source_target_pairs={{0,2},{1,3},{2,0},{3,1},{4,6},{5,7},{6,4},{7,5},{8,10},{9,11},{10,... | collective-permute-start | bytes 2101256 | tf_op jit(solution)/shard_map/ppermute | solution.py:51
  62.9 7.4 %collective-permute-start.20 = (bf16[24,7296]{1,0:T(8,128)(2,1)S(1)}, bf16[24,7296]{1,0:T(8,128)(2,1)S(1)}, u32[]{:S(2)}, u32[]{:S(2)}) collective-permute-start(bf16[24,7296]{1,0:T(8,128)(2,1)S(1)} %slice.33), channel_id=1, source_target_pairs={{0,1},{1,0},{2,6},{3,7},{4,5},{5,4},{6,2},{7,3},{8,9},{9,8},{10,14... | collective-permute-start | bytes 1050632 | tf_op jit(solution)/shard_map/ppermute | solution.py:51
  64.7 11.1 %collective-permute-start.18 = (bf16[24,7296]{1,0:T(8,128)(2,1)S(1)}, bf16[24,7296]{1,0:T(8,128)(2,1)S(1)}, u32[]{:S(2)}, u32[]{:S(2)}) collective-permute-start(bf16[24,7296]{1,0:T(8,128)(2,1)S(1)} %slice.32), channel_id=1, source_target_pairs={{0,1},{1,0},{2,6},{3,7},{4,5},{5,4},{6,2},{7,3},{8,9},{9,8},{10,14... | collective-permute-start | bytes 1050632 | tf_op jit(solution)/shard_map/ppermute | solution.py:51
  70.5 7.2 %collective-permute-start.23 = (bf16[12,7296]{1,0:T(8,128)(2,1)S(1)}, bf16[12,7296]{1,0:T(8,128)(2,1)S(1)}, u32[]{:S(2)}, u32[]{:S(2)}) collective-permute-start(bf16[12,7296]{1,0:T(8,128)(2,1)S(1)} %slice.35), channel_id=1, source_target_pairs={{0,4},{1,5},{2,3},{3,2},{4,0},{5,1},{6,7},{7,6},{8,12},{9,13},{10,... | collective-permute-start | bytes 525320 | tf_op jit(solution)/shard_map/ppermute | solution.py:51
  76.0 6.1 %collective-permute-start.21 = (bf16[12,7296]{1,0:T(8,128)(2,1)S(1)}, bf16[12,7296]{1,0:T(8,128)(2,1)S(1)}, u32[]{:S(2)}, u32[]{:S(2)}) collective-permute-start(bf16[12,7296]{1,0:T(8,128)(2,1)S(1)} %slice.34), channel_id=1, source_target_pairs={{0,4},{1,5},{2,3},{3,2},{4,0},{5,1},{6,7},{7,6},{8,12},{9,13},{10,... | collective-permute-start | bytes 525320 | tf_op jit(solution)/shard_map/ppermute | solution.py:51
  77.7 8.7 %collective-permute-start.25 = (bf16[24,1920]{1,0:T(8,128)(2,1)S(1)}, bf16[24,1920]{1,0:T(8,128)(2,1)S(1)}, u32[]{:S(2)}, u32[]{:S(2)}) collective-permute-start(bf16[24,1920]{1,0:T(8,128)(2,1)S(1)} %get-tuple-element.33), channel_id=1, source_target_pairs={{0,24},{1,25},{2,26},{3,27},{4,28},{5,29},{6,30},{7,31},{8,16},{9,... | collective-permute-start | bytes 276488 | tf_op jit(solution)/shard_map/ppermute | solution.py:51
  80.4 7.1 %collective-permute-start.24 = (bf16[24,1920]{1,0:T(8,128)(2,1)S(1)}, bf16[24,1920]{1,0:T(8,128)(2,1)S(1)}, u32[]{:S(2)}, u32[]{:S(2)}) collective-permute-start(bf16[24,1920]{1,0:T(8,128)(2,1)S(1)} %get-tuple-element.32.after), channel_id=1, source_target_pairs={{0,16},{1,17},{2,18},{3,19},{4,20},{5,21},{6,22},{7,23},{8,24},{9,... | collective-permute-start | bytes 276488 | tf_op jit(solution)/shard_map/ppermute | solution.py:51
  82.2 6.0 %collective-permute-start.22 = (bf16[24,1920]{1,0:T(8,128)(2,1)S(1)}, bf16[24,1920]{1,0:T(8,128)(2,1)S(1)}, u32[]{:S(2)}, u32[]{:S(2)}) collective-permute-start(bf16[24,1920]{1,0:T(8,128)(2,1)S(1)} %get-tuple-element.31), channel_id=1, source_target_pairs={{0,8},{1,9},{2,10},{3,11},{4,12},{5,13},{6,14},{7,15},{8,0},{9,1},... | collective-permute-start | bytes 276488 | tf_op jit(solution)/shard_map/ppermute | solution.py:51
  82.3 5.9 %copy-start = (s32[6,8]{1,0:T(8,128)S(1)}, s32[6,8]{1,0:T(8,128)}, u32[]{:S(2)}) copy-start(s32[6,8]{1,0:T(8,128)} %ids.1) | copy-start | bytes 580

commit v4 on v3

--- a/solution.py
+++ b/solution.py
@@ -158,14 +158,13 @@
         for copy in pair:
             copy.start()
     middle = x.shape[0] // 2
-    for out, kind in ((dy, 1), (x, 0)):
-        assemble(out, 0, near, height, kind)
-        assemble(out, middle, far, height, kind)
-    back = []
-    for copy, h in zip(downs, halves, strict=True):
+    assemble(dy, 0, near, height, 1)
+    assemble(dy, middle, far, height, 1)
+    for copy in downs:
         copy.wait()
-        back.append(dot(dy[...], wd[h, :], (1, 1)))
-    back = jnp.concatenate(back, axis=1)
+    back = dot(dy[...], wd[...], (1, 1))
+    assemble(x, 0, near, height, 0)
+    assemble(x, middle, far, height, 0)
     for i, c in enumerate(steps):
         gates[i].wait()
         ups[i].wait()
@@ -288,8 +287,10 @@
 
 def outer_kernel(tall, size, a, b, after, out, ended, done, sem):
     copies = []
-    for i in range((a if tall else b).shape[1] // size):
-        part = pl.ds(i * size, size)
+    whole = (a if tall else b).shape[1]
+    edges = [0, size // 4] + list(range(size, whole + 1, size))
+    for i, (low, high) in enumerate(zip(edges, edges[1:])):
+        part = pl.ds(low, high - low)
         here = (part, slice(None)) if tall else (slice(None), part)
         left, right = (a[:, part], b[...]) if tall else (a[...], b[:, part])
         done[here] = dot(left, right, (0, 0)).astype(BF16)
@@ -310,7 +311,7 @@
         out_shape=(jax.ShapeDtypeStruct((1, *shape), BF16), jax.ShapeDtypeStruct((8, LANES), F32)),
         in_specs=[VMEM, VMEM, ANY],
         out_specs=(ANY, VMEM),
-        scratch_shapes=[pltpu.VMEM(shape, BF16), pltpu.SemaphoreType.DMA((max(shape) // size,))],
+        scratch_shapes=[pltpu.VMEM(shape, BF16), pltpu.SemaphoreType.DMA((max(shape) // size + 1,))],
         compiler_params=params(20),
         cost_estimate=cost(2 * rows * shape[0] * shape[1], 2 * shape[0] * shape[1]),
         name="outer",

time: 89.2 us -> 89.3 us (level)
  no operation moved by 1% of the time
where the time goes in v4:
time: 89.3 us; the launch traced here: 89.1 us
  waiting for transfers between devices  30.7 us (34%)
  Pallas kernels  29.9 us (33%)
  starting transfers between devices  27.1 us (30%)
    ppermute x26, waiting for transfers between devices, send(): return lax.ppermute(block, AXES, pairs)  30.7 us
    ppermute x26, starting transfers between devices, send(): return lax.ppermute(block, AXES, pairs)  27.1 us
    pallas_call x1, Pallas kernels, hidden(): pl.pallas_call(functools.partial(hidden_kernel, n, height, size), out_sha...  16.3 us
    pallas_call x3, Pallas kernels, outer(): pl.pallas_call(functools.partial(outer_kernel, tall, size), out_shape=(ja...  11.2 us
  transfers between devices with their start and end apart: 26, of which 12 were waited for; matrix products, arithmetic and copies ran while one was open for 1% of the time, Pallas kernels for 13%

profile of v4, /device:TPU:0, one launch (start us, length us, event | category | flops | bytes accessed | tf_op | source)
XLA Modules:
  0.0 89.1 jit_solution(15484212650837202077)
XLA Ops:
  0.6 1.1 %pack.1.a = bf16[48,1920]{1,0:T(8,128)(2,1)S(1)} custom-call(bf16[6,7168]{1,0:T(8,128)(2,1)} %x_hbm.1, bf16[6,7168]{1,0:T(8,128)(2,1)} %dy_hbm.1, bf16[6,8]{1,0:T(8,128)(2,1)} %g_hbm.1, s32[6,8]{1,0:T(8,128)} %ids.1), custom_call_target="tpu_custom_call" | custom-call | tf_op jit(solution)/shard_map/pack/pallas_call | solution.py:86
  1.8 3.1 %collective-permute-start = (bf16[48,1920]{1,0:T(8,128)(2,1)S(1)}, bf16[48,1920]{1,0:T(8,128)(2,1)S(1)}, u32[]{:S(2)}, u32[]{:S(2)}) collective-permute-start(bf16[48,1920]{1,0:T(8,128)(2,1)S(1)} %pack.1.a), channel_id=1, source_target_pairs={{0,8},{1,9},{2,10},{3,11},{4,12},{5,13},{6,14},{7,15},{8,0},{9,1},... | collective-permute-start | bytes 552968 | tf_op jit(solution)/shard_map/ppermute | solution.py:51
  4.8 2.5 %collective-permute-start.9 = (bf16[48,1920]{1,0:T(8,128)(2,1)S(1)}, bf16[48,1920]{1,0:T(8,128)(2,1)S(1)}, u32[]{:S(2)}, u32[]{:S(2)}) collective-permute-start(bf16[48,1920]{1,0:T(8,128)(2,1)S(1)} %pack.1.a), channel_id=1, source_target_pairs={{0,24},{1,25},{2,26},{3,27},{4,28},{5,29},{6,30},{7,31},{8,16},{9,... | collective-permute-start | bytes 552968 | tf_op jit(solution)/shard_map/ppermute | solution.py:51
  7.3 0.1 collective-permute-start.8
  7.4 2.5 %collective-permute-done.b = bf16[48,1920]{1,0:T(8,128)(2,1)S(1)} collective-permute-done((bf16[48,1920]{1,0:T(8,128)(2,1)S(1)}, bf16[48,1920]{1,0:T(8,128)(2,1)S(1)}, u32[]{:S(2)}, u32[]{:S(2)}) %collective-permute-start) | collective-permute-done | bytes 184352 | tf_op jit(solution)/shard_map/ppermute | solution.py:51
  9.9 0.1 pair.2.refs_0_
  10.0 0.1 collective-permute-start.4
  10.0 1.6 %collective-permute-start.2 = (bf16[48,3712]{1,0:T(8,128)(2,1)S(1)}, bf16[48,3712]{1,0:T(8,128)(2,1)S(1)}, u32[]{:S(2)}, u32[]{:S(2)}) collective-permute-start(bf16[48,3712]{1,0:T(8,128)(2,1)S(1)} %pair.2.refs_0_), channel_id=1, source_target_pairs={{0,1},{1,0},{2,6},{3,7},{4,5},{5,4},{6,2},{7,3},{8,9},{9,8},{10,14... | collective-permute-start | bytes 1069064 | tf_op jit(solution)/shard_map/ppermute | solution.py:51
  11.6 1.5 %collective-permute-start.1 = (bf16[48,3712]{1,0:T(8,128)(2,1)S(1)}, bf16[48,3712]{1,0:T(8,128)(2,1)S(1)}, u32[]{:S(2)}, u32[]{:S(2)}) collective-permute-start(bf16[48,3712]{1,0:T(8,128)(2,1)S(1)} %pair.2.refs_0_), channel_id=1, source_target_pairs={{0,4},{1,5},{2,3},{3,2},{4,0},{5,1},{6,7},{7,6},{8,12},{9,13},{10,... | collective-permute-start | bytes 1069064 | tf_op jit(solution)/shard_map/ppermute | solution.py:51
  13.1 3.7 %collective-permute-done.9.b = bf16[48,1920]{1,0:T(8,128)(2,1)S(1)} collective-permute-done((bf16[48,1920]{1,0:T(8,128)(2,1)S(1)}, bf16[48,1920]{1,0:T(8,128)(2,1)S(1)}, u32[]{:S(2)}, u32[]{:S(2)}) %collective-permute-start.9) | collective-permute-done | bytes 184352 | tf_op jit(solution)/shard_map/ppermute | solution.py:51
  16.9 6.8 %collective-permute-done.8.a = bf16[48,1920]{1,0:T(8,128)(2,1)S(1)} collective-permute-done((bf16[48,1920]{1,0:T(8,128)(2,1)S(1)}, bf16[48,1920]{1,0:T(8,128)(2,1)S(1)}, u32[]{:S(2)}, u32[]{:S(2)}) %collective-permute-start.8) | collective-permute-done | bytes 184352 | tf_op jit(solution)/shard_map/ppermute | solution.py:51
  23.6 0.1 pair.3.refs_8_
  23.7 1.6 %collective-permute-start.10 = (bf16[48,3712]{1,0:T(8,128)(2,1)S(1)}, bf16[48,3712]{1,0:T(8,128)(2,1)S(1)}, u32[]{:S(2)}, u32[]{:S(2)}) collective-permute-start(bf16[48,3712]{1,0:T(8,128)(2,1)S(1)} %pair.3.refs_8_), channel_id=1, source_target_pairs={{0,4},{1,5},{2,3},{3,2},{4,0},{5,1},{6,7},{7,6},{8,12},{9,13},{10,... | collective-permute-start | bytes 1069064 | tf_op jit(solution)/shard_map/ppermute | solution.py:51
  25.3 1.5 %collective-permute-start.11 = (bf16[48,3712]{1,0:T(8,128)(2,1)S(1)}, bf16[48,3712]{1,0:T(8,128)(2,1)S(1)}, u32[]{:S(2)}, u32[]{:S(2)}) collective-permute-start(bf16[48,3712]{1,0:T(8,128)(2,1)S(1)} %pair.3.refs_8_), channel_id=1, source_target_pairs={{0,1},{1,0},{2,6},{3,7},{4,5},{5,4},{6,2},{7,3},{8,9},{9,8},{10,14... | collective-permute-start | bytes 1069064 | tf_op jit(solution)/shard_map/ppermute | solution.py:51
  26.8 0.7 collective-permute-start.3
  27.5 6.4 %collective-permute-done.10.refs_9_ = bf16[48,3712]{1,0:T(8,128)(2,1)S(1)} collective-permute-done((bf16[48,3712]{1,0:T(8,128)(2,1)S(1)}, bf16[48,3712]{1,0:T(8,128)(2,1)S(1)}, u32[]{:S(2)}, u32[]{:S(2)}) %collective-permute-start.10) | collective-permute-done | bytes 356384 | tf_op jit(solution)/shard_map/ppermute | solution.py:51
  34.0 1.5 %collective-permute-start.12 = (bf16[48,3712]{1,0:T(8,128)(2,1)S(1)}, bf16[48,3712]{1,0:T(8,128)(2,1)}, u32[]{:S(2)}, u32[]{:S(2)}) collective-permute-start(bf16[48,3712]{1,0:T(8,128)(2,1)S(1)} %collective-permute-done.10.refs_9_), channel_id=1, source_target_pairs={{0,1},{1,0},{2,6},{3,7},{4,5},{5,4},{6,2},{7,3},{8,9},{9,8},{10,14... | collective-permute-start | bytes 1069064 | tf_op jit(solution)/shard_map/ppermute | solution.py:51
  35.5 0.5 collective-permute-start.14
  36.0 0.1 collective-permute-start.15
  36.1 0.8 collective-permute-done.3.refs_3_
  36.9 2.1 %collective-permute-start.7 = (bf16[48,3712]{1,0:T(8,128)(2,1)}, bf16[48,3712]{1,0:T(8,128)(2,1)}, u32[]{:S(2)}, u32[]{:S(2)}) collective-permute-start(bf16[48,3712]{1,0:T(8,128)(2,1)} %collective-permute-done.3.refs_3_), channel_id=1, source_target_pairs={{0,2},{1,3},{2,0},{3,1},{4,6},{5,7},{6,4},{7,5},{8,10},{9,11},{10,... | collective-permute-start | bytes 1069064 | tf_op jit(solution)/shard_map/ppermute | solution.py:51
  39.0 2.4 %collective-permute-done.12.refs_11_ = bf16[48,3712]{1,0:T(8,128)(2,1)} collective-permute-done((bf16[48,3712]{1,0:T(8,128)(2,1)S(1)}, bf16[48,3712]{1,0:T(8,128)(2,1)}, u32[]{:S(2)}, u32[]{:S(2)}) %collective-permute-start.12) | collective-permute-done | bytes 356384 | tf_op jit(solution)/shard_map/ppermute | solution.py:51
  41.5 1.1 %collective-permute-start.16 = (bf16[48,3712]{1,0:T(8,128)(2,1)}, bf16[48,3712]{1,0:T(8,128)(2,1)}, u32[]{:S(2)}, u32[]{:S(2)}) collective-permute-start(bf16[48,3712]{1,0:T(8,128)(2,1)} %collective-permute-done.12.refs_11_), channel_id=1, source_target_pairs={{0,2},{1,3},{2,0},{3,1},{4,6},{5,7},{6,4},{7,5},{8,10},{9,11},{10,... | collective-permute-start | bytes 1069064 | tf_op jit(solution)/shard_map/ppermute | solution.py:51
  42.6 1.6 %collective-permute-done.16.refs_15_ = bf16[48,3712]{1,0:T(8,128)(2,1)} collective-permute-done((bf16[48,3712]{1,0:T(8,128)(2,1)}, bf16[48,3712]{1,0:T(8,128)(2,1)}, u32[]{:S(2)}, u32[]{:S(2)}) %collective-permute-start.16) | collective-permute-done | bytes 356384 | tf_op jit(solution)/shard_map/ppermute | solution.py:51
  44.2 16.3 %hidden.1 = (bf16[192,7168]{1,0:T(8,128)(2,1)S(1)}, bf16[192,7168]{1,0:T(8,128)(2,1)S(1)}, bf16[192,512]{1,0:T(8,128)(2,1)S(1)}, bf16[192,512]{1,0:T(8,128)(2,1)...) custom-call(s32[1]{0:T(128)} %bitcast.mine_ref, ...), custom_call_target="tpu_custom_call" | custom-call | flops 5637144576 | bytes 22020096 | tf_op jit(solution)/shard_map/hidden/pallas_call | solution.py:199
  60.5 0.4 collective-permute-start.19
  61.0 0.2 collective-permute-start.17
  61.2 1.5 %collective-permute-done.19 = bf16[48,7296]{1,0:T(8,128)(2,1)S(1)} collective-permute-done((bf16[48,7296]{1,0:T(8,128)(2,1)S(1)}, bf16[48,7296]{1,0:T(8,128)(2,1)S(1)}, u32[]{:S(2)}, u32[]{:S(2)}) %collective-permute-start.19) | collective-permute-done | bytes 700448 | tf_op jit(solution)/shard_map/ppermute | solution.py:51
  62.8 0.2 add_convert_fusion.own
  63.0 1.6 %collective-permute-start.20 = (bf16[24,7296]{1,0:T(8,128)(2,1)S(1)}, bf16[24,7296]{1,0:T(8,128)(2,1)S(1)}, u32[]{:S(2)}, u32[]{:S(2)}) collective-permute-start(bf16[24,7296]{1,0:T(8,128)(2,1)S(1)} %slice.33), channel_id=1, source_target_pairs={{0,1},{1,0},{2,6},{3,7},{4,5},{5,4},{6,2},{7,3},{8,9},{9,8},{10,14... | collective-permute-start | bytes 1050632 | tf_op jit(solution)/shard_map/ppermute | solution.py:51
  64.6 0.2 add_convert_fusion.1.after.own
  64.8 0.8 collective-permute-start.18
  65.5 3.5 %outer.3 = (bf16[1,7168,512]{2,1,0:T(8,128)(2,1)}, f32[8,128]{1,0:T(8,128)S(1)}) custom-call(bf16[192,7168]{1,0:T(8,128)(2,1)S(1)} %get-tuple-element.24.a, bf16[192,512]{1,0:T(8,128)(2,1)S(1)} %get-tuple-element.27.b, bf16[48,7296]{1,0:T(8,128)(2,1)S(1)} %add_convert_fusion.1.after.own), custom_call_target="tpu_custom_call" | custom-call | flops 1409286144 | bytes 7340032 | tf_op jit(solution)/shard_map/outer/pallas_call | solution.py:309
  69.0 1.3 %collective-permute-done.20.other = bf16[24,7296]{1,0:T(8,128)(2,1)S(1)} collective-permute-done((bf16[24,7296]{1,0:T(8,128)(2,1)S(1)}, bf16[24,7296]{1,0:T(8,128)(2,1)S(1)}, u32[]{:S(2)}, u32[]{:S(2)}) %collective-permute-start.20) | collective-permute-done | bytes 350240 | tf_op jit(solution)/shard_map/ppermute | solution.py:51
  70.4 0.1 fold.2.after.own
  70.5 1.8 %collective-permute-start.23 = (bf16[12,7296]{1,0:T(8,128)(2,1)S(1)}, bf16[12,7296]{1,0:T(8,128)(2,1)S(1)}, u32[]{:S(2)}, u32[]{:S(2)}) collective-permute-start(bf16[12,7296]{1,0:T(8,128)(2,1)S(1)} %slice.35), channel_id=1, source_target_pairs={{0,4},{1,5},{2,3},{3,2},{4,0},{5,1},{6,7},{7,6},{8,12},{9,13},{10,... | collective-permute-start | bytes 525320 | tf_op jit(solution)/shard_map/ppermute | solution.py:51
  72.4 3.6 %outer.4 = (bf16[1,7168,512]{2,1,0:T(8,128)(2,1)}, f32[8,128]{1,0:T(8,128)S(1)}) custom-call(bf16[192,7168]{1,0:T(8,128)(2,1)S(1)} %get-tuple-element.24.a, bf16[192,512]{1,0:T(8,128)(2,1)S(1)} %get-tuple-element.25.b, bf16[24,7296]{1,0:T(8,128)(2,1)S(1)} %fold.2.after.own), custom_call_target="tpu_custom_call" | custom-call | flops 1409286144 | bytes 7340032 | tf_op jit(solution)/shard_map/outer/pallas_call | solution.py:309
  76.0 0.1 fold.3.own
  76.2 1.5 %collective-permute-start.21 = (bf16[12,7296]{1,0:T(8,128)(2,1)S(1)}, bf16[12,7296]{1,0:T(8,128)(2,1)S(1)}, u32[]{:S(2)}, u32[]{:S(2)}) collective-permute-start(bf16[12,7296]{1,0:T(8,128)(2,1)S(1)} %slice.34), channel_id=1, source_target_pairs={{0,4},{1,5},{2,3},{3,2},{4,0},{5,1},{6,7},{7,6},{8,12},{9,13},{10,... | collective-permute-start | bytes 525320 | tf_op jit(solution)/shard_map/ppermute | solution.py:51
  77.7 0.1 split.3
  77.8 2.7 %collective-permute-start.25 = (bf16[24,1920]{1,0:T(8,128)(2,1)S(1)}, bf16[24,1920]{1,0:T(8,128)(2,1)S(1)}, u32[]{:S(2)}, u32[]{:S(2)}) collective-permute-start(bf16[24,1920]{1,0:T(8,128)(2,1)S(1)} %get-tuple-element.33), channel_id=1, source_target_pairs={{0,24},{1,25},{2,26},{3,27},{4,28},{5,29},{6,30},{7,31},{8,16},{9,... | collective-permute-start | bytes 276488 | tf_op jit(solution)/shard_map/ppermute | solution.py:51
  80.5 1.8 %collective-permute-done.21.other = bf16[12,7296]{1,0:T(8,128)(2,1)S(1)} collective-permute-done((bf16[12,7296]{1,0:T(8,128)(2,1)S(1)}, bf16[12,7296]{1,0:T(8,128)(2,1)S(1)}, u32[]{:S(2)}, u32[]{:S(2)}) %collective-permute-start.21) | collective-permute-done | bytes 175136 | tf_op jit(solution)/shard_map/ppermute | solution.py:51
  82.3 0.1 split.2
  82.4 0.1 collective-permute-start.22
  82.5 4.1 %outer.5 = (bf16[1,512,7168]{2,1,0:T(8,128)(2,1)}, f32[8,128]{1,0:T(8,128)}) custom-call(bf16[192,512]{1,0:T(8,128)(2,1)S(1)} %get-tuple-element.38.a, bf16[192,7168]{1,0:T(8,128)(2,1)S(1)} %get-tuple-element.39.b, bf16[24,1920]{1,0:T(8,128)(2,1)S(1)} %get-tuple-element.32.after), custom_call_target="tpu_custom_call" | custom-call | flops 1409286144 | bytes 7340032 | tf_op jit(solution)/shard_map/outer/pallas_call | solution.py:309
  86.6 1.0 %collective-permute-done.24.c = bf16[24,1920]{1,0:T(8,128)(2,1)S(1)} collective-permute-done((bf16[24,1920]{1,0:T(8,128)(2,1)S(1)}, bf16[24,1920]{1,0:T(8,128)(2,1)S(1)}, u32[]{:S(2)}, u32[]{:S(2)}) %collective-permute-start.24) | collective-permute-done | bytes 92192 | tf_op jit(solution)/shard_map/ppermute | solution.py:51
  87.7 0.7 collective-permute-done.22.b
  88.4 0.8 finish.1
  (26 shorter events, 0.3 us)
Async XLA Ops:
  1.8 8.1 %collective-permute-start = (bf16[48,1920]{1,0:T(8,128)(2,1)S(1)}, bf16[48,1920]{1,0:T(8,128)(2,1)S(1)}, u32[]{:S(2)}, u32[]{:S(2)}) collective-permute-start(bf16[48,1920]{1,0:T(8,128)(2,1)S(1)} %pack.1.a), channel_id=1, source_target_pairs={{0,8},{1,9},{2,10},{3,11},{4,12},{5,13},{6,14},{7,15},{8,0},{9,1},... | collective-permute-start | bytes 552968 | tf_op jit(solution)/shard_map/ppermute | solution.py:51
  4.8 12.0 %collective-permute-start.9 = (bf16[48,1920]{1,0:T(8,128)(2,1)S(1)}, bf16[48,1920]{1,0:T(8,128)(2,1)S(1)}, u32[]{:S(2)}, u32[]{:S(2)}) collective-permute-start(bf16[48,1920]{1,0:T(8,128)(2,1)S(1)} %pack.1.a), channel_id=1, source_target_pairs={{0,24},{1,25},{2,26},{3,27},{4,28},{5,29},{6,30},{7,31},{8,16},{9,... | collective-permute-start | bytes 552968 | tf_op jit(solution)/shard_map/ppermute | solution.py:51
  7.3 16.3 %collective-permute-start.8 = (bf16[48,1920]{1,0:T(8,128)(2,1)S(1)}, bf16[48,1920]{1,0:T(8,128)(2,1)S(1)}, u32[]{:S(2)}, u32[]{:S(2)}) collective-permute-start(bf16[48,1920]{1,0:T(8,128)(2,1)S(1)} %pack.1.a), channel_id=1, source_target_pairs={{0,16},{1,17},{2,18},{3,19},{4,20},{5,21},{6,22},{7,23},{8,24},{9,... | collective-permute-start | bytes 552968 | tf_op jit(solution)/shard_map/ppermute | solution.py:51
  10.0 15.3 %collective-permute-start.4 = (bf16[48,3712]{1,0:T(8,128)(2,1)S(1)}, bf16[48,3712]{1,0:T(8,128)(2,1)S(1)}, u32[]{:S(2)}, u32[]{:S(2)}) collective-permute-start(bf16[48,3712]{1,0:T(8,128)(2,1)S(1)} %pair.2.refs_0_), channel_id=1, source_target_pairs={{0,2},{1,3},{2,0},{3,1},{4,6},{5,7},{6,4},{7,5},{8,10},{9,11},{10,... | collective-permute-start | bytes 1069064 | tf_op jit(solution)/shard_map/ppermute | solution.py:51
  10.0 16.8 %collective-permute-start.2 = (bf16[48,3712]{1,0:T(8,128)(2,1)S(1)}, bf16[48,3712]{1,0:T(8,128)(2,1)S(1)}, u32[]{:S(2)}, u32[]{:S(2)}) collective-permute-start(bf16[48,3712]{1,0:T(8,128)(2,1)S(1)} %pair.2.refs_0_), channel_id=1, source_target_pairs={{0,1},{1,0},{2,6},{3,7},{4,5},{5,4},{6,2},{7,3},{8,9},{9,8},{10,14... | collective-permute-start | bytes 1069064 | tf_op jit(solution)/shard_map/ppermute | solution.py:51
  11.6 15.2 %collective-permute-start.1 = (bf16[48,3712]{1,0:T(8,128)(2,1)S(1)}, bf16[48,3712]{1,0:T(8,128)(2,1)S(1)}, u32[]{:S(2)}, u32[]{:S(2)}) collective-permute-start(bf16[48,3712]{1,0:T(8,128)(2,1)S(1)} %pair.2.refs_0_), channel_id=1, source_target_pairs={{0,4},{1,5},{2,3},{3,2},{4,0},{5,1},{6,7},{7,6},{8,12},{9,13},{10,... | collective-permute-start | bytes 1069064 | tf_op jit(solution)/shard_map/ppermute | solution.py:51
  23.7 10.2 %collective-permute-start.10 = (bf16[48,3712]{1,0:T(8,128)(2,1)S(1)}, bf16[48,3712]{1,0:T(8,128)(2,1)S(1)}, u32[]{:S(2)}, u32[]{:S(2)}) collective-permute-start(bf16[48,3712]{1,0:T(8,128)(2,1)S(1)} %pair.3.refs_8_), channel_id=1, source_target_pairs={{0,4},{1,5},{2,3},{3,2},{4,0},{5,1},{6,7},{7,6},{8,12},{9,13},{10,... | collective-permute-start | bytes 1069064 | tf_op jit(solution)/shard_map/ppermute | solution.py:51
  25.3 10.2 %collective-permute-start.13 = (bf16[48,3712]{1,0:T(8,128)(2,1)S(1)}, bf16[48,3712]{1,0:T(8,128)(2,1)S(1)}, u32[]{:S(2)}, u32[]{:S(2)}) collective-permute-start(bf16[48,3712]{1,0:T(8,128)(2,1)S(1)} %pair.3.refs_8_), channel_id=1, source_target_pairs={{0,2},{1,3},{2,0},{3,1},{4,6},{5,7},{6,4},{7,5},{8,10},{9,11},{10,... | collective-permute-start | bytes 1069064 | tf_op jit(solution)/shard_map/ppermute | solution.py:51
  25.3 10.2 %collective-permute-start.11 = (bf16[48,3712]{1,0:T(8,128)(2,1)S(1)}, bf16[48,3712]{1,0:T(8,128)(2,1)S(1)}, u32[]{:S(2)}, u32[]{:S(2)}) collective-permute-start(bf16[48,3712]{1,0:T(8,128)(2,1)S(1)} %pair.3.refs_8_), channel_id=1, source_target_pairs={{0,1},{1,0},{2,6},{3,7},{4,5},{5,4},{6,2},{7,3},{8,9},{9,8},{10,14... | collective-permute-start | bytes 1069064 | tf_op jit(solution)/shard_map/ppermute | solution.py:51
  26.8 9.2 %collective-permute-start.6 = (bf16[48,3712]{1,0:T(8,128)(2,1)S(1)}, bf16[48,3712]{1,0:T(8,128)(2,1)S(1)}, u32[]{:S(2)}, u32[]{:S(2)}) collective-permute-start(bf16[48,3712]{1,0:T(8,128)(2,1)S(1)} %collective-permute-done.2.refs_2_), channel_id=1, source_target_pairs={{0,2},{1,3},{2,0},{3,1},{4,6},{5,7},{6,4},{7,5},{8,10},{9,11},{10,... | collective-permute-start | bytes 1069064 | tf_op jit(solution)/shard_map/ppermute | solution.py:51
  26.8 10.1 %collective-permute-start.3 = (bf16[48,3712]{1,0:T(8,128)(2,1)S(1)}, bf16[48,3712]{1,0:T(8,128)(2,1)}, u32[]{:S(2)}, u32[]{:S(2)}) collective-permute-start(bf16[48,3712]{1,0:T(8,128)(2,1)S(1)} %collective-permute-done.1.refs_1_), channel_id=1, source_target_pairs={{0,1},{1,0},{2,6},{3,7},{4,5},{5,4},{6,2},{7,3},{8,9},{9,8},{10,14... | collective-permute-start | bytes 1069064 | tf_op jit(solution)/shard_map/ppermute | solution.py:51
  34.0 7.5 %collective-permute-start.12 = (bf16[48,3712]{1,0:T(8,128)(2,1)S(1)}, bf16[48,3712]{1,0:T(8,128)(2,1)}, u32[]{:S(2)}, u32[]{:S(2)}) collective-permute-start(bf16[48,3712]{1,0:T(8,128)(2,1)S(1)} %collective-permute-done.10.refs_9_), channel_id=1, source_target_pairs={{0,1},{1,0},{2,6},{3,7},{4,5},{5,4},{6,2},{7,3},{8,9},{9,8},{10,14... | collective-permute-start | bytes 1069064 | tf_op jit(solution)/shard_map/ppermute | solution.py:51
  35.5 7.1 %collective-permute-start.5 = (bf16[48,3712]{1,0:T(8,128)(2,1)S(1)}, bf16[48,3712]{1,0:T(8,128)(2,1)}, u32[]{:S(2)}, u32[]{:S(2)}) collective-permute-start(bf16[48,3712]{1,0:T(8,128)(2,1)S(1)} %collective-permute-done.1.refs_1_), channel_id=1, source_target_pairs={{0,2},{1,3},{2,0},{3,1},{4,6},{5,7},{6,4},{7,5},{8,10},{9,11},{10,... | collective-permute-start | bytes 1069064 | tf_op jit(solution)/shard_map/ppermute | solution.py:51
  35.5 7.1 %collective-permute-start.14 = (bf16[48,3712]{1,0:T(8,128)(2,1)S(1)}, bf16[48,3712]{1,0:T(8,128)(2,1)}, u32[]{:S(2)}, u32[]{:S(2)}) collective-permute-start(bf16[48,3712]{1,0:T(8,128)(2,1)S(1)} %collective-permute-done.10.refs_9_), channel_id=1, source_target_pairs={{0,2},{1,3},{2,0},{3,1},{4,6},{5,7},{6,4},{7,5},{8,10},{9,11},{10,... | collective-permute-start | bytes 1069064 | tf_op jit(solution)/shard_map/ppermute | solution.py:51
  36.0 6.6 %collective-permute-start.15 = (bf16[48,3712]{1,0:T(8,128)(2,1)S(1)}, bf16[48,3712]{1,0:T(8,128)(2,1)}, u32[]{:S(2)}, u32[]{:S(2)}) collective-permute-start(bf16[48,3712]{1,0:T(8,128)(2,1)S(1)} %collective-permute-done.11.refs_10_), channel_id=1, source_target_pairs={{0,2},{1,3},{2,0},{3,1},{4,6},{5,7},{6,4},{7,5},{8,10},{9,11},{10,... | collective-permute-start | bytes 1069064 | tf_op jit(solution)/shard_map/ppermute | solution.py:51
  36.9 5.7 %collective-permute-start.7 = (bf16[48,3712]{1,0:T(8,128)(2,1)}, bf16[48,3712]{1,0:T(8,128)(2,1)}, u32[]{:S(2)}, u32[]{:S(2)}) collective-permute-start(bf16[48,3712]{1,0:T(8,128)(2,1)} %collective-permute-done.3.refs_3_), channel_id=1, source_target_pairs={{0,2},{1,3},{2,0},{3,1},{4,6},{5,7},{6,4},{7,5},{8,10},{9,11},{10,... | collective-permute-start | bytes 1069064 | tf_op jit(solution)/shard_map/ppermute | solution.py:51
  41.5 2.7 %collective-permute-start.16 = (bf16[48,3712]{1,0:T(8,128)(2,1)}, bf16[48,3712]{1,0:T(8,128)(2,1)}, u32[]{:S(2)}, u32[]{:S(2)}) collective-permute-start(bf16[48,3712]{1,0:T(8,128)(2,1)} %collective-permute-done.12.refs_11_), channel_id=1, source_target_pairs={{0,2},{1,3},{2,0},{3,1},{4,6},{5,7},{6,4},{7,5},{8,10},{9,11},{10,... | collective-permute-start | bytes 1069064 | tf_op jit(solution)/shard_map/ppermute | solution.py:51
  60.5 2.2 %collective-permute-start.19 = (bf16[48,7296]{1,0:T(8,128)(2,1)S(1)}, bf16[48,7296]{1,0:T(8,128)(2,1)S(1)}, u32[]{:S(2)}, u32[]{:S(2)}) collective-permute-start(bf16[48,7296]{1,0:T(8,128)(2,1)S(1)} %slice.28), channel_id=1, source_target_pairs={{0,2},{1,3},{2,0},{3,1},{4,6},{5,7},{6,4},{7,5},{8,10},{9,11},{10,... | collective-permute-start | bytes 2101256 | tf_op jit(solution)/shard_map/ppermute | solution.py:51
  61.0 3.5 %collective-permute-start.17 = (bf16[48,7296]{1,0:T(8,128)(2,1)S(1)}, bf16[48,7296]{1,0:T(8,128)(2,1)S(1)}, u32[]{:S(2)}, u32[]{:S(2)}) collective-permute-start(bf16[48,7296]{1,0:T(8,128)(2,1)S(1)} %slice.25), channel_id=1, source_target_pairs={{0,2},{1,3},{2,0},{3,1},{4,6},{5,7},{6,4},{7,5},{8,10},{9,11},{10,... | collective-permute-start | bytes 2101256 | tf_op jit(solution)/shard_map/ppermute | solution.py:51
  63.0 7.4 %collective-permute-start.20 = (bf16[24,7296]{1,0:T(8,128)(2,1)S(1)}, bf16[24,7296]{1,0:T(8,128)(2,1)S(1)}, u32[]{:S(2)}, u32[]{:S(2)}) collective-permute-start(bf16[24,7296]{1,0:T(8,128)(2,1)S(1)} %slice.33), channel_id=1, source_target_pairs={{0,1},{1,0},{2,6},{3,7},{4,5},{5,4},{6,2},{7,3},{8,9},{9,8},{10,14... | collective-permute-start | bytes 1050632 | tf_op jit(solution)/shard_map/ppermute | solution.py:51
  64.8 11.2 %collective-permute-start.18 = (bf16[24,7296]{1,0:T(8,128)(2,1)S(1)}, bf16[24,7296]{1,0:T(8,128)(2,1)S(1)}, u32[]{:S(2)}, u32[]{:S(2)}) collective-permute-start(bf16[24,7296]{1,0:T(8,128)(2,1)S(1)} %slice.32), channel_id=1, source_target_pairs={{0,1},{1,0},{2,6},{3,7},{4,5},{5,4},{6,2},{7,3},{8,9},{9,8},{10,14... | collective-permute-start | bytes 1050632 | tf_op jit(solution)/shard_map/ppermute | solution.py:51
  70.5 7.2 %collective-permute-start.23 = (bf16[12,7296]{1,0:T(8,128)(2,1)S(1)}, bf16[12,7296]{1,0:T(8,128)(2,1)S(1)}, u32[]{:S(2)}, u32[]{:S(2)}) collective-permute-start(bf16[12,7296]{1,0:T(8,128)(2,1)S(1)} %slice.35), channel_id=1, source_target_pairs={{0,4},{1,5},{2,3},{3,2},{4,0},{5,1},{6,7},{7,6},{8,12},{9,13},{10,... | collective-permute-start | bytes 525320 | tf_op jit(solution)/shard_map/ppermute | solution.py:51
  76.2 6.1 %collective-permute-start.21 = (bf16[12,7296]{1,0:T(8,128)(2,1)S(1)}, bf16[12,7296]{1,0:T(8,128)(2,1)S(1)}, u32[]{:S(2)}, u32[]{:S(2)}) collective-permute-start(bf16[12,7296]{1,0:T(8,128)(2,1)S(1)} %slice.34), channel_id=1, source_target_pairs={{0,4},{1,5},{2,3},{3,2},{4,0},{5,1},{6,7},{7,6},{8,12},{9,13},{10,... | collective-permute-start | bytes 525320 | tf_op jit(solution)/shard_map/ppermute | solution.py:51
  77.8 8.8 %collective-permute-start.25 = (bf16[24,1920]{1,0:T(8,128)(2,1)S(1)}, bf16[24,1920]{1,0:T(8,128)(2,1)S(1)}, u32[]{:S(2)}, u32[]{:S(2)}) collective-permute-start(bf16[24,1920]{1,0:T(8,128)(2,1)S(1)} %get-tuple-element.33), channel_id=1, source_target_pairs={{0,24},{1,25},{2,26},{3,27},{4,28},{5,29},{6,30},{7,31},{8,16},{9,... | collective-permute-start | bytes 276488 | tf_op jit(solution)/shard_map/ppermute | solution.py:51
  80.5 7.2 %collective-permute-start.24 = (bf16[24,1920]{1,0:T(8,128)(2,1)S(1)}, bf16[24,1920]{1,0:T(8,128)(2,1)S(1)}, u32[]{:S(2)}, u32[]{:S(2)}) collective-permute-start(bf16[24,1920]{1,0:T(8,128)(2,1)S(1)} %get-tuple-element.32.after), channel_id=1, source_target_pairs={{0,16},{1,17},{2,18},{3,19},{4,20},{5,21},{6,22},{7,23},{8,24},{9,... | collective-permute-start | bytes 276488 | tf_op jit(solution)/shard_map/ppermute | solution.py:51
  82.4 6.0 %collective-permute-start.22 = (bf16[24,1920]{1,0:T(8,128)(2,1)S(1)}, bf16[24,1920]{1,0:T(8,128)(2,1)S(1)}, u32[]{:S(2)}, u32[]{:S(2)}) collective-permute-start(bf16[24,1920]{1,0:T(8,128)(2,1)S(1)} %get-tuple-element.31), channel_id=1, source_target_pairs={{0,8},{1,9},{2,10},{3,11},{4,12},{5,13},{6,14},{7,15},{8,0},{9,1},... | collective-permute-start | bytes 276488 | tf_op jit(solution)/shard_map/ppermute | solution.py:51
  82.5 5.9 %copy-start = (s32[6,8]{1,0:T(8,128)S(1)}, s32[6,8]{1,0:T(8,128)}, u32[]{:S(2)}) copy-start(s32[6,8]{1,0:T(8,128)} %ids.1) | copy-start | bytes 580
